TPU v7x, 1024 devices: a whole 4x8x16 slice. The times are simulated.
1024 devices in a mesh: gx: 16 (over z), gy: 4 (over x), gz: 16 (over y, core).
Axes of the slice: x: 4, y: 8, z: 16, core: 2. Of those that a mesh axis runs over, the one named last changes fastest.
Arguments:
- sources: float32 [32, 64, 64, 512], P(None, 'gz', 'gx', 'gy'), may hold values from -6 to 6
- labels: int32 [64, 64, 512], P('gz', 'gx', 'gy'), may hold values from 1 to 8
- region_table: float32 [8, 4], replicated, may hold values from 0.5 to 2
- sweep_index: int32 [32], replicated, may hold values from 0 to 31
- sweep_gain: float32 [32, 8], replicated, may hold values from 0.5 to 2
Outputs:
- solution: float32 [32, 64, 64, 512], P(None, 'gz', 'gx', 'gy')
- residual: float32 [32, 64, 64, 512], P(None, 'gz', 'gx', 'gy')
All inputs are finite; a program needn't handle non-finite values.
Results may differ from a plain program's by a relative error of at most 0.0003.
Values sent between devices are 32-bit elements; how exact they have to be, the bound alone decides.
No kernel may reach another device: no remote copies, remote signals or barrier semaphores. Data moves between devices by JAX's collectives and lax.ppermute only.
A program may use at most 32 MiB of HBM per device.

v0:
```python
import jax
import jax.numpy as jnp
from jax import lax
from jax.sharding import PartitionSpec as P

S = 4
NREG = 8


SIGMA = 8.0
THETA = 8.0


def padded_2(block, sides, width):
    for axis, dim in sides:
        count = lax.axis_size(axis)
        forward = [(i, i + 1) for i in range(count - 1)]
        backward = [(target, source) for source, target in forward]
        low = lax.ppermute(
            lax.slice_in_dim(block, block.shape[dim] - width, None, axis=dim), axis, forward
        )
        high = lax.ppermute(lax.slice_in_dim(block, 0, width, axis=dim), axis, backward)
        block = jnp.concatenate([low, block, high], axis=dim)
    return block


def region_fields(labels, region_table):
    fields = [jnp.zeros(labels.shape, jnp.float32) for column in range(4)]
    for region in range(NREG):
        hit = (labels == region + 1).astype(jnp.float32)
        fields = [fields[column] + hit * region_table[region, column] for column in range(4)]
    return fields


def trimmed(array, depth):
    lead = [slice(None)] * (array.ndim - 3)
    return array[tuple(lead + [slice(depth, -depth)] * 3)]


def shifted(padded, dim, offset):
    lead = [slice(None)] * (padded.ndim - 3)
    index = [slice(1, -1)] * 3
    size = padded.shape[padded.ndim - 3 + dim]
    index[dim] = slice(1 + offset, size - 1 + offset)
    return padded[tuple(lead + index)]


def face_set(fields):
    faces = []
    for dim in range(3):
        center = trimmed(fields[dim], 1)
        faces.append(0.5 * (center + shifted(fields[dim], dim, 1)))
        faces.append(0.5 * (center + shifted(fields[dim], dim, -1)))
    diag = trimmed(fields[3], 1) + faces[0] + faces[1] + faces[2] + faces[3] + faces[4] + faces[5]
    return (faces, diag)


def next_power(padded, faces, diag):
    beside = faces[0] * shifted(padded, 0, 1) + faces[1] * shifted(padded, 0, -1)
    beside = beside + faces[2] * shifted(padded, 1, 1) + faces[3] * shifted(padded, 1, -1)
    beside = beside + faces[4] * shifted(padded, 2, 1) + faces[5] * shifted(padded, 2, -1)
    center = trimmed(padded, 1)
    image = diag * center - beside
    return (image - SIGMA * center) / THETA


def body(sources, labels, region_table, sweep_index, sweep_gain):
    count = sources.shape[0]
    gain_rows = sweep_gain[sweep_index]
    regions = jnp.arange(1, NREG + 1, dtype=jnp.int32)
    one_hot = (labels.reshape(1, -1) == regions[:, None]).astype(jnp.float32)
    gain = jnp.dot(
        gain_rows, one_hot, precision=lax.Precision.HIGHEST, preferred_element_type=jnp.float32
    )
    rhs = sources * gain.reshape(sources.shape)
    basis = [rhs]
    near_labels = padded_2(labels, (("gx", 1), ("gy", 2), ("gz", 0)), 1)
    faces, diag = face_set(region_fields(near_labels, region_table))
    current = rhs
    for step in range(S):
        padded = padded_2(current, (("gx", 2), ("gy", 3), ("gz", 1)), 1)
        current = next_power(padded, faces, diag)
        basis.append(current)
    flat = jnp.concatenate([block.reshape(count, -1) for block in basis], 0)
    partial_gram = jnp.dot(
        flat, flat.T, precision=lax.Precision.HIGHEST, preferred_element_type=jnp.float32
    )
    gram = lax.psum(partial_gram, ("gx", "gy", "gz"))
    width = S * count
    mat = THETA * gram[:width, count:] + SIGMA * gram[:width, :width]
    mat = 0.5 * (mat + mat.T)
    factor = jnp.linalg.cholesky(mat)
    coef = jax.scipy.linalg.cho_solve((factor, True), gram[:width, :count])
    combo = jnp.zeros(((S + 1) * count, count), jnp.float32)
    combo = combo.at[:width].add(SIGMA * coef)
    combo = combo.at[count:].add(THETA * coef)
    solution = jnp.dot(
        coef.T, flat[:width], precision=lax.Precision.HIGHEST, preferred_element_type=jnp.float32
    )
    taken = jnp.dot(
        combo.T, flat, precision=lax.Precision.HIGHEST, preferred_element_type=jnp.float32
    )
    residual = flat[:count] - taken
    return (solution.reshape(sources.shape), residual.reshape(sources.shape))


def solution(mesh):
    placed = (P(None, "gz", "gx", "gy"), P("gz", "gx", "gy"), P(), P(), P())
    return jax.shard_map(
        body,
        mesh=mesh,
        in_specs=placed,
        out_specs=(P(None, "gz", "gx", "gy"), P(None, "gz", "gx", "gy")),
        check_vma=False,
    )
```

profile of v0, /device:TPU:1, one launch (start us, length us, event | category | flops | bytes accessed | tf_op | source)
XLA Modules:
  0.0 722.1 jit_solution(6737383193984629989)
XLA Ops:
  8.0 4.8 collective-permute-start
  18.5 4.6 collective-permute-start.6
  25.3 3.1 collective-permute-start.2
  29.7 3.2 collective-permute-done.3
  33.0 5.8 collective-permute-start.4
  38.7 7.3 %collective-permute-start.5 = (s32[1,6,130]{2,1,0:T(8,128)S(1)}, s32[1,6,130]{2,1,0:T(8,128)S(1)}, u32[]{:S(2)}, u32[]{:S(2)}) collective-permute-start(s32[1,6,130]{2,1,0:T(8,128)S(1)} %get-tuple-element.77), channel_id=1, source_target_pairs={{1,0},{2,1},{3,2},{4,3},{5,4},{6,5},{7,6},{8,7},{9,8},{10,9},{11,1... | collective-permute-start | bytes 9368 | tf_op jit(solution)/shard_map/ppermute | solution.py:22
  48.7 5.1 select_add_fusion.2
  53.8 5.0 select_add_fusion.1
  60.6 4.0 collective-permute-start.8
  64.6 5.1 select_add_fusion
  69.7 4.7 collective-permute-done.9
  75.7 3.4 collective-permute-start.10
  81.3 3.2 broadcast_multiply_fusion.4
  86.2 4.3 collective-permute-start.12
  91.8 3.7 collective-permute-done.13
  97.2 4.8 collective-permute-start.14
  101.9 8.6 %collective-permute-done.15 = f32[32,4,6,1]{3,2,1,0:T(8,128)S(1)} collective-permute-done((f32[32,4,6,1]{3,2,1,0:T(8,128)S(1)}, f32[32,4,6,1]{3,2,1,0:T(8,128)S(1)}, u32[]{:S(2)}, u32[]{:S(2)}) %collective-permute-start.15) | collective-permute-done | bytes 3104 | tf_op jit(solution)/shard_map/ppermute | solution.py:22
  111.9 4.5 collective-permute-start.16
  124.6 4.9 collective-permute-start.18
  130.8 5.2 collective-permute-done.19
  137.7 4.8 collective-permute-start.20
  142.6 8.1 %collective-permute-done.21 = f32[32,4,6,1]{3,2,1,0:T(8,128)S(1)} collective-permute-done((f32[32,4,6,1]{3,2,1,0:T(8,128)S(1)}, f32[32,4,6,1]{3,2,1,0:T(8,128)S(1)}, u32[]{:S(2)}, u32[]{:S(2)}) %collective-permute-start.21) | collective-permute-done | bytes 3104 | tf_op jit(solution)/shard_map/ppermute | solution.py:22
  155.7 5.2 collective-permute-start.23
  164.5 3.3 broadcast_multiply_fusion
  167.9 4.6 collective-permute-start.24
  174.8 2.7 collective-permute-done.25
  180.1 4.8 collective-permute-start.26
  185.1 6.9 collective-permute-done.27
  196.4 9.2 %collective-permute-start.29 = (f32[32,1,6,130]{3,2,1,0:T(8,128)S(1)}, f32[32,1,6,130]{3,2,1,0:T(8,128)S(1)}, u32[]{:S(2)}, u32[]{:S(2)}) collective-permute-start(f32[32,1,6,130]{3,2,1,0:T(8,128)S(1)} %get-tuple-element.53), channel_id=1, source_target_pairs={{0,1},{1,2},{2,3},{3,4},{4,5},{5,6},{6,7},{7,8},{8,9},{9,10},{10,1... | collective-permute-start | bytes 299528 | tf_op jit(solution)/shard_map/ppermute | solution.py:19
  212.5 472.8 %all-reduce.3.cloned.1.call-done = f32[160,160]{0,1:T(8,128)} async-done(((f32[160,160]{0,1:T(8,128)}), f32[160,160]{0,1:T(8,128)}) %all-reduce.3.cloned.1.call-update) | async-done | bytes 102416 | tf_op jit(solution)/shard_map/psum | solution.py:88
  687.3 11.7 %cholesky.16 = f32[128,128]{1,0:T(8,128)S(1)} custom-call(f32[128,128]{1,0:T(8,128)S(1)} %fusion.67), custom_call_target="Cholesky" | custom-call | tf_op jit(solution)/shard_map/jit(cholesky)/cholesky | solution.py:92
  700.4 9.8 %custom-call.10 = f32[1,128,128]{1,2,0:T(8,128)S(1)} custom-call(f32[1,128,128]{2,1,0:T(8,128)S(1)} %fusion.61), custom_call_target="InvertDiagBlocksLowerTriangular" | custom-call | tf_op jit(solution)/shard_map/jit(_cho_solve)/triangular_solve | solution.py:93
  (135 shorter events, 68.2 us)
Async XLA Ops:
  7.2 678.1 %all-reduce.3.cloned.1.call-start = ((), (), s32[]{:S(2)}) async-start(), calls=%async_computation | async-start | bytes 327680 | tf_op jit(solution)/shard_map/psum | solution.py:88
  8.0 17.1 %collective-permute-start = (s32[4,1,128]{2,1,0:T(1,128)S(1)}, s32[4,1,128]{2,1,0:T(1,128)S(1)}, u32[]{:S(2)}, u32[]{:S(2)}) collective-permute-start(s32[4,1,128]{2,1,0:T(1,128)S(1)} %get-tuple-element.80), channel_id=1, source_target_pairs={{0,64},{64,128},{128,192},{192,256},{256,320},{320,384},{384,448},... | collective-permute-start | bytes 6152 | tf_op jit(solution)/shard_map/ppermute | solution.py:19
  12.8 12.3 %collective-permute-start.1 = (s32[4,1,128]{2,1,0:T(1,128)S(1)}, s32[4,1,128]{2,1,0:T(1,128)S(1)}, u32[]{:S(2)}, u32[]{:S(2)}) collective-permute-start(s32[4,1,128]{2,1,0:T(1,128)S(1)} %get-tuple-element.81), channel_id=1, source_target_pairs={{64,0},{128,64},{192,128},{256,192},{320,256},{384,320},{448,384},... | collective-permute-start | bytes 6152 | tf_op jit(solution)/shard_map/ppermute | solution.py:22
  18.5 40.4 %collective-permute-start.6 = (f32[32,4,1,128]{3,2,1,0:T(1,128)S(1)}, f32[32,4,1,128]{3,2,1,0:T(1,128)S(1)}, u32[]{:S(2)}, u32[]{:S(2)}) collective-permute-start(f32[32,4,1,128]{3,2,1,0:T(1,128)S(1)} %get-tuple-element.74), channel_id=1, source_target_pairs={{0,64},{64,128},{128,192},{192,256},{256,320},{320,384},{384,448},... | collective-permute-start | bytes 196616 | tf_op jit(solution)/shard_map/ppermute | solution.py:19
  23.1 35.8 %collective-permute-start.7 = (f32[32,4,1,128]{3,2,1,0:T(1,128)S(1)}, f32[32,4,1,128]{3,2,1,0:T(1,128)S(1)}, u32[]{:S(2)}, u32[]{:S(2)}) collective-permute-start(f32[32,4,1,128]{3,2,1,0:T(1,128)S(1)} %get-tuple-element.75), channel_id=1, source_target_pairs={{64,0},{128,64},{192,128},{256,192},{320,256},{384,320},{448,384},... | collective-permute-start | bytes 196616 | tf_op jit(solution)/shard_map/ppermute | solution.py:22
  25.3 4.4 collective-permute-start.2
  28.4 4.5 collective-permute-start.3
  33.0 13.8 %collective-permute-start.4 = (s32[1,6,130]{2,1,0:T(8,128)S(1)}, s32[1,6,130]{2,1,0:T(8,128)S(1)}, u32[]{:S(2)}, u32[]{:S(2)}) collective-permute-start(s32[1,6,130]{2,1,0:T(8,128)S(1)} %get-tuple-element.76), channel_id=1, source_target_pairs={{0,1},{1,2},{2,3},{3,4},{4,5},{5,6},{6,7},{7,8},{8,9},{9,10},{10,1... | collective-permute-start | bytes 9368 | tf_op jit(solution)/shard_map/ppermute | solution.py:19
  38.7 8.1 %collective-permute-start.5 = (s32[1,6,130]{2,1,0:T(8,128)S(1)}, s32[1,6,130]{2,1,0:T(8,128)S(1)}, u32[]{:S(2)}, u32[]{:S(2)}) collective-permute-start(s32[1,6,130]{2,1,0:T(8,128)S(1)} %get-tuple-element.77), channel_id=1, source_target_pairs={{1,0},{2,1},{3,2},{4,3},{5,4},{6,5},{7,6},{8,7},{9,8},{10,9},{11,1... | collective-permute-start | bytes 9368 | tf_op jit(solution)/shard_map/ppermute | solution.py:22
  59.3 15.1 %collective-permute-start.9 = (f32[32,4,6,1]{3,2,1,0:T(8,128)S(1)}, f32[32,4,6,1]{3,2,1,0:T(8,128)S(1)}, u32[]{:S(2)}, u32[]{:S(2)}) collective-permute-start(f32[32,4,6,1]{3,2,1,0:T(8,128)S(1)} %get-tuple-element.66), channel_id=1, source_target_pairs={{16,0},{32,16},{48,32},{17,1},{33,17},{49,33},{18,2},{34,18},{50,3... | collective-permute-start | bytes 9224 | tf_op jit(solution)/shard_map/ppermute | solution.py:22
  60.6 14.6 %collective-permute-start.8 = (f32[32,4,6,1]{3,2,1,0:T(8,128)S(1)}, f32[32,4,6,1]{3,2,1,0:T(8,128)S(1)}, u32[]{:S(2)}, u32[]{:S(2)}) collective-permute-start(f32[32,4,6,1]{3,2,1,0:T(8,128)S(1)} %get-tuple-element.67), channel_id=1, source_target_pairs={{0,16},{16,32},{32,48},{1,17},{17,33},{33,49},{2,18},{18,34},{34,5... | collective-permute-start | bytes 9224 | tf_op jit(solution)/shard_map/ppermute | solution.py:19
  75.7 8.9 %collective-permute-start.10 = (f32[32,1,6,130]{3,2,1,0:T(8,128)S(1)}, f32[32,1,6,130]{3,2,1,0:T(8,128)S(1)}, u32[]{:S(2)}, u32[]{:S(2)}) collective-permute-start(f32[32,1,6,130]{3,2,1,0:T(8,128)S(1)} %get-tuple-element.58), channel_id=1, source_target_pairs={{1,0},{2,1},{3,2},{4,3},{5,4},{6,5},{7,6},{8,7},{9,8},{10,9},{11,1... | collective-permute-start | bytes 299528 | tf_op jit(solution)/shard_map/ppermute | solution.py:22
  79.1 5.5 collective-permute-start.11
  86.2 5.6 collective-permute-start.12
  90.5 5.0 collective-permute-start.13
  95.9 14.6 %collective-permute-start.15 = (f32[32,4,6,1]{3,2,1,0:T(8,128)S(1)}, f32[32,4,6,1]{3,2,1,0:T(8,128)S(1)}, u32[]{:S(2)}, u32[]{:S(2)}) collective-permute-start(f32[32,4,6,1]{3,2,1,0:T(8,128)S(1)} %get-tuple-element.64), channel_id=1, source_target_pairs={{16,0},{32,16},{48,32},{17,1},{33,17},{49,33},{18,2},{34,18},{50,3... | collective-permute-start | bytes 9224 | tf_op jit(solution)/shard_map/ppermute | solution.py:22
  97.2 14.2 %collective-permute-start.14 = (f32[32,4,6,1]{3,2,1,0:T(8,128)S(1)}, f32[32,4,6,1]{3,2,1,0:T(8,128)S(1)}, u32[]{:S(2)}, u32[]{:S(2)}) collective-permute-start(f32[32,4,6,1]{3,2,1,0:T(8,128)S(1)} %get-tuple-element.65), channel_id=1, source_target_pairs={{0,16},{16,32},{32,48},{1,17},{17,33},{33,49},{2,18},{18,34},{34,5... | collective-permute-start | bytes 9224 | tf_op jit(solution)/shard_map/ppermute | solution.py:19
  111.9 9.2 %collective-permute-start.16 = (f32[32,1,6,130]{3,2,1,0:T(8,128)S(1)}, f32[32,1,6,130]{3,2,1,0:T(8,128)S(1)}, u32[]{:S(2)}, u32[]{:S(2)}) collective-permute-start(f32[32,1,6,130]{3,2,1,0:T(8,128)S(1)} %get-tuple-element.56), channel_id=1, source_target_pairs={{1,0},{2,1},{3,2},{4,3},{5,4},{6,5},{7,6},{8,7},{9,8},{10,9},{11,1... | collective-permute-start | bytes 299528 | tf_op jit(solution)/shard_map/ppermute | solution.py:22
  116.5 5.9 collective-permute-start.17
  124.6 6.2 collective-permute-start.18
  129.5 6.5 collective-permute-start.19
  136.4 14.3 %collective-permute-start.21 = (f32[32,4,6,1]{3,2,1,0:T(8,128)S(1)}, f32[32,4,6,1]{3,2,1,0:T(8,128)S(1)}, u32[]{:S(2)}, u32[]{:S(2)}) collective-permute-start(f32[32,4,6,1]{3,2,1,0:T(8,128)S(1)} %get-tuple-element.62), channel_id=1, source_target_pairs={{16,0},{32,16},{48,32},{17,1},{33,17},{49,33},{18,2},{34,18},{50,3... | collective-permute-start | bytes 9224 | tf_op jit(solution)/shard_map/ppermute | solution.py:22
  137.7 14.7 %collective-permute-start.20 = (f32[32,4,6,1]{3,2,1,0:T(8,128)S(1)}, f32[32,4,6,1]{3,2,1,0:T(8,128)S(1)}, u32[]{:S(2)}, u32[]{:S(2)}) collective-permute-start(f32[32,4,6,1]{3,2,1,0:T(8,128)S(1)} %get-tuple-element.63), channel_id=1, source_target_pairs={{0,16},{16,32},{32,48},{1,17},{17,33},{33,49},{2,18},{18,34},{34,5... | collective-permute-start | bytes 9224 | tf_op jit(solution)/shard_map/ppermute | solution.py:19
  153.7 9.6 %collective-permute-start.22 = (f32[32,1,6,130]{3,2,1,0:T(8,128)}, f32[32,1,6,130]{3,2,1,0:T(8,128)}, u32[]{:S(2)}, u32[]{:S(2)}) collective-permute-start(f32[32,1,6,130]{3,2,1,0:T(8,128)} %get-tuple-element.54), channel_id=1, source_target_pairs={{1,0},{2,1},{3,2},{4,3},{5,4},{6,5},{7,6},{8,7},{9,8},{10,9},{11,1... | collective-permute-start | bytes 299528 | tf_op jit(solution)/shard_map/ppermute | solution.py:22
  155.7 8.8 %collective-permute-start.23 = (f32[32,1,6,130]{3,2,1,0:T(8,128)}, f32[32,1,6,130]{3,2,1,0:T(8,128)}, u32[]{:S(2)}, u32[]{:S(2)}) collective-permute-start(f32[32,1,6,130]{3,2,1,0:T(8,128)} %get-tuple-element.55), channel_id=1, source_target_pairs={{0,1},{1,2},{2,3},{3,4},{4,5},{5,6},{6,7},{7,8},{8,9},{9,10},{10,1... | collective-permute-start | bytes 299528 | tf_op jit(solution)/shard_map/ppermute | solution.py:19
  167.9 6.9 collective-permute-start.24
  172.5 5.0 collective-permute-start.25
  178.9 13.2 %collective-permute-start.27 = (f32[32,4,6,1]{3,2,1,0:T(8,128)}, f32[32,4,6,1]{3,2,1,0:T(8,128)S(1)}, u32[]{:S(2)}, u32[]{:S(2)}) collective-permute-start(f32[32,4,6,1]{3,2,1,0:T(8,128)} %get-tuple-element.60), channel_id=1, source_target_pairs={{16,0},{32,16},{48,32},{17,1},{33,17},{49,33},{18,2},{34,18},{50,3... | collective-permute-start | bytes 9224 | tf_op jit(solution)/shard_map/ppermute | solution.py:22
  180.1 13.8 %collective-permute-start.26 = (f32[32,4,6,1]{3,2,1,0:T(8,128)}, f32[32,4,6,1]{3,2,1,0:T(8,128)S(1)}, u32[]{:S(2)}, u32[]{:S(2)}) collective-permute-start(f32[32,4,6,1]{3,2,1,0:T(8,128)} %get-tuple-element.61), channel_id=1, source_target_pairs={{0,16},{16,32},{32,48},{1,17},{17,33},{33,49},{2,18},{18,34},{34,5... | collective-permute-start | bytes 9224 | tf_op jit(solution)/shard_map/ppermute | solution.py:19
  194.5 13.3 %collective-permute-start.28 = (f32[32,1,6,130]{3,2,1,0:T(8,128)S(1)}, f32[32,1,6,130]{3,2,1,0:T(8,128)S(1)}, u32[]{:S(2)}, u32[]{:S(2)}) collective-permute-start(f32[32,1,6,130]{3,2,1,0:T(8,128)S(1)} %get-tuple-element.52), channel_id=1, source_target_pairs={{1,0},{2,1},{3,2},{4,3},{5,4},{6,5},{7,6},{8,7},{9,8},{10,9},{11,1... | collective-permute-start | bytes 299528 | tf_op jit(solution)/shard_map/ppermute | solution.py:22
  196.4 12.5 %collective-permute-start.29 = (f32[32,1,6,130]{3,2,1,0:T(8,128)S(1)}, f32[32,1,6,130]{3,2,1,0:T(8,128)S(1)}, u32[]{:S(2)}, u32[]{:S(2)}) collective-permute-start(f32[32,1,6,130]{3,2,1,0:T(8,128)S(1)} %get-tuple-element.53), channel_id=1, source_target_pairs={{0,1},{1,2},{2,3},{3,4},{4,5},{5,6},{6,7},{7,8},{8,9},{9,10},{10,1... | collective-permute-start | bytes 299528 | tf_op jit(solution)/shard_map/ppermute | solution.py:19
  212.5 499.0 %copy-start.3 = (f32[32,2048]{1,0:T(8,128)S(1)}, f32[32,2048]{1,0:T(8,128)}, u32[]{:S(2)}) copy-start(f32[32,2048]{1,0:T(8,128)} %copy-done.2) | copy-start | bytes 786436
  (16 other events, 900.3 us)
Sparse Core Ops, SparseCore 0:
  212.6 472.6 all-reduce.2
where the time goes:
time: 724 us; the launch traced here: 722 us
  waiting for transfers between devices  531 us (73%)
  starting transfers between devices  102 us (14%)
  other arithmetic  58.9 us (8%)
  between operations  14.8 us (2%)
  local copies, waits for them, and re-layouts  9.74 us (1%)
    psum x1, waiting for transfers between devices, body(): gram = lax.psum(partial_gram, ('gx', 'gy', 'gz'))  473 us
    ppermute x15, starting transfers between devices, padded_2(): lax.ppermute(lax.slice_in_dim(block, block.shape[dim] - width, None, axis...  69.5 us
    ppermute x15, waiting for transfers between devices, padded_2(): lax.ppermute(lax.slice_in_dim(block, 0, width, axis=dim), axis, backward)  49.6 us
    ppermute x15, starting transfers between devices, padded_2(): lax.ppermute(lax.slice_in_dim(block, 0, width, axis=dim), axis, backward)  32.2 us
    add x4, other arithmetic, region_fields(): fields[column] + hit * region_table[region, column]  16.5 us
  transfers between devices with their start and end apart: 31, of which 20 were waited for; matrix products, arithmetic and copies ran while one was open for 4% of the time, Pallas kernels for 0%

commit v1 on v0

--- a/solution.py
+++ b/solution.py
@@ -64,6 +64,18 @@
     return (image - SIGMA * center) / THETA
 
 
+def total(values):
+    parts = lax.axis_size("gz")
+    others = lax.axis_size("gx") * lax.axis_size("gy")
+    pieces = lax.all_to_all(values.reshape(parts, -1, 128), "gz", 0, 0)
+    piece = pieces.sum(0)
+    pieces = lax.all_to_all(
+        jnp.broadcast_to(piece, (others,) + piece.shape), ("gx", "gy"), 0, 0
+    )
+    piece = pieces.sum(0)
+    return lax.all_to_all(jnp.broadcast_to(piece, (parts,) + piece.shape), "gz", 0, 0)
+
+
 def body(sources, labels, region_table, sweep_index, sweep_gain):
     count = sources.shape[0]
     gain_rows = sweep_gain[sweep_index]
@@ -82,15 +94,27 @@
         current = next_power(padded, faces, diag)
         basis.append(current)
     flat = jnp.concatenate([block.reshape(count, -1) for block in basis], 0)
-    partial_gram = jnp.dot(
-        flat, flat.T, precision=lax.Precision.HIGHEST, preferred_element_type=jnp.float32
+    flats = [block.reshape(count, -1) for block in basis]
+    moments = []
+    for order in range(2 * S):
+        moments.append(
+            lax.dot_general(
+                flats[order // 2],
+                flats[order - order // 2],
+                (((1,), (1,)), ((), ())),
+                precision=lax.Precision.HIGHEST,
+                preferred_element_type=jnp.float32,
+            )
+        )
+    moments = total(jnp.stack(moments)).reshape(2 * S, count, count)
+    width = S * count
+    sums = THETA * moments[1:] + SIGMA * moments[:-1]
+    mat = jnp.concatenate(
+        [jnp.concatenate([sums[i + j] for j in range(S)], 1) for i in range(S)], 0
     )
-    gram = lax.psum(partial_gram, ("gx", "gy", "gz"))
-    width = S * count
-    mat = THETA * gram[:width, count:] + SIGMA * gram[:width, :width]
     mat = 0.5 * (mat + mat.T)
     factor = jnp.linalg.cholesky(mat)
-    coef = jax.scipy.linalg.cho_solve((factor, True), gram[:width, :count])
+    coef = jax.scipy.linalg.cho_solve((factor, True), moments[:S].reshape(width, count))
     combo = jnp.zeros(((S + 1) * count, count), jnp.float32)
     combo = combo.at[:width].add(SIGMA * coef)
     combo = combo.at[count:].add(THETA * coef)

time: 724 us -> 294 us (0.41)
  waiting for transfers between devices: 531 us -> 85.6 us
  starting transfers between devices: 102 us -> 134 us
  between operations: 14.8 us -> 1.44 us
    psum x1 -> x0, waiting for transfers between devices: 473 us -> none  [body(): gram = lax.psum(partial_gram, ('gx', 'gy', 'gz'))]
    all_to_all x0 -> x3, starting transfers between devices: none -> 32.1 us  [the longest x1 19.5 us: total(): lax.all_to_all(jnp.broadcast_to(piece, (others,) + piece.shape), ('gx', '...]
    all_to_all x0 -> x3, waiting for transfers between devices: none -> 29.5 us  [the longest x1 14.7 us: total(): lax.all_to_all(jnp.broadcast_to(piece, (others,) + piece.shape), ('gx', '...]
  transfers between devices with their start and end apart: 31 -> 33, of which waited for: 20 -> 22; matrix products, arithmetic and copies ran while one was open for 4% -> 10% of each run, Pallas kernels for 0% -> 0%
where the time goes in v1:
time: 294 us; the launch traced here: 292 us
  starting transfers between devices  134 us (46%)
  waiting for transfers between devices  85.6 us (29%)
  other arithmetic  54.3 us (18%)
  local copies, waits for them, and re-layouts  11 us (4%)
  matrix products  6.3 us (2%)
    ppermute x15, starting transfers between devices, padded_2(): lax.ppermute(lax.slice_in_dim(block, block.shape[dim] - width, None, axis...  69.8 us
    ppermute x15, waiting for transfers between devices, padded_2(): lax.ppermute(lax.slice_in_dim(block, 0, width, axis=dim), axis, backward)  47.3 us
    ppermute x15, starting transfers between devices, padded_2(): lax.ppermute(lax.slice_in_dim(block, 0, width, axis=dim), axis, backward)  32 us
    all_to_all x1, starting transfers between devices, total(): lax.all_to_all(jnp.broadcast_to(piece, (others,) + piece.shape), ('gx', '...  19.5 us
    add x4, other arithmetic, region_fields(): fields[column] + hit * region_table[region, column]  16.6 us
    all_to_all x1, waiting for transfers between devices, total(): lax.all_to_all(jnp.broadcast_to(piece, (others,) + piece.shape), ('gx', '...  14.7 us
    another operation x3, other arithmetic, body(): factor = jnp.linalg.cholesky(mat)  12.4 us
    another operation x2, other arithmetic, body(): jax.scipy.linalg.cho_solve((factor, True), moments[:S].reshape(width, cou...  10.5 us
  transfers between devices with their start and end apart: 33, of which 22 were waited for; matrix products, arithmetic and copies ran while one was open for 10% of the time, Pallas kernels for 0%

profile of v1, /device:TPU:1, one launch (start us, length us, event | category | flops | bytes accessed | tf_op | source)
XLA Modules:
  0.0 292.5 jit_solution(11812765431501253606)
XLA Ops:
  1.4 4.8 %collective-permute-start = (s32[4,1,128]{2,1,0:T(1,128)S(1)}, s32[4,1,128]{2,1,0:T(1,128)S(1)}, u32[]{:S(2)}, u32[]{:S(2)}) collective-permute-start(s32[4,1,128]{2,1,0:T(1,128)S(1)} %get-tuple-element.91), channel_id=1, source_target_pairs={{0,64},{64,128},{128,192},{192,256},{256,320},{320,384},{384,448},... | collective-permute-start | bytes 6152 | tf_op jit(solution)/shard_map/ppermute | solution.py:19
  11.9 4.6 %collective-permute-start.6 = (f32[32,4,1,128]{3,2,1,0:T(1,128)S(1)}, f32[32,4,1,128]{3,2,1,0:T(1,128)S(1)}, u32[]{:S(2)}, u32[]{:S(2)}) collective-permute-start(f32[32,4,1,128]{3,2,1,0:T(1,128)S(1)} %get-tuple-element.74), channel_id=1, source_target_pairs={{0,64},{64,128},{128,192},{192,256},{256,320},{320,384},{384,448},... | collective-permute-start | bytes 196616 | tf_op jit(solution)/shard_map/ppermute | solution.py:19
  26.4 5.8 %collective-permute-start.4 = (s32[1,6,130]{2,1,0:T(8,128)S(1)}, s32[1,6,130]{2,1,0:T(8,128)S(1)}, u32[]{:S(2)}, u32[]{:S(2)}) collective-permute-start(s32[1,6,130]{2,1,0:T(8,128)S(1)} %get-tuple-element.80), channel_id=1, source_target_pairs={{0,1},{1,2},{2,3},{3,4},{4,5},{5,6},{6,7},{7,8},{8,9},{9,10},{10,1... | collective-permute-start | bytes 9368 | tf_op jit(solution)/shard_map/ppermute | solution.py:19
  32.2 7.3 %collective-permute-start.5 = (s32[1,6,130]{2,1,0:T(8,128)S(1)}, s32[1,6,130]{2,1,0:T(8,128)S(1)}, u32[]{:S(2)}, u32[]{:S(2)}) collective-permute-start(s32[1,6,130]{2,1,0:T(8,128)S(1)} %get-tuple-element.81), channel_id=1, source_target_pairs={{1,0},{2,1},{3,2},{4,3},{5,4},{6,5},{7,6},{8,7},{9,8},{10,9},{11,1... | collective-permute-start | bytes 9368 | tf_op jit(solution)/shard_map/ppermute | solution.py:22
  42.3 5.2 %select_add_fusion.2 = (f32[6,6,130]{2,1,0:T(8,128)S(1)}, pred[6,6,130]{2,1,0:T(8,128)(4,1)S(1)}, pred[6,6,130]{2,1,0:T(8,128)(4,1)S(1)}, pred[6,6,130]{2,1,0:T(...) fusion(pred[6,6,130]{2,1,0:T(8,128)(4,1)S(1)} %get-tuple-element.45, ...), kind=kLoop, calls=%fused_computation.209 | loop fusion | flops 93600 | bytes 74912 | tf_op jit(solution)/shard_map/add | solution.py:31
  47.4 5.0 %select_add_fusion.1 = f32[6,6,130]{2,1,0:T(8,128)S(1)} fusion(pred[6,6,130]{2,1,0:T(8,128)(4,1)S(1)} %get-tuple-element.51, pred[6,6,130]{2,1,0:T(8,128)(4,1)S(1)} %get-tuple-element.50, pred[6,6,130]{2,1,0:T(8,128)(4,1)S(1)} %get-tuple-element.49, pred[6,6,130]{2,1,0:T(8,128)(4,1)S(1)} %get-tuple-element.48, pred[6,6,130]{2,1,0:T(8,128)(4,1)S(1)} %get-tuple-element.47, ...), kind=kLoop, calls=%fused_computation.208 | loop fusion | flops 70200 | bytes 56192 | tf_op jit(solution)/shard_map/add | solution.py:31
  54.2 4.0 %collective-permute-start.8 = (f32[32,4,6,1]{3,2,1,0:T(8,128)S(1)}, f32[32,4,6,1]{3,2,1,0:T(8,128)S(1)}, u32[]{:S(2)}, u32[]{:S(2)}) collective-permute-start(f32[32,4,6,1]{3,2,1,0:T(8,128)S(1)} %get-tuple-element.67), channel_id=1, source_target_pairs={{0,16},{16,32},{32,48},{1,17},{17,33},{33,49},{2,18},{18,34},{34,5... | collective-permute-start | bytes 9224 | tf_op jit(solution)/shard_map/ppermute | solution.py:19
  58.2 5.0 %select_add_fusion = f32[6,6,130]{2,1,0:T(8,128)S(1)} fusion(pred[6,6,130]{2,1,0:T(8,128)(4,1)S(1)} %get-tuple-element.51, pred[6,6,130]{2,1,0:T(8,128)(4,1)S(1)} %get-tuple-element.50, pred[6,6,130]{2,1,0:T(8,128)(4,1)S(1)} %get-tuple-element.49, pred[6,6,130]{2,1,0:T(8,128)(4,1)S(1)} %get-tuple-element.48, pred[6,6,130]{2,1,0:T(8,128)(4,1)S(1)} %get-tuple-element.47, ...), kind=kLoop, calls=%fused_computation.207 | loop fusion | flops 70200 | bytes 56192 | tf_op jit(solution)/shard_map/add | solution.py:31
  63.2 4.7 %collective-permute-done.9 = f32[32,4,6,1]{3,2,1,0:T(8,128)S(1)} collective-permute-done((f32[32,4,6,1]{3,2,1,0:T(8,128)S(1)}, f32[32,4,6,1]{3,2,1,0:T(8,128)S(1)}, u32[]{:S(2)}, u32[]{:S(2)}) %collective-permute-start.9) | collective-permute-done | bytes 3104 | tf_op jit(solution)/shard_map/ppermute | solution.py:22
  69.3 3.4 %collective-permute-start.10 = (f32[32,1,6,130]{3,2,1,0:T(8,128)S(1)}, f32[32,1,6,130]{3,2,1,0:T(8,128)S(1)}, u32[]{:S(2)}, u32[]{:S(2)}) collective-permute-start(f32[32,1,6,130]{3,2,1,0:T(8,128)S(1)} %get-tuple-element.58), channel_id=1, source_target_pairs={{1,0},{2,1},{3,2},{4,3},{5,4},{6,5},{7,6},{8,7},{9,8},{10,9},{11,1... | collective-permute-start | bytes 299528 | tf_op jit(solution)/shard_map/ppermute | solution.py:22
  79.8 4.3 %collective-permute-start.12 = (f32[32,4,1,128]{3,2,1,0:T(1,128)S(1)}, f32[32,4,1,128]{3,2,1,0:T(1,128)S(1)}, u32[]{:S(2)}, u32[]{:S(2)}) collective-permute-start(f32[32,4,1,128]{3,2,1,0:T(1,128)S(1)} %get-tuple-element.72), channel_id=1, source_target_pairs={{0,64},{64,128},{128,192},{192,256},{256,320},{320,384},{384,448},... | collective-permute-start | bytes 196616 | tf_op jit(solution)/shard_map/ppermute | solution.py:19
  85.4 3.7 %collective-permute-done.13 = f32[32,4,1,128]{3,2,1,0:T(1,128)S(1)} collective-permute-done((f32[32,4,1,128]{3,2,1,0:T(1,128)S(1)}, f32[32,4,1,128]{3,2,1,0:T(1,128)S(1)}, u32[]{:S(2)}, u32[]{:S(2)}) %collective-permute-start.13) | collective-permute-done | bytes 65568 | tf_op jit(solution)/shard_map/ppermute | solution.py:22
  90.8 4.8 %collective-permute-start.14 = (f32[32,4,6,1]{3,2,1,0:T(8,128)S(1)}, f32[32,4,6,1]{3,2,1,0:T(8,128)S(1)}, u32[]{:S(2)}, u32[]{:S(2)}) collective-permute-start(f32[32,4,6,1]{3,2,1,0:T(8,128)S(1)} %get-tuple-element.65), channel_id=1, source_target_pairs={{0,16},{16,32},{32,48},{1,17},{17,33},{33,49},{2,18},{18,34},{34,5... | collective-permute-start | bytes 9224 | tf_op jit(solution)/shard_map/ppermute | solution.py:19
  95.5 8.6 %collective-permute-done.15 = f32[32,4,6,1]{3,2,1,0:T(8,128)S(1)} collective-permute-done((f32[32,4,6,1]{3,2,1,0:T(8,128)S(1)}, f32[32,4,6,1]{3,2,1,0:T(8,128)S(1)}, u32[]{:S(2)}, u32[]{:S(2)}) %collective-permute-start.15) | collective-permute-done | bytes 3104 | tf_op jit(solution)/shard_map/ppermute | solution.py:22
  105.6 4.5 %collective-permute-start.16 = (f32[32,1,6,130]{3,2,1,0:T(8,128)S(1)}, f32[32,1,6,130]{3,2,1,0:T(8,128)S(1)}, u32[]{:S(2)}, u32[]{:S(2)}) collective-permute-start(f32[32,1,6,130]{3,2,1,0:T(8,128)S(1)} %get-tuple-element.56), channel_id=1, source_target_pairs={{1,0},{2,1},{3,2},{4,3},{5,4},{6,5},{7,6},{8,7},{9,8},{10,9},{11,1... | collective-permute-start | bytes 299528 | tf_op jit(solution)/shard_map/ppermute | solution.py:22
  117.5 4.9 %collective-permute-start.18 = (f32[32,4,1,128]{3,2,1,0:T(1,128)S(1)}, f32[32,4,1,128]{3,2,1,0:T(1,128)S(1)}, u32[]{:S(2)}, u32[]{:S(2)}) collective-permute-start(f32[32,4,1,128]{3,2,1,0:T(1,128)S(1)} %get-tuple-element.70), channel_id=1, source_target_pairs={{0,64},{64,128},{128,192},{192,256},{256,320},{320,384},{384,448},... | collective-permute-start | bytes 196616 | tf_op jit(solution)/shard_map/ppermute | solution.py:19
  124.1 4.7 %collective-permute-done.19 = f32[32,4,1,128]{3,2,1,0:T(1,128)S(1)} collective-permute-done((f32[32,4,1,128]{3,2,1,0:T(1,128)S(1)}, f32[32,4,1,128]{3,2,1,0:T(1,128)S(1)}, u32[]{:S(2)}, u32[]{:S(2)}) %collective-permute-start.19) | collective-permute-done | bytes 65568 | tf_op jit(solution)/shard_map/ppermute | solution.py:22
  130.5 4.8 %collective-permute-start.20 = (f32[32,4,6,1]{3,2,1,0:T(8,128)S(1)}, f32[32,4,6,1]{3,2,1,0:T(8,128)S(1)}, u32[]{:S(2)}, u32[]{:S(2)}) collective-permute-start(f32[32,4,6,1]{3,2,1,0:T(8,128)S(1)} %get-tuple-element.63), channel_id=1, source_target_pairs={{0,16},{16,32},{32,48},{1,17},{17,33},{33,49},{2,18},{18,34},{34,5... | collective-permute-start | bytes 9224 | tf_op jit(solution)/shard_map/ppermute | solution.py:19
  135.7 7.8 %collective-permute-done.21 = f32[32,4,6,1]{3,2,1,0:T(8,128)S(1)} collective-permute-done((f32[32,4,6,1]{3,2,1,0:T(8,128)S(1)}, f32[32,4,6,1]{3,2,1,0:T(8,128)S(1)}, u32[]{:S(2)}, u32[]{:S(2)}) %collective-permute-start.21) | collective-permute-done | bytes 3104 | tf_op jit(solution)/shard_map/ppermute | solution.py:22
  147.7 5.5 %collective-permute-start.23 = (f32[32,1,6,130]{3,2,1,0:T(8,128)S(1)}, f32[32,1,6,130]{3,2,1,0:T(8,128)S(1)}, u32[]{:S(2)}, u32[]{:S(2)}) collective-permute-start(f32[32,1,6,130]{3,2,1,0:T(8,128)S(1)} %get-tuple-element.55), channel_id=1, source_target_pairs={{0,1},{1,2},{2,3},{3,4},{4,5},{5,6},{6,7},{7,8},{8,9},{9,10},{10,1... | collective-permute-start | bytes 299528 | tf_op jit(solution)/shard_map/ppermute | solution.py:19
  157.8 4.6 %collective-permute-start.24 = (f32[32,4,1,128]{3,2,1,0:T(1,128)S(1)}, f32[32,4,1,128]{3,2,1,0:T(1,128)S(1)}, u32[]{:S(2)}, u32[]{:S(2)}) collective-permute-start(f32[32,4,1,128]{3,2,1,0:T(1,128)S(1)} %get-tuple-element.68), channel_id=1, source_target_pairs={{0,64},{64,128},{128,192},{192,256},{256,320},{320,384},{384,448},... | collective-permute-start | bytes 196616 | tf_op jit(solution)/shard_map/ppermute | solution.py:19
  169.1 4.8 %collective-permute-start.26 = (f32[32,4,6,1]{3,2,1,0:T(8,128)S(1)}, f32[32,4,6,1]{3,2,1,0:T(8,128)S(1)}, u32[]{:S(2)}, u32[]{:S(2)}) collective-permute-start(f32[32,4,6,1]{3,2,1,0:T(8,128)S(1)} %get-tuple-element.61), channel_id=1, source_target_pairs={{0,16},{16,32},{32,48},{1,17},{17,33},{33,49},{2,18},{18,34},{34,5... | collective-permute-start | bytes 9224 | tf_op jit(solution)/shard_map/ppermute | solution.py:19
  174.4 6.4 %collective-permute-done.27 = f32[32,4,6,1]{3,2,1,0:T(8,128)S(1)} collective-permute-done((f32[32,4,6,1]{3,2,1,0:T(8,128)S(1)}, f32[32,4,6,1]{3,2,1,0:T(8,128)S(1)}, u32[]{:S(2)}, u32[]{:S(2)}) %collective-permute-start.27) | collective-permute-done | bytes 3104 | tf_op jit(solution)/shard_map/ppermute | solution.py:22
  185.0 9.3 %collective-permute-start.29 = (f32[32,1,6,130]{3,2,1,0:T(8,128)S(1)}, f32[32,1,6,130]{3,2,1,0:T(8,128)S(1)}, u32[]{:S(2)}, u32[]{:S(2)}) collective-permute-start(f32[32,1,6,130]{3,2,1,0:T(8,128)S(1)} %get-tuple-element.53), channel_id=1, source_target_pairs={{0,1},{1,2},{2,3},{3,4},{4,5},{5,6},{6,7},{7,8},{8,9},{9,10},{10,1... | collective-permute-start | bytes 299528 | tf_op jit(solution)/shard_map/ppermute | solution.py:19
  200.3 5.9 %all-to-all-start = ((f32[16,4,128]{2,1,0:T(4,128)}), f32[16,4,128]{2,1,0:T(4,128)S(1)}, u32[]{:S(2)}, u32[]{:S(2)}) async-start(f32[16,4,128]{2,1,0:T(4,128)} %reshape.135), calls=%async_computation | async-start | bytes 65536 | tf_op jit(solution)/shard_map/all_to_all | solution.py:70
  206.3 7.3 %all-to-all-done = f32[16,4,128]{2,1,0:T(4,128)S(1)} async-done(((f32[16,4,128]{2,1,0:T(4,128)}), f32[16,4,128]{2,1,0:T(4,128)S(1)}, u32[]{:S(2)}, u32[]{:S(2)}) %all-to-all-start) | async-done | bytes 32800 | tf_op jit(solution)/shard_map/all_to_all | solution.py:70
  214.3 19.5 %all-to-all-start.1 = ((f32[64,4,128]{2,1,0:T(4,128)}), f32[64,4,128]{2,1,0:T(4,128)S(1)}, u32[]{:S(2)}, u32[]{:S(2)}) async-start(f32[64,4,128]{2,1,0:T(4,128)} %broadcast_in_dim.8), calls=%async_computation.1 | async-start | bytes 262144 | tf_op jit(solution)/shard_map/all_to_all | solution.py:72
  234.1 14.7 %all-to-all-done.1 = f32[64,4,128]{2,1,0:T(4,128)S(1)} async-done(((f32[64,4,128]{2,1,0:T(4,128)}), f32[64,4,128]{2,1,0:T(4,128)S(1)}, u32[]{:S(2)}, u32[]{:S(2)}) %all-to-all-start.1) | async-done | bytes 131104 | tf_op jit(solution)/shard_map/all_to_all | solution.py:72
  249.6 6.7 %all-to-all-start.2 = ((f32[16,4,128]{2,1,0:T(4,128)}), f32[16,4,128]{2,1,0:T(4,128)S(1)}, u32[]{:S(2)}, u32[]{:S(2)}) async-start(f32[16,4,128]{2,1,0:T(4,128)} %broadcast_in_dim.9), calls=%async_computation.2 | async-start | bytes 65536 | tf_op jit(solution)/shard_map/all_to_all | solution.py:76
  256.3 7.5 %all-to-all-done.2 = f32[16,4,128]{2,1,0:T(4,128)S(1)} async-done(((f32[16,4,128]{2,1,0:T(4,128)}), f32[16,4,128]{2,1,0:T(4,128)S(1)}, u32[]{:S(2)}, u32[]{:S(2)}) %all-to-all-start.2) | async-done | bytes 32800 | tf_op jit(solution)/shard_map/all_to_all | solution.py:76
  265.5 11.7 %cholesky.16 = f32[128,128]{1,0:T(8,128)S(1)} custom-call(f32[128,128]{1,0:T(8,128)S(1)} %fusion.86), custom_call_target="Cholesky" | custom-call | tf_op jit(solution)/shard_map/jit(cholesky)/cholesky | solution.py:116
  278.5 9.8 %custom-call.10 = f32[1,128,128]{1,2,0:T(8,128)S(1)} custom-call(f32[1,128,128]{2,1,0:T(8,128)S(1)} %fusion.81), custom_call_target="InvertDiagBlocksLowerTriangular" | custom-call | tf_op jit(solution)/shard_map/jit(_cho_solve)/triangular_solve | solution.py:117
  (136 shorter events, 79.7 us)
Async XLA Ops:
  1.4 17.1 %collective-permute-start = (s32[4,1,128]{2,1,0:T(1,128)S(1)}, s32[4,1,128]{2,1,0:T(1,128)S(1)}, u32[]{:S(2)}, u32[]{:S(2)}) collective-permute-start(s32[4,1,128]{2,1,0:T(1,128)S(1)} %get-tuple-element.91), channel_id=1, source_target_pairs={{0,64},{64,128},{128,192},{192,256},{256,320},{320,384},{384,448},... | collective-permute-start | bytes 6152 | tf_op jit(solution)/shard_map/ppermute | solution.py:19
  6.3 12.3 %collective-permute-start.1 = (s32[4,1,128]{2,1,0:T(1,128)S(1)}, s32[4,1,128]{2,1,0:T(1,128)S(1)}, u32[]{:S(2)}, u32[]{:S(2)}) collective-permute-start(s32[4,1,128]{2,1,0:T(1,128)S(1)} %get-tuple-element.92), channel_id=1, source_target_pairs={{64,0},{128,64},{192,128},{256,192},{320,256},{384,320},{448,384},... | collective-permute-start | bytes 6152 | tf_op jit(solution)/shard_map/ppermute | solution.py:22
  11.9 40.6 %collective-permute-start.6 = (f32[32,4,1,128]{3,2,1,0:T(1,128)S(1)}, f32[32,4,1,128]{3,2,1,0:T(1,128)S(1)}, u32[]{:S(2)}, u32[]{:S(2)}) collective-permute-start(f32[32,4,1,128]{3,2,1,0:T(1,128)S(1)} %get-tuple-element.74), channel_id=1, source_target_pairs={{0,64},{64,128},{128,192},{192,256},{256,320},{320,384},{384,448},... | collective-permute-start | bytes 196616 | tf_op jit(solution)/shard_map/ppermute | solution.py:19
  16.5 35.9 %collective-permute-start.7 = (f32[32,4,1,128]{3,2,1,0:T(1,128)S(1)}, f32[32,4,1,128]{3,2,1,0:T(1,128)S(1)}, u32[]{:S(2)}, u32[]{:S(2)}) collective-permute-start(f32[32,4,1,128]{3,2,1,0:T(1,128)S(1)} %get-tuple-element.75), channel_id=1, source_target_pairs={{64,0},{128,64},{192,128},{256,192},{320,256},{384,320},{448,384},... | collective-permute-start | bytes 196616 | tf_op jit(solution)/shard_map/ppermute | solution.py:22
  21.8 4.5 %collective-permute-start.3 = (s32[4,6,1]{2,1,0:T(8,128)S(1)}, s32[4,6,1]{2,1,0:T(8,128)S(1)}, u32[]{:S(2)}, u32[]{:S(2)}) collective-permute-start(s32[4,6,1]{2,1,0:T(8,128)S(1)} %get-tuple-element.90), channel_id=1, source_target_pairs={{16,0},{32,16},{48,32},{17,1},{33,17},{49,33},{18,2},{34,18},{50,3... | collective-permute-start | bytes 296 | tf_op jit(solution)/shard_map/ppermute | solution.py:22
  26.4 13.8 %collective-permute-start.4 = (s32[1,6,130]{2,1,0:T(8,128)S(1)}, s32[1,6,130]{2,1,0:T(8,128)S(1)}, u32[]{:S(2)}, u32[]{:S(2)}) collective-permute-start(s32[1,6,130]{2,1,0:T(8,128)S(1)} %get-tuple-element.80), channel_id=1, source_target_pairs={{0,1},{1,2},{2,3},{3,4},{4,5},{5,6},{6,7},{7,8},{8,9},{9,10},{10,1... | collective-permute-start | bytes 9368 | tf_op jit(solution)/shard_map/ppermute | solution.py:19
  32.2 8.1 %collective-permute-start.5 = (s32[1,6,130]{2,1,0:T(8,128)S(1)}, s32[1,6,130]{2,1,0:T(8,128)S(1)}, u32[]{:S(2)}, u32[]{:S(2)}) collective-permute-start(s32[1,6,130]{2,1,0:T(8,128)S(1)} %get-tuple-element.81), channel_id=1, source_target_pairs={{1,0},{2,1},{3,2},{4,3},{5,4},{6,5},{7,6},{8,7},{9,8},{10,9},{11,1... | collective-permute-start | bytes 9368 | tf_op jit(solution)/shard_map/ppermute | solution.py:22
  52.9 15.1 %collective-permute-start.9 = (f32[32,4,6,1]{3,2,1,0:T(8,128)S(1)}, f32[32,4,6,1]{3,2,1,0:T(8,128)S(1)}, u32[]{:S(2)}, u32[]{:S(2)}) collective-permute-start(f32[32,4,6,1]{3,2,1,0:T(8,128)S(1)} %get-tuple-element.66), channel_id=1, source_target_pairs={{16,0},{32,16},{48,32},{17,1},{33,17},{49,33},{18,2},{34,18},{50,3... | collective-permute-start | bytes 9224 | tf_op jit(solution)/shard_map/ppermute | solution.py:22
  54.2 14.6 %collective-permute-start.8 = (f32[32,4,6,1]{3,2,1,0:T(8,128)S(1)}, f32[32,4,6,1]{3,2,1,0:T(8,128)S(1)}, u32[]{:S(2)}, u32[]{:S(2)}) collective-permute-start(f32[32,4,6,1]{3,2,1,0:T(8,128)S(1)} %get-tuple-element.67), channel_id=1, source_target_pairs={{0,16},{16,32},{32,48},{1,17},{17,33},{33,49},{2,18},{18,34},{34,5... | collective-permute-start | bytes 9224 | tf_op jit(solution)/shard_map/ppermute | solution.py:19
  69.3 8.8 %collective-permute-start.10 = (f32[32,1,6,130]{3,2,1,0:T(8,128)S(1)}, f32[32,1,6,130]{3,2,1,0:T(8,128)S(1)}, u32[]{:S(2)}, u32[]{:S(2)}) collective-permute-start(f32[32,1,6,130]{3,2,1,0:T(8,128)S(1)} %get-tuple-element.58), channel_id=1, source_target_pairs={{1,0},{2,1},{3,2},{4,3},{5,4},{6,5},{7,6},{8,7},{9,8},{10,9},{11,1... | collective-permute-start | bytes 299528 | tf_op jit(solution)/shard_map/ppermute | solution.py:22
  72.8 5.5 %collective-permute-start.11 = (f32[32,1,6,130]{3,2,1,0:T(8,128)S(1)}, f32[32,1,6,130]{3,2,1,0:T(8,128)S(1)}, u32[]{:S(2)}, u32[]{:S(2)}) collective-permute-start(f32[32,1,6,130]{3,2,1,0:T(8,128)S(1)} %get-tuple-element.59), channel_id=1, source_target_pairs={{0,1},{1,2},{2,3},{3,4},{4,5},{5,6},{6,7},{7,8},{8,9},{9,10},{10,1... | collective-permute-start | bytes 299528 | tf_op jit(solution)/shard_map/ppermute | solution.py:19
  79.8 5.6 %collective-permute-start.12 = (f32[32,4,1,128]{3,2,1,0:T(1,128)S(1)}, f32[32,4,1,128]{3,2,1,0:T(1,128)S(1)}, u32[]{:S(2)}, u32[]{:S(2)}) collective-permute-start(f32[32,4,1,128]{3,2,1,0:T(1,128)S(1)} %get-tuple-element.72), channel_id=1, source_target_pairs={{0,64},{64,128},{128,192},{192,256},{256,320},{320,384},{384,448},... | collective-permute-start | bytes 196616 | tf_op jit(solution)/shard_map/ppermute | solution.py:19
  84.1 5.0 %collective-permute-start.13 = (f32[32,4,1,128]{3,2,1,0:T(1,128)S(1)}, f32[32,4,1,128]{3,2,1,0:T(1,128)S(1)}, u32[]{:S(2)}, u32[]{:S(2)}) collective-permute-start(f32[32,4,1,128]{3,2,1,0:T(1,128)S(1)} %get-tuple-element.73), channel_id=1, source_target_pairs={{64,0},{128,64},{192,128},{256,192},{320,256},{384,320},{448,384},... | collective-permute-start | bytes 196616 | tf_op jit(solution)/shard_map/ppermute | solution.py:22
  89.5 14.7 %collective-permute-start.15 = (f32[32,4,6,1]{3,2,1,0:T(8,128)S(1)}, f32[32,4,6,1]{3,2,1,0:T(8,128)S(1)}, u32[]{:S(2)}, u32[]{:S(2)}) collective-permute-start(f32[32,4,6,1]{3,2,1,0:T(8,128)S(1)} %get-tuple-element.64), channel_id=1, source_target_pairs={{16,0},{32,16},{48,32},{17,1},{33,17},{49,33},{18,2},{34,18},{50,3... | collective-permute-start | bytes 9224 | tf_op jit(solution)/shard_map/ppermute | solution.py:22
  90.8 14.3 %collective-permute-start.14 = (f32[32,4,6,1]{3,2,1,0:T(8,128)S(1)}, f32[32,4,6,1]{3,2,1,0:T(8,128)S(1)}, u32[]{:S(2)}, u32[]{:S(2)}) collective-permute-start(f32[32,4,6,1]{3,2,1,0:T(8,128)S(1)} %get-tuple-element.65), channel_id=1, source_target_pairs={{0,16},{16,32},{32,48},{1,17},{17,33},{33,49},{2,18},{18,34},{34,5... | collective-permute-start | bytes 9224 | tf_op jit(solution)/shard_map/ppermute | solution.py:19
  105.6 9.2 %collective-permute-start.16 = (f32[32,1,6,130]{3,2,1,0:T(8,128)S(1)}, f32[32,1,6,130]{3,2,1,0:T(8,128)S(1)}, u32[]{:S(2)}, u32[]{:S(2)}) collective-permute-start(f32[32,1,6,130]{3,2,1,0:T(8,128)S(1)} %get-tuple-element.56), channel_id=1, source_target_pairs={{1,0},{2,1},{3,2},{4,3},{5,4},{6,5},{7,6},{8,7},{9,8},{10,9},{11,1... | collective-permute-start | bytes 299528 | tf_op jit(solution)/shard_map/ppermute | solution.py:22
  110.1 5.9 %collective-permute-start.17 = (f32[32,1,6,130]{3,2,1,0:T(8,128)S(1)}, f32[32,1,6,130]{3,2,1,0:T(8,128)S(1)}, u32[]{:S(2)}, u32[]{:S(2)}) collective-permute-start(f32[32,1,6,130]{3,2,1,0:T(8,128)S(1)} %get-tuple-element.57), channel_id=1, source_target_pairs={{0,1},{1,2},{2,3},{3,4},{4,5},{5,6},{6,7},{7,8},{8,9},{9,10},{10,1... | collective-permute-start | bytes 299528 | tf_op jit(solution)/shard_map/ppermute | solution.py:19
  117.5 6.6 %collective-permute-start.18 = (f32[32,4,1,128]{3,2,1,0:T(1,128)S(1)}, f32[32,4,1,128]{3,2,1,0:T(1,128)S(1)}, u32[]{:S(2)}, u32[]{:S(2)}) collective-permute-start(f32[32,4,1,128]{3,2,1,0:T(1,128)S(1)} %get-tuple-element.70), channel_id=1, source_target_pairs={{0,64},{64,128},{128,192},{192,256},{256,320},{320,384},{384,448},... | collective-permute-start | bytes 196616 | tf_op jit(solution)/shard_map/ppermute | solution.py:19
  122.3 6.5 %collective-permute-start.19 = (f32[32,4,1,128]{3,2,1,0:T(1,128)S(1)}, f32[32,4,1,128]{3,2,1,0:T(1,128)S(1)}, u32[]{:S(2)}, u32[]{:S(2)}) collective-permute-start(f32[32,4,1,128]{3,2,1,0:T(1,128)S(1)} %get-tuple-element.71), channel_id=1, source_target_pairs={{64,0},{128,64},{192,128},{256,192},{320,256},{384,320},{448,384},... | collective-permute-start | bytes 196616 | tf_op jit(solution)/shard_map/ppermute | solution.py:22
  129.2 14.2 %collective-permute-start.21 = (f32[32,4,6,1]{3,2,1,0:T(8,128)S(1)}, f32[32,4,6,1]{3,2,1,0:T(8,128)S(1)}, u32[]{:S(2)}, u32[]{:S(2)}) collective-permute-start(f32[32,4,6,1]{3,2,1,0:T(8,128)S(1)} %get-tuple-element.62), channel_id=1, source_target_pairs={{16,0},{32,16},{48,32},{17,1},{33,17},{49,33},{18,2},{34,18},{50,3... | collective-permute-start | bytes 9224 | tf_op jit(solution)/shard_map/ppermute | solution.py:22
  130.5 14.7 %collective-permute-start.20 = (f32[32,4,6,1]{3,2,1,0:T(8,128)S(1)}, f32[32,4,6,1]{3,2,1,0:T(8,128)S(1)}, u32[]{:S(2)}, u32[]{:S(2)}) collective-permute-start(f32[32,4,6,1]{3,2,1,0:T(8,128)S(1)} %get-tuple-element.63), channel_id=1, source_target_pairs={{0,16},{16,32},{32,48},{1,17},{17,33},{33,49},{2,18},{18,34},{34,5... | collective-permute-start | bytes 9224 | tf_op jit(solution)/shard_map/ppermute | solution.py:19
  145.8 9.3 %collective-permute-start.22 = (f32[32,1,6,130]{3,2,1,0:T(8,128)S(1)}, f32[32,1,6,130]{3,2,1,0:T(8,128)S(1)}, u32[]{:S(2)}, u32[]{:S(2)}) collective-permute-start(f32[32,1,6,130]{3,2,1,0:T(8,128)S(1)} %get-tuple-element.54), channel_id=1, source_target_pairs={{1,0},{2,1},{3,2},{4,3},{5,4},{6,5},{7,6},{8,7},{9,8},{10,9},{11,1... | collective-permute-start | bytes 299528 | tf_op jit(solution)/shard_map/ppermute | solution.py:22
  147.7 8.6 %collective-permute-start.23 = (f32[32,1,6,130]{3,2,1,0:T(8,128)S(1)}, f32[32,1,6,130]{3,2,1,0:T(8,128)S(1)}, u32[]{:S(2)}, u32[]{:S(2)}) collective-permute-start(f32[32,1,6,130]{3,2,1,0:T(8,128)S(1)} %get-tuple-element.55), channel_id=1, source_target_pairs={{0,1},{1,2},{2,3},{3,4},{4,5},{5,6},{6,7},{7,8},{8,9},{9,10},{10,1... | collective-permute-start | bytes 299528 | tf_op jit(solution)/shard_map/ppermute | solution.py:19
  157.8 6.3 %collective-permute-start.24 = (f32[32,4,1,128]{3,2,1,0:T(1,128)S(1)}, f32[32,4,1,128]{3,2,1,0:T(1,128)S(1)}, u32[]{:S(2)}, u32[]{:S(2)}) collective-permute-start(f32[32,4,1,128]{3,2,1,0:T(1,128)S(1)} %get-tuple-element.68), channel_id=1, source_target_pairs={{0,64},{64,128},{128,192},{192,256},{256,320},{320,384},{384,448},... | collective-permute-start | bytes 196616 | tf_op jit(solution)/shard_map/ppermute | solution.py:19
  162.4 5.0 %collective-permute-start.25 = (f32[32,4,1,128]{3,2,1,0:T(1,128)S(1)}, f32[32,4,1,128]{3,2,1,0:T(1,128)S(1)}, u32[]{:S(2)}, u32[]{:S(2)}) collective-permute-start(f32[32,4,1,128]{3,2,1,0:T(1,128)S(1)} %get-tuple-element.69), channel_id=1, source_target_pairs={{64,0},{128,64},{192,128},{256,192},{320,256},{384,320},{448,384},... | collective-permute-start | bytes 196616 | tf_op jit(solution)/shard_map/ppermute | solution.py:22
  167.8 13.0 %collective-permute-start.27 = (f32[32,4,6,1]{3,2,1,0:T(8,128)S(1)}, f32[32,4,6,1]{3,2,1,0:T(8,128)S(1)}, u32[]{:S(2)}, u32[]{:S(2)}) collective-permute-start(f32[32,4,6,1]{3,2,1,0:T(8,128)S(1)} %get-tuple-element.60), channel_id=1, source_target_pairs={{16,0},{32,16},{48,32},{17,1},{33,17},{49,33},{18,2},{34,18},{50,3... | collective-permute-start | bytes 9224 | tf_op jit(solution)/shard_map/ppermute | solution.py:22
  169.1 13.4 %collective-permute-start.26 = (f32[32,4,6,1]{3,2,1,0:T(8,128)S(1)}, f32[32,4,6,1]{3,2,1,0:T(8,128)S(1)}, u32[]{:S(2)}, u32[]{:S(2)}) collective-permute-start(f32[32,4,6,1]{3,2,1,0:T(8,128)S(1)} %get-tuple-element.61), channel_id=1, source_target_pairs={{0,16},{16,32},{32,48},{1,17},{17,33},{33,49},{2,18},{18,34},{34,5... | collective-permute-start | bytes 9224 | tf_op jit(solution)/shard_map/ppermute | solution.py:19
  183.1 13.3 %collective-permute-start.28 = (f32[32,1,6,130]{3,2,1,0:T(8,128)S(1)}, f32[32,1,6,130]{3,2,1,0:T(8,128)S(1)}, u32[]{:S(2)}, u32[]{:S(2)}) collective-permute-start(f32[32,1,6,130]{3,2,1,0:T(8,128)S(1)} %get-tuple-element.52), channel_id=1, source_target_pairs={{1,0},{2,1},{3,2},{4,3},{5,4},{6,5},{7,6},{8,7},{9,8},{10,9},{11,1... | collective-permute-start | bytes 299528 | tf_op jit(solution)/shard_map/ppermute | solution.py:22
  185.0 12.6 %collective-permute-start.29 = (f32[32,1,6,130]{3,2,1,0:T(8,128)S(1)}, f32[32,1,6,130]{3,2,1,0:T(8,128)S(1)}, u32[]{:S(2)}, u32[]{:S(2)}) collective-permute-start(f32[32,1,6,130]{3,2,1,0:T(8,128)S(1)} %get-tuple-element.53), channel_id=1, source_target_pairs={{0,1},{1,2},{2,3},{3,4},{4,5},{5,6},{6,7},{7,8},{8,9},{9,10},{10,1... | collective-permute-start | bytes 299528 | tf_op jit(solution)/shard_map/ppermute | solution.py:19
  200.3 13.3 %all-to-all-start = ((f32[16,4,128]{2,1,0:T(4,128)}), f32[16,4,128]{2,1,0:T(4,128)S(1)}, u32[]{:S(2)}, u32[]{:S(2)}) async-start(f32[16,4,128]{2,1,0:T(4,128)} %reshape.135), calls=%async_computation | async-start | bytes 65536 | tf_op jit(solution)/shard_map/all_to_all | solution.py:70
  214.3 34.6 %all-to-all-start.1 = ((f32[64,4,128]{2,1,0:T(4,128)}), f32[64,4,128]{2,1,0:T(4,128)S(1)}, u32[]{:S(2)}, u32[]{:S(2)}) async-start(f32[64,4,128]{2,1,0:T(4,128)} %broadcast_in_dim.8), calls=%async_computation.1 | async-start | bytes 262144 | tf_op jit(solution)/shard_map/all_to_all | solution.py:72
  249.6 14.2 %all-to-all-start.2 = ((f32[16,4,128]{2,1,0:T(4,128)}), f32[16,4,128]{2,1,0:T(4,128)S(1)}, u32[]{:S(2)}, u32[]{:S(2)}) async-start(f32[16,4,128]{2,1,0:T(4,128)} %broadcast_in_dim.9), calls=%async_computation.2 | async-start | bytes 65536 | tf_op jit(solution)/shard_map/all_to_all | solution.py:76
  (3 other events, 39.6 us)

commit v2 on v0

v2 whole, which is shorter than its diff:
```python
import functools

import jax
import jax.numpy as jnp
from jax import lax
from jax.experimental import pallas as pl
from jax.experimental.pallas import tpu as pltpu
from jax.sharding import PartitionSpec as P

S = 4
NREG = 8
R = 32
SIDE = 4
CELLS = SIDE * SIDE
LANES = 128
WIDE = SIDE + 2 * S
HALF = 16
EDGE_ROWS = R + 8
KEPT = sum(SIDE + 2 * (S - d) for d in range(1, S + 1))
PLANES = KEPT + 5


SIGMA = 8.0
THETA = 8.0

VMEM = pl.BlockSpec(memory_space=pltpu.VMEM)
SMEM = pl.BlockSpec(memory_space=pltpu.SMEM)


def call(kernel, name, outs, specs, scratch=()):
    return pl.pallas_call(
        kernel,
        name=name,
        out_shape=[jax.ShapeDtypeStruct(shape, jnp.float32) for shape in outs],
        in_specs=specs,
        out_specs=[VMEM] * len(outs),
        scratch_shapes=list(scratch),
        compiler_params=pltpu.CompilerParams(vmem_limit_bytes=40 * 1024 * 1024),
    )


def lane_index(shape):
    return lax.broadcasted_iota(jnp.int32, shape, len(shape) - 1)


def rhs_kernel(index_ref, gain_ref, source_ref, label_ref, block_ref, edge_ref, row_ref):
    for j in range(R):
        row_ref[pl.ds(j, 1), :] = gain_ref[pl.ds(index_ref[j], 1), :]
    rows = row_ref[...]
    columns = [jnp.broadcast_to(rows[:, k : k + 1], (R, LANES)) for k in range(NREG)]
    group = lane_index((R, LANES)) // (2 * S)
    group_row = lane_index((8, LANES)) // (2 * S)
    edge = jnp.zeros((R, LANES), jnp.float32)
    edge_label = jnp.zeros((8, LANES), jnp.float32)
    labels = label_ref[...].astype(jnp.float32)
    for cell in range(CELLS):
        label = jnp.broadcast_to(labels[cell : cell + 1, :], (R, LANES))
        gain = jnp.zeros((R, LANES), jnp.float32)
        for k in range(NREG):
            gain = jnp.where(label == k + 1.0, columns[k], gain)
        rhs = source_ref[pl.ds(cell, R, stride=CELLS), :] * gain
        block_ref[cell] = rhs
        turn = (cell * 2 * S + S) % LANES
        edge = jnp.where(group == cell, pltpu.roll(rhs, turn, 1), edge)
        edge_label = jnp.where(
            group_row == cell, pltpu.roll(label[:8], turn, 1), edge_label
        )
    block_ref[CELLS, 0:CELLS, :] = labels
    block_ref[CELLS, CELLS:R, :] = jnp.zeros((R - CELLS, LANES), jnp.float32)
    edge_ref[0:R, :] = edge
    edge_ref[R:EDGE_ROWS, :] = edge_label


def kept_cells(order):
    return [
        (row, x)
        for d, row in zip(range(1, S + 1), order)
        for x in range(-(S - d), SIDE + S - d)
    ]


def merge_kernel(own_ref, low_ref, high_ref, e0, e1, e2, e3, e4, e5, down_ref, up_ref):
    blocks = (low_ref, own_ref, high_ref)
    for out_ref, order in ((down_ref, (0, 1, 2, 3)), (up_ref, (3, 2, 1, 0))):
        for slot, (row, x) in enumerate(kept_cells(order)):
            out_ref[slot] = blocks[(x + SIDE) // SIDE][row * SIDE + x % SIDE]
    left = lane_index((EDGE_ROWS, LANES)) % (2 * S) < S
    for g, (before, after) in enumerate(((e0, e1), (e2, e3), (e4, e5))):
        edge = jnp.where(left, before[...], after[...])
        labels = blocks[g][CELLS, 0:CELLS, :]
        for out_ref in (down_ref, up_ref):
            out_ref[KEPT + g] = edge[:R]
            if g < 2:
                out_ref[KEPT + 3, g * CELLS : (g + 1) * CELLS, :] = labels
            else:
                out_ref[KEPT + 4, 0:CELLS, :] = labels
            out_ref[KEPT + 4, CELLS + g : CELLS + g + 1, :] = edge[R : R + 1]
    for out_ref in (down_ref, up_ref):
        out_ref[KEPT + 4, CELLS + 3 : R, :] = jnp.zeros((R - CELLS - 3, LANES), jnp.float32)


def coefficients(table_ref, label_ref, cond_ref, coef_ref):
    def conduct(z, carry):
        label = label_ref[z]
        fields = [jnp.zeros((2 * HALF, LANES), jnp.float32) for _ in range(4)]
        for region in range(NREG):
            hit = label == region + 1.0
            fields = [
                jnp.where(hit, table_ref[region, column], fields[column]) for column in range(4)
            ]
        for column in range(4):
            cond_ref[column, z] = fields[column]
        return carry

    lax.fori_loop(0, WIDE, conduct, 0)
    lane = lane_index((2 * HALF, LANES))

    def faces(z, carry):
        inside = label_ref[z] > 0.5
        along_z, along_x, along_y, shunt = (cond_ref[column, z] for column in range(4))
        after = pltpu.roll(along_y, LANES - 1, 1)
        before = pltpu.roll(along_y, 1, 1)
        after = jnp.where(lane == LANES - 1, pltpu.roll(after, HALF, 0), after)
        before = jnp.where(lane == 0, pltpu.roll(before, HALF, 0), before)
        found = [
            0.5 * (along_z + cond_ref[0, z + 1]),
            0.5 * (along_z + cond_ref[0, z - 1]),
            0.5 * (along_x + pltpu.roll(along_x, 2 * HALF - 1, 0)),
            0.5 * (along_x + pltpu.roll(along_x, 1, 0)),
            0.5 * (along_y + after),
            0.5 * (along_y + before),
        ]
        diag = shunt
        for face in found:
            diag = diag + face
        found.append(diag - SIGMA)
        for k, value in enumerate(found):
            coef_ref[k, z] = jnp.where(inside, value * (1.0 / THETA), 0.0)
        return carry

    lax.fori_loop(1, WIDE - 1, faces, 0)


def power_row(source_ref, target_ref, coef_ref, z, xs):
    lane = lane_index((R, LANES))
    first, last = lane == 0, lane == LANES - 1
    for x in xs:
        center = [source_ref[z, x, t] for t in range(2)]
        down = [pltpu.roll(value, 1, 1) for value in center]
        up = [pltpu.roll(value, LANES - 1, 1) for value in center]
        for t in range(2):
            row = t * HALF + x

            def weight(k):
                return jnp.broadcast_to(coef_ref[k, z, row : row + 1, :], (R, LANES))

            after = jnp.where(last, up[1 - t], up[t])
            before = jnp.where(first, down[1 - t], down[t])
            beside = weight(0) * source_ref[z + 1, x, t] + weight(1) * source_ref[z - 1, x, t]
            beside = beside + weight(2) * source_ref[z, x + 1, t]
            beside = beside + weight(3) * source_ref[z, x - 1, t]
            beside = beside + weight(4) * after + weight(5) * before
            target_ref[z, x, t] = weight(6) * center[t] - beside


def power_kernel(
    table_ref,
    own_ref,
    low_ref,
    high_ref,
    mid_ref,
    below_ref,
    above_ref,
    basis_ref,
    moment_ref,
    label_ref,
    cond_ref,
    coef_ref,
    even_ref,
    odd_ref,
):
    blocks = (low_ref, own_ref, high_ref)
    label_ref[...] = jnp.zeros(label_ref.shape, jnp.float32)
    sides = ((0, below_ref), (S, mid_ref), (S + SIDE, above_ref))
    for base, ref in sides:
        for g in range(3):
            for row in range(SIDE):
                labels = (
                    ref[KEPT + 3, g * CELLS + row * SIDE : g * CELLS + (row + 1) * SIDE, :]
                    if g < 2
                    else ref[KEPT + 4, row * SIDE : (row + 1) * SIDE, :]
                )
                label_ref[base + row, g * SIDE : (g + 1) * SIDE, :] = labels
                edge = ref[KEPT + 4, CELLS + g : CELLS + g + 1, :]
                for x in range(SIDE):
                    turn = -((row * SIDE + x) * 2 * S + S) % LANES
                    at = HALF + g * SIDE + x
                    label_ref[base + row, at : at + 1, :] = pltpu.roll(edge, turn, 1)
    coefficients(table_ref, label_ref, cond_ref, coef_ref)

    for row in range(SIDE):
        for x in range(-S, SIDE + S):
            even_ref[S + row, S + x, 0] = blocks[(x + SIDE) // SIDE][row * SIDE + x % SIDE]
    for slot, (row, x) in enumerate(kept_cells((3, 2, 1, 0))):
        even_ref[row, S + x, 0] = below_ref[slot]
    for slot, (row, x) in enumerate(kept_cells((0, 1, 2, 3))):
        even_ref[S + SIDE + row, S + x, 0] = above_ref[slot]
    for base, ref in sides:
        for g in range(3):
            edge = ref[KEPT + g]
            for row in range(SIDE):
                for x in range(SIDE):
                    turn = -((row * SIDE + x) * 2 * S + S) % LANES
                    even_ref[base + row, g * SIDE + x, 1] = pltpu.roll(edge, turn, 1)

    refs = (even_ref, odd_ref)
    flats = []
    for k in range(S + 1):
        now = refs[k % 2]
        cells = []
        for row in range(SIDE):
            for x in range(SIDE):
                value = now[S + row, S + x, 0]
                basis_ref[k, row * SIDE + x] = value
                cells.append(value)
        if k < S:
            later = refs[1 - k % 2]

            def one(z, carry):
                power_row(now, later, coef_ref, z, range(k + 1, WIDE - 1 - k))
                return carry

            lax.fori_loop(k + 1, WIDE - 1 - k, one, 0)
    for k in range(S):
        this = jnp.concatenate([basis_ref[k, cell] for cell in range(CELLS)], 1)
        after = jnp.concatenate([basis_ref[k + 1, cell] for cell in range(CELLS)], 1)
        pair = lax.dot_general(
            this,
            jnp.concatenate([this, after], 0),
            (((1,), (1,)), ((), ())),
            precision=lax.Precision.HIGHEST,
            preferred_element_type=jnp.float32,
        )
        half, at = divmod(2 * k * R, LANES)
        moment_ref[half * R : (half + 1) * R, at : at + 2 * R] = pair


def eliminate(mat, right):
    tiles = [mat[8 * i : 8 * i + 8] for i in range(16)]
    sides = [right[8 * i : 8 * i + 8] for i in range(16)]
    sub = lax.broadcasted_iota(jnp.int32, (8, LANES), 0)
    for k in range(S * R):
        p, s = divmod(k, 8)
        row = jnp.broadcast_to(tiles[p][s : s + 1, :], (8, LANES))
        side = jnp.broadcast_to(sides[p][s : s + 1, :], (8, LANES))
        inverse = 1.0 / jnp.broadcast_to(row[:, k : k + 1], (8, LANES))
        row, side = row * inverse, side * inverse
        for i in range(16):
            column = jnp.broadcast_to(tiles[i][:, k : k + 1], (8, LANES))
            tile, rest = tiles[i] - column * row, sides[i] - column * side
            if i == p:
                tile, rest = jnp.where(sub == s, row, tile), jnp.where(sub == s, side, rest)
            tiles[i], sides[i] = tile, rest
    return jnp.concatenate(sides, 0)


def solve_kernel(moment_ref, basis_ref, solution_ref, residual_ref):
    low, high = moment_ref[0:R, :], moment_ref[R : 2 * R, :]
    lane = lane_index((R, LANES))

    def window(first, second, shift):
        if shift == 0:
            return first
        keep = lane < LANES - shift
        turn = LANES - shift
        return jnp.where(keep, pltpu.roll(first, turn, 1), pltpu.roll(second, turn, 1))

    first = THETA * window(low, high, R) + SIGMA * low
    second = THETA * window(high, high, R) + SIGMA * high
    mat = jnp.concatenate([window(first, second, i * R) for i in range(S)], 0)
    mat = 0.5 * (mat + mat.T)
    right = jnp.concatenate([window(low, high, i * R) for i in range(S)], 0)
    coef = eliminate(mat, right)
    zero = jnp.zeros((R, LANES), jnp.float32)
    here = jnp.concatenate([coef, zero], 0)
    there = jnp.concatenate([zero, coef], 0)
    combo = SIGMA * here + THETA * there
    wide = lane_index(here.shape)
    weights = jnp.where(
        wide < R, here, jnp.where(wide < 2 * R, pltpu.roll(combo, R, 1), 0.0)
    )
    weights = jnp.concatenate([weights, jnp.zeros((96, LANES), jnp.float32)], 0)
    weights = weights.T[: 2 * R, : (S + 1) * R]
    for cell in range(CELLS):
        block = jnp.concatenate([basis_ref[k, cell] for k in range(S + 1)], 0)
        taken = lax.dot_general(
            weights,
            block,
            (((1,), (0,)), ((), ())),
            precision=lax.Precision.HIGHEST,
            preferred_element_type=jnp.float32,
        )
        solution_ref[pl.ds(cell, R, stride=CELLS), :] = taken[:R]
        residual_ref[pl.ds(cell, R, stride=CELLS), :] = basis_ref[0, cell] - taken[R:]


def neighbour(value, axes, offsets):
    sizes = [lax.axis_size(axis) for axis in axes]
    pairs = []
    for at in range(sizes[0] * (sizes[1] if len(sizes) > 1 else 1)):
        place = divmod(at, sizes[1]) if len(sizes) > 1 else (at,)
        to = [p + o for p, o in zip(place, offsets)]
        if all(0 <= t < n for t, n in zip(to, sizes)):
            pairs.append((at, to[0] if len(to) == 1 else to[0] * sizes[1] + to[1]))
    return lax.ppermute(value, axes if len(axes) > 1 else axes[0], pairs)


def total(values):
    parts = lax.axis_size("gz")
    others = lax.axis_size("gx") * lax.axis_size("gy")
    pieces = lax.all_to_all(values.reshape(parts, -1, LANES), "gz", 0, 0)
    piece = pieces.sum(0)
    pieces = lax.all_to_all(
        jnp.broadcast_to(piece, (others,) + piece.shape), ("gx", "gy"), 0, 0
    )
    piece = pieces.sum(0)
    pieces = lax.all_to_all(jnp.broadcast_to(piece, (parts,) + piece.shape), "gz", 0, 0)
    return pieces.reshape(values.shape)


def body(sources, labels, region_table, sweep_index, sweep_gain):
    block, edge = call(
        rhs_kernel,
        "rhs",
        [(CELLS + 1, R, LANES), (EDGE_ROWS, LANES)],
        [SMEM, VMEM, VMEM, VMEM],
        [pltpu.VMEM((R, NREG), jnp.float32)],
    )(sweep_index, sweep_gain, sources.reshape(R * CELLS, LANES), labels.reshape(CELLS, LANES))
    low = neighbour(block, ("gx",), (1,))
    high = neighbour(block, ("gx",), (-1,))
    edges = [
        neighbour(edge, ("gx", "gy"), (dx, dy)) for dx in (1, 0, -1) for dy in (1, -1)
    ]
    down, up = call(
        merge_kernel, "merge", [(PLANES, R, LANES)] * 2, [VMEM] * 9
    )(block, low, high, *edges)
    below = neighbour(up, ("gz",), (1,))
    above = neighbour(down, ("gz",), (-1,))
    basis, moments = call(
        power_kernel,
        "powers",
        [(S + 1, CELLS, R, LANES), (2 * R, LANES)],
        [SMEM] + [VMEM] * 6,
        [
            pltpu.VMEM((WIDE, 2 * HALF, LANES), jnp.float32),
            pltpu.VMEM((4, WIDE, 2 * HALF, LANES), jnp.float32),
            pltpu.VMEM((7, WIDE, 2 * HALF, LANES), jnp.float32),
            pltpu.VMEM((WIDE, WIDE, 2, R, LANES), jnp.float32),
            pltpu.VMEM((WIDE, WIDE, 2, R, LANES), jnp.float32),
        ],
    )(region_table, block, low, high, down, below, above)
    solution, residual = call(
        solve_kernel, "solve", [(R * CELLS, LANES)] * 2, [VMEM] * 2
    )(total(moments), basis)
    return (solution.reshape(sources.shape), residual.reshape(sources.shape))


def solution(mesh):
    placed = (P(None, "gz", "gx", "gy"), P("gz", "gx", "gy"), P(), P(), P())
    return jax.shard_map(
        body,
        mesh=mesh,
        in_specs=placed,
        out_specs=(P(None, "gz", "gx", "gy"), P(None, "gz", "gx", "gy")),
        check_vma=False,
    )
```

time: 724 us -> 147 us (0.20)
  waiting for transfers between devices: 531 us -> 4.5 us
  blocking collectives: 0 us -> 64.4 us
  starting transfers between devices: 102 us -> 40.3 us
  other arithmetic: 58.9 us -> 0.1 us
  Pallas kernels: 0 us -> 31.1 us
  between operations: 14.8 us -> 0.77 us
    psum x1 -> x0, waiting for transfers between devices: 473 us -> none  [body(): gram = lax.psum(partial_gram, ('gx', 'gy', 'gz'))]
    all_to_all x0 -> x3, blocking collectives: none -> 64.4 us  [the longest x1 38.2 us: total(): lax.all_to_all(jnp.broadcast_to(piece, (others,) + piece.shape), ('gx', '...]
    ppermute x30 -> x10, starting transfers between devices: 102 us -> 40.3 us  [neighbour(): return lax.ppermute(value, axes if len(axes) > 1 else axes[0], pairs)]
    ppermute x30 -> x10, waiting for transfers between devices: 58.5 us -> 4.5 us  [neighbour(): return lax.ppermute(value, axes if len(axes) > 1 else axes[0], pairs)]
    pallas_call x0 -> x4, Pallas kernels: none -> 31.1 us  [the longest x1 19.9 us: body(): call(solve_kernel, 'solve', [(R * CELLS, LANES)] * 2, [VMEM] * 2)]
    another operation x5 -> x0, other arithmetic: 22.9 us -> none  [the longest x3 12.4 us: body(): factor = jnp.linalg.cholesky(mat)]
    add x7 -> x0, other arithmetic: 17.5 us -> none  [the longest x4 16.5 us: region_fields(): fields[column] + hit * region_table[region, column]]
    div x5 -> x0, other arithmetic: 8.38 us -> none  [the longest x4 8.37 us: next_power(): return (image - SIGMA * center) / THETA]
  transfers between devices with their start and end apart: 31 -> 10, of which waited for: 20 -> 3; matrix products, arithmetic and copies ran while one was open for 4% -> 1% of each run, Pallas kernels for 0% -> 0%
where the time goes in v2:
time: 147 us
  blocking collectives  64.4 us (44%)
  starting transfers between devices  40.3 us (27%)
  Pallas kernels  31.1 us (21%)
  local copies, waits for them, and re-layouts  5.69 us (4%)
  waiting for transfers between devices  4.5 us (3%)
    ppermute x10, starting transfers between devices, neighbour(): return lax.ppermute(value, axes if len(axes) > 1 else axes[0], pairs)  40.3 us
    all_to_all x1, blocking collectives, total(): lax.all_to_all(jnp.broadcast_to(piece, (others,) + piece.shape), ('gx', '...  38.2 us
    pallas_call x1, Pallas kernels, body(): call(solve_kernel, 'solve', [(R * CELLS, LANES)] * 2, [VMEM] * 2)  19.9 us
    all_to_all x1, blocking collectives, total(): lax.all_to_all(jnp.broadcast_to(piece, (parts,) + piece.shape), 'gz', 0, 0)  13.3 us
    all_to_all x1, blocking collectives, total(): pieces = lax.all_to_all(values.reshape(parts, -1, LANES), 'gz', 0, 0)  13 us
    pallas_call x1, Pallas kernels, body(): call(power_kernel, 'powers', [(S + 1, CELLS, R, LANES), (2 * R, LANES)],...  10.3 us
    unnamed x12, local copies, waits for them, and re-layouts  5.66 us
    ppermute x10, waiting for transfers between devices, neighbour(): return lax.ppermute(value, axes if len(axes) > 1 else axes[0], pairs)  4.5 us
  transfers between devices with their start and end apart: 10, of which 3 were waited for; matrix products, arithmetic and copies ran while one was open for 1% of the time, Pallas kernels for 0%

profile of v2, /device:TPU:1, one launch (start us, length us, event | category | flops | bytes accessed | tf_op | source)
XLA Modules:
  0.0 146.8 jit_solution(16738438971482959021)
XLA Ops:
  0.6 0.8 copy.11.gain_ref
  1.4 0.9 copy-done.2
  2.3 0.7 copy-done.3
  3.0 0.7 copy-done.4
  3.7 0.9 rhs.1
  4.6 1.3 collective-permute-start.1
  5.9 5.5 %collective-permute-start = (f32[17,32,128]{2,1,0:T(8,128)S(1)}, f32[17,32,128]{2,1,0:T(8,128)S(1)}, u32[]{:S(2)}, u32[]{:S(2)}) collective-permute-start(f32[17,32,128]{2,1,0:T(8,128)S(1)} %get-tuple-element.10.own_ref), channel_id=1, source_target_pairs={{0,64},{64,128},{128,192},{192,256},{256,320},{320,384},{384,448},... | collective-permute-start | bytes 835592 | tf_op jit(solution)/shard_map/ppermute | solution.py:315
  11.3 1.3 collective-permute-start.7
  12.6 0.7 collective-permute-start.6
  13.3 1.3 collective-permute-start.5
  14.6 2.8 %collective-permute-done.7.e5 = f32[40,128]{1,0:T(8,128)S(1)} collective-permute-done((f32[40,128]{1,0:T(8,128)S(1)}, f32[40,128]{1,0:T(8,128)S(1)}, u32[]{:S(2)}, u32[]{:S(2)}) %collective-permute-start.7) | collective-permute-done | bytes 20512 | tf_op jit(solution)/shard_map/ppermute | solution.py:315
  17.4 3.1 %collective-permute-start.4 = (f32[40,128]{1,0:T(8,128)S(1)}, f32[40,128]{1,0:T(8,128)S(1)}, u32[]{:S(2)}, u32[]{:S(2)}) collective-permute-start(f32[40,128]{1,0:T(8,128)S(1)} %get-tuple-element.11), channel_id=1, source_target_pairs={{0,16},{16,32},{32,48},{64,80},{80,96},{96,112},{128,144},{144,160... | collective-permute-start | bytes 61448 | tf_op jit(solution)/shard_map/ppermute | solution.py:315
  20.6 0.7 collective-permute-start.3
  21.2 0.0 collective-permute-done.5.e3
  21.3 9.4 %collective-permute-start.2 = (f32[40,128]{1,0:T(8,128)S(1)}, f32[40,128]{1,0:T(8,128)S(1)}, u32[]{:S(2)}, u32[]{:S(2)}) collective-permute-start(f32[40,128]{1,0:T(8,128)S(1)} %get-tuple-element.11), channel_id=1, source_target_pairs={{0,80},{16,96},{32,112},{64,144},{80,160},{96,176},{128,208},{144,... | collective-permute-start | bytes 61448 | tf_op jit(solution)/shard_map/ppermute | solution.py:315
  30.7 0.0 collective-permute-done.4.e2
  30.7 0.0 collective-permute-done.3.e1
  30.7 0.9 collective-permute-done.2.e0
  31.6 0.0 collective-permute-done.1.high_ref
  31.6 0.1 merge.1
  31.6 6.3 %collective-permute-start.8 = (f32[33,32,128]{2,1,0:T(8,128)S(1)}, f32[33,32,128]{2,1,0:T(8,128)S(1)}, u32[]{:S(2)}, u32[]{:S(2)}) collective-permute-start(f32[33,32,128]{2,1,0:T(8,128)S(1)} %get-tuple-element.13), channel_id=1, source_target_pairs={{0,1},{1,2},{2,3},{3,4},{4,5},{5,6},{6,7},{7,8},{8,9},{9,10},{10,1... | collective-permute-start | bytes 1622024 | tf_op jit(solution)/shard_map/ppermute | solution.py:315
  38.0 10.8 %collective-permute-start.9 = (f32[33,32,128]{2,1,0:T(8,128)S(1)}, f32[33,32,128]{2,1,0:T(8,128)S(1)}, u32[]{:S(2)}, u32[]{:S(2)}) collective-permute-start(f32[33,32,128]{2,1,0:T(8,128)S(1)} %get-tuple-element.12.mid_ref), channel_id=1, source_target_pairs={{1,0},{2,1},{3,2},{4,3},{5,4},{6,5},{7,6},{8,7},{9,8},{10,9},{11,1... | collective-permute-start | bytes 1622024 | tf_op jit(solution)/shard_map/ppermute | solution.py:315
  48.8 0.8 copy.12.table_ref
  49.5 0.8 collective-permute-done.9.above_ref
  50.3 0.8 copy-done
  51.1 1.0 copy-done.1
  52.2 10.3 %powers.1 = (f32[5,16,32,128]{3,2,1,0:T(8,128)S(1)}, f32[64,128]{1,0:T(8,128)S(1)}) custom-call(f32[8,4]{1,0:T(8,128)S(1)} %copy.12.table_ref, f32[17,32,128]{2,1,0:T(8,128)S(1)} %get-tuple-element.10.own_ref, f32[17,32,128]{2,1,0:T(8,128)S(1)} %collective-permute-done.low_ref, f32[17,32,128]{2,1,0:T(8,128)S(1)} %collective-permute-done.1.high_ref, ...), custom_call_target="tpu_custom_call" | custom-call | tf_op jit(solution)/shard_map/powers/pallas_call | solution.py:349
  62.4 13.0 %all_to_all.15 = f32[16,4,128]{2,1,0:T(4,128)S(1)} all-to-all(f32[16,4,128]{2,1,0:T(4,128)S(1)} %bitcast.8), channel_id=1, replica_groups=mesh['gx'=16,'gy'=4,'gz'=16] {'gz'}, dimensions={0} | all-to-all | bytes 65536 | tf_op jit(solution)/shard_map/all_to_all | solution.py:321
  75.4 38.2 %all_to_all.16 = f32[64,4,128]{2,1,0:T(4,128)S(1)} all-to-all(f32[64,4,128]{2,1,0:T(4,128)S(1)} %broadcast_in_dim.6), channel_id=1, replica_groups=mesh['gx'=16,'gy'=4,'gz'=16] {'gx','gy'}, dimensions={0} | all-to-all | bytes 262144 | tf_op jit(solution)/shard_map/all_to_all | solution.py:323
  113.6 0.1 reduce_sum.19
  113.7 13.3 %all_to_all.17 = f32[16,4,128]{2,1,0:T(4,128)S(1)} all-to-all(f32[16,4,128]{2,1,0:T(4,128)S(1)} %broadcast_in_dim.7), channel_id=1, replica_groups=mesh['gx'=16,'gy'=4,'gz'=16] {'gz'}, dimensions={0} | all-to-all | bytes 65536 | tf_op jit(solution)/shard_map/all_to_all | solution.py:327
  127.0 19.9 %solve.1 = (f32[512,128]{1,0:T(8,128)}, f32[512,128]{1,0:T(8,128)}) custom-call(f32[64,128]{1,0:T(8,128)S(1)} %bitcast.7, f32[5,16,32,128]{3,2,1,0:T(8,128)S(1)} %get-tuple-element.15.basis_ref), custom_call_target="tpu_custom_call" | custom-call | tf_op jit(solution)/shard_map/solve/pallas_call | solution.py:362
  (11 shorter events, 0.1 us)
Async XLA Ops:
  1.4 0.9 copy-start.2
  2.3 0.7 copy-start.3
  3.0 0.7 copy-start.4
  4.6 27.0 %collective-permute-start.1 = (f32[17,32,128]{2,1,0:T(8,128)S(1)}, f32[17,32,128]{2,1,0:T(8,128)S(1)}, u32[]{:S(2)}, u32[]{:S(2)}) collective-permute-start(f32[17,32,128]{2,1,0:T(8,128)S(1)} %get-tuple-element.10.own_ref), channel_id=1, source_target_pairs={{64,0},{128,64},{192,128},{256,192},{320,256},{384,320},{448,384},... | collective-permute-start | bytes 835592 | tf_op jit(solution)/shard_map/ppermute | solution.py:315
  5.9 25.7 %collective-permute-start = (f32[17,32,128]{2,1,0:T(8,128)S(1)}, f32[17,32,128]{2,1,0:T(8,128)S(1)}, u32[]{:S(2)}, u32[]{:S(2)}) collective-permute-start(f32[17,32,128]{2,1,0:T(8,128)S(1)} %get-tuple-element.10.own_ref), channel_id=1, source_target_pairs={{0,64},{64,128},{128,192},{192,256},{256,320},{320,384},{384,448},... | collective-permute-start | bytes 835592 | tf_op jit(solution)/shard_map/ppermute | solution.py:315
  11.3 6.1 %collective-permute-start.7 = (f32[40,128]{1,0:T(8,128)S(1)}, f32[40,128]{1,0:T(8,128)S(1)}, u32[]{:S(2)}, u32[]{:S(2)}) collective-permute-start(f32[40,128]{1,0:T(8,128)S(1)} %get-tuple-element.11), channel_id=1, source_target_pairs={{80,0},{96,16},{112,32},{144,64},{160,80},{176,96},{208,128},{224,... | collective-permute-start | bytes 61448 | tf_op jit(solution)/shard_map/ppermute | solution.py:315
  12.6 7.9 %collective-permute-start.6 = (f32[40,128]{1,0:T(8,128)S(1)}, f32[40,128]{1,0:T(8,128)S(1)}, u32[]{:S(2)}, u32[]{:S(2)}) collective-permute-start(f32[40,128]{1,0:T(8,128)S(1)} %get-tuple-element.11), channel_id=1, source_target_pairs={{64,16},{80,32},{96,48},{128,80},{144,96},{160,112},{192,144},{208... | collective-permute-start | bytes 61448 | tf_op jit(solution)/shard_map/ppermute | solution.py:315
  13.3 7.9 %collective-permute-start.5 = (f32[40,128]{1,0:T(8,128)S(1)}, f32[40,128]{1,0:T(8,128)S(1)}, u32[]{:S(2)}, u32[]{:S(2)}) collective-permute-start(f32[40,128]{1,0:T(8,128)S(1)} %get-tuple-element.11), channel_id=1, source_target_pairs={{16,0},{32,16},{48,32},{80,64},{96,80},{112,96},{144,128},{160,144... | collective-permute-start | bytes 61448 | tf_op jit(solution)/shard_map/ppermute | solution.py:315
  17.4 13.2 %collective-permute-start.4 = (f32[40,128]{1,0:T(8,128)S(1)}, f32[40,128]{1,0:T(8,128)S(1)}, u32[]{:S(2)}, u32[]{:S(2)}) collective-permute-start(f32[40,128]{1,0:T(8,128)S(1)} %get-tuple-element.11), channel_id=1, source_target_pairs={{0,16},{16,32},{32,48},{64,80},{80,96},{96,112},{128,144},{144,160... | collective-permute-start | bytes 61448 | tf_op jit(solution)/shard_map/ppermute | solution.py:315
  20.6 10.1 %collective-permute-start.3 = (f32[40,128]{1,0:T(8,128)S(1)}, f32[40,128]{1,0:T(8,128)S(1)}, u32[]{:S(2)}, u32[]{:S(2)}) collective-permute-start(f32[40,128]{1,0:T(8,128)S(1)} %get-tuple-element.11), channel_id=1, source_target_pairs={{16,64},{32,80},{48,96},{80,128},{96,144},{112,160},{144,192},{160... | collective-permute-start | bytes 61448 | tf_op jit(solution)/shard_map/ppermute | solution.py:315
  21.3 10.3 %collective-permute-start.2 = (f32[40,128]{1,0:T(8,128)S(1)}, f32[40,128]{1,0:T(8,128)S(1)}, u32[]{:S(2)}, u32[]{:S(2)}) collective-permute-start(f32[40,128]{1,0:T(8,128)S(1)} %get-tuple-element.11), channel_id=1, source_target_pairs={{0,80},{16,96},{32,112},{64,144},{80,160},{96,176},{128,208},{144,... | collective-permute-start | bytes 61448 | tf_op jit(solution)/shard_map/ppermute | solution.py:315
  31.6 17.9 %collective-permute-start.8 = (f32[33,32,128]{2,1,0:T(8,128)S(1)}, f32[33,32,128]{2,1,0:T(8,128)S(1)}, u32[]{:S(2)}, u32[]{:S(2)}) collective-permute-start(f32[33,32,128]{2,1,0:T(8,128)S(1)} %get-tuple-element.13), channel_id=1, source_target_pairs={{0,1},{1,2},{2,3},{3,4},{4,5},{5,6},{6,7},{7,8},{8,9},{9,10},{10,1... | collective-permute-start | bytes 1622024 | tf_op jit(solution)/shard_map/ppermute | solution.py:315
  38.0 12.3 %collective-permute-start.9 = (f32[33,32,128]{2,1,0:T(8,128)S(1)}, f32[33,32,128]{2,1,0:T(8,128)S(1)}, u32[]{:S(2)}, u32[]{:S(2)}) collective-permute-start(f32[33,32,128]{2,1,0:T(8,128)S(1)} %get-tuple-element.12.mid_ref), channel_id=1, source_target_pairs={{1,0},{2,1},{3,2},{4,3},{5,4},{6,5},{7,6},{8,7},{9,8},{10,9},{11,1... | collective-permute-start | bytes 1622024 | tf_op jit(solution)/shard_map/ppermute | solution.py:315
  50.3 0.8 copy-start
  51.1 1.0 copy-start.1

commit v3 on v2

--- a/solution.py
+++ b/solution.py
@@ -1,5 +1,3 @@
-import functools
-
 import jax
 import jax.numpy as jnp
 from jax import lax
@@ -25,9 +23,10 @@
 
 VMEM = pl.BlockSpec(memory_space=pltpu.VMEM)
 SMEM = pl.BlockSpec(memory_space=pltpu.SMEM)
-
-
-def call(kernel, name, outs, specs, scratch=()):
+HBM = pl.BlockSpec(memory_space=pltpu.HBM)
+
+
+def call(kernel, name, outs, specs, scratch=(), mebi=8):
     return pl.pallas_call(
         kernel,
         name=name,
@@ -35,7 +34,7 @@
         in_specs=specs,
         out_specs=[VMEM] * len(outs),
         scratch_shapes=list(scratch),
-        compiler_params=pltpu.CompilerParams(vmem_limit_bytes=40 * 1024 * 1024),
+        compiler_params=pltpu.CompilerParams(vmem_limit_bytes=mebi * 1024 * 1024),
     )
 
 
@@ -43,11 +42,29 @@
     return lax.broadcasted_iota(jnp.int32, shape, len(shape) - 1)
 
 
-def rhs_kernel(index_ref, gain_ref, source_ref, label_ref, block_ref, edge_ref, row_ref):
+def rhs_kernel(
+    index_ref, gain_ref, source_hbm, label_hbm, block_ref, edge_ref, source_ref, label_ref, sems
+):
+    copies = [
+        pltpu.make_async_copy(source_hbm, source_ref, sems.at[0]),
+        pltpu.make_async_copy(label_hbm, label_ref, sems.at[1]),
+    ]
+    for copy in copies:
+        copy.start()
+    sub = lax.broadcasted_iota(jnp.int32, (R, gain_ref.shape[1]), 0)
+    point = jnp.zeros(sub.shape, jnp.int32)
     for j in range(R):
-        row_ref[pl.ds(j, 1), :] = gain_ref[pl.ds(index_ref[j], 1), :]
-    rows = row_ref[...]
+        point = jnp.where(sub == j, index_ref[j], point)
+    rows = lax.dot_general(
+        (point == lane_index(point.shape)).astype(jnp.float32),
+        gain_ref[...],
+        (((1,), (1,)), ((), ())),
+        precision=lax.Precision.HIGHEST,
+        preferred_element_type=jnp.float32,
+    )
     columns = [jnp.broadcast_to(rows[:, k : k + 1], (R, LANES)) for k in range(NREG)]
+    for copy in copies:
+        copy.wait()
     group = lane_index((R, LANES)) // (2 * S)
     group_row = lane_index((8, LANES)) // (2 * S)
     edge = jnp.zeros((R, LANES), jnp.float32)
@@ -71,6 +88,14 @@
     edge_ref[R:EDGE_ROWS, :] = edge_label
 
 
+def join_kernel(block_ref, before_ref, after_ref, out_ref):
+    left = lane_index((EDGE_ROWS, LANES)) % (2 * S) < S
+    edge = jnp.where(left, before_ref[...], after_ref[...])
+    out_ref[0 : CELLS + 1] = block_ref[...]
+    out_ref[CELLS, CELLS : CELLS + 1, :] = edge[R : R + 1]
+    out_ref[CELLS + 1] = edge[:R]
+
+
 def kept_cells(order):
     return [
         (row, x)
@@ -79,23 +104,20 @@
     ]
 
 
-def merge_kernel(own_ref, low_ref, high_ref, e0, e1, e2, e3, e4, e5, down_ref, up_ref):
+def merge_kernel(own_ref, low_ref, high_ref, down_ref, up_ref):
     blocks = (low_ref, own_ref, high_ref)
     for out_ref, order in ((down_ref, (0, 1, 2, 3)), (up_ref, (3, 2, 1, 0))):
         for slot, (row, x) in enumerate(kept_cells(order)):
             out_ref[slot] = blocks[(x + SIDE) // SIDE][row * SIDE + x % SIDE]
-    left = lane_index((EDGE_ROWS, LANES)) % (2 * S) < S
-    for g, (before, after) in enumerate(((e0, e1), (e2, e3), (e4, e5))):
-        edge = jnp.where(left, before[...], after[...])
-        labels = blocks[g][CELLS, 0:CELLS, :]
-        for out_ref in (down_ref, up_ref):
-            out_ref[KEPT + g] = edge[:R]
+        for g in range(3):
+            out_ref[KEPT + g] = blocks[g][CELLS + 1]
+            labels = blocks[g][CELLS, 0:CELLS, :]
             if g < 2:
                 out_ref[KEPT + 3, g * CELLS : (g + 1) * CELLS, :] = labels
             else:
                 out_ref[KEPT + 4, 0:CELLS, :] = labels
-            out_ref[KEPT + 4, CELLS + g : CELLS + g + 1, :] = edge[R : R + 1]
-    for out_ref in (down_ref, up_ref):
+            edge = blocks[g][CELLS, CELLS : CELLS + 1, :]
+            out_ref[KEPT + 4, CELLS + g : CELLS + g + 1, :] = edge
         out_ref[KEPT + 4, CELLS + 3 : R, :] = jnp.zeros((R - CELLS - 3, LANES), jnp.float32)
 
 
@@ -106,7 +128,7 @@
         for region in range(NREG):
             hit = label == region + 1.0
             fields = [
-                jnp.where(hit, table_ref[region, column], fields[column]) for column in range(4)
+                jnp.where(hit, table_ref[column, region], fields[column]) for column in range(4)
             ]
         for column in range(4):
             cond_ref[column, z] = fields[column]
@@ -249,17 +271,42 @@
     tiles = [mat[8 * i : 8 * i + 8] for i in range(16)]
     sides = [right[8 * i : 8 * i + 8] for i in range(16)]
     sub = lax.broadcasted_iota(jnp.int32, (8, LANES), 0)
-    for k in range(S * R):
+
+    def spread(row):
+        return jnp.broadcast_to(row, (8, LANES))
+
+    for k in range(0, S * R, 4):
         p, s = divmod(k, 8)
-        row = jnp.broadcast_to(tiles[p][s : s + 1, :], (8, LANES))
-        side = jnp.broadcast_to(sides[p][s : s + 1, :], (8, LANES))
-        inverse = 1.0 / jnp.broadcast_to(row[:, k : k + 1], (8, LANES))
-        row, side = row * inverse, side * inverse
+        a = [spread(tiles[p][s + i : s + i + 1, :]) for i in range(4)]
+        b = [spread(sides[p][s + i : s + i + 1, :]) for i in range(4)]
+        e = {(i, j): spread(a[i][:, k + j : k + j + 1]) for i in range(4) for j in range(i, 4)}
+        inv = 1.0 / (e[0, 0] * e[1, 1] - e[0, 1] * e[0, 1])
+        q00, q01, q11 = e[1, 1] * inv, -e[0, 1] * inv, e[0, 0] * inv
+        w = [[q00 * e[0, j] + q01 * e[1, j] for j in (2, 3)], [q01 * e[0, j] + q11 * e[1, j] for j in (2, 3)]]
+        c00 = e[2, 2] - (e[0, 2] * w[0][0] + e[1, 2] * w[1][0])
+        c01 = e[2, 3] - (e[0, 2] * w[0][1] + e[1, 2] * w[1][1])
+        c11 = e[3, 3] - (e[0, 3] * w[0][1] + e[1, 3] * w[1][1])
+        inv = 1.0 / (c00 * c11 - c01 * c01)
+        d00, d01, d11 = c11 * inv, -c01 * inv, c00 * inv
+
+        def solve(r):
+            y0 = r[2] - (w[0][0] * r[0] + w[1][0] * r[1])
+            y1 = r[3] - (w[0][1] * r[0] + w[1][1] * r[1])
+            x2 = d00 * y0 + d01 * y1
+            x3 = d01 * y0 + d11 * y1
+            x0 = (q00 * r[0] + q01 * r[1]) - (w[0][0] * x2 + w[0][1] * x3)
+            x1 = (q01 * r[0] + q11 * r[1]) - (w[1][0] * x2 + w[1][1] * x3)
+            return [x0, x1, x2, x3]
+
+        a, b = solve(a), solve(b)
         for i in range(16):
-            column = jnp.broadcast_to(tiles[i][:, k : k + 1], (8, LANES))
-            tile, rest = tiles[i] - column * row, sides[i] - column * side
+            col = [spread(tiles[i][:, k + j : k + j + 1]) for j in range(4)]
+            tile = tiles[i] - ((col[0] * a[0] + col[1] * a[1]) + (col[2] * a[2] + col[3] * a[3]))
+            rest = sides[i] - ((col[0] * b[0] + col[1] * b[1]) + (col[2] * b[2] + col[3] * b[3]))
             if i == p:
-                tile, rest = jnp.where(sub == s, row, tile), jnp.where(sub == s, side, rest)
+                for j in range(4):
+                    tile = jnp.where(sub == s + j, a[j], tile)
+                    rest = jnp.where(sub == s + j, b[j], rest)
             tiles[i], sides[i] = tile, rest
     return jnp.concatenate(sides, 0)
 
@@ -304,15 +351,10 @@
         residual_ref[pl.ds(cell, R, stride=CELLS), :] = basis_ref[0, cell] - taken[R:]
 
 
-def neighbour(value, axes, offsets):
-    sizes = [lax.axis_size(axis) for axis in axes]
-    pairs = []
-    for at in range(sizes[0] * (sizes[1] if len(sizes) > 1 else 1)):
-        place = divmod(at, sizes[1]) if len(sizes) > 1 else (at,)
-        to = [p + o for p, o in zip(place, offsets)]
-        if all(0 <= t < n for t, n in zip(to, sizes)):
-            pairs.append((at, to[0] if len(to) == 1 else to[0] * sizes[1] + to[1]))
-    return lax.ppermute(value, axes if len(axes) > 1 else axes[0], pairs)
+def neighbour(value, axis, offset):
+    count = lax.axis_size(axis)
+    pairs = [(at, at + offset) for at in range(count) if 0 <= at + offset < count]
+    return lax.ppermute(value, axis, pairs)
 
 
 def total(values):
@@ -333,19 +375,20 @@
         rhs_kernel,
         "rhs",
         [(CELLS + 1, R, LANES), (EDGE_ROWS, LANES)],
-        [SMEM, VMEM, VMEM, VMEM],
-        [pltpu.VMEM((R, NREG), jnp.float32)],
-    )(sweep_index, sweep_gain, sources.reshape(R * CELLS, LANES), labels.reshape(CELLS, LANES))
-    low = neighbour(block, ("gx",), (1,))
-    high = neighbour(block, ("gx",), (-1,))
-    edges = [
-        neighbour(edge, ("gx", "gy"), (dx, dy)) for dx in (1, 0, -1) for dy in (1, -1)
-    ]
-    down, up = call(
-        merge_kernel, "merge", [(PLANES, R, LANES)] * 2, [VMEM] * 9
-    )(block, low, high, *edges)
-    below = neighbour(up, ("gz",), (1,))
-    above = neighbour(down, ("gz",), (-1,))
+        [SMEM, VMEM, HBM, HBM],
+        [
+            pltpu.VMEM((R * CELLS, LANES), jnp.float32),
+            pltpu.VMEM((CELLS, LANES), jnp.int32),
+            pltpu.SemaphoreType.DMA((2,)),
+        ],
+    )(sweep_index, sweep_gain.T, sources.reshape(R * CELLS, LANES), labels.reshape(CELLS, LANES))
+    before, after = neighbour(edge, "gy", 1), neighbour(edge, "gy", -1)
+    block = call(join_kernel, "join", [(CELLS + 2, R, LANES)], [VMEM] * 3)(block, before, after)[0]
+    low, high = neighbour(block, "gx", 1), neighbour(block, "gx", -1)
+    down, up = call(merge_kernel, "merge", [(PLANES, R, LANES)] * 2, [VMEM] * 3)(
+        block, low, high
+    )
+    below, above = neighbour(up, "gz", 1), neighbour(down, "gz", -1)
     basis, moments = call(
         power_kernel,
         "powers",
@@ -358,7 +401,8 @@
             pltpu.VMEM((WIDE, WIDE, 2, R, LANES), jnp.float32),
             pltpu.VMEM((WIDE, WIDE, 2, R, LANES), jnp.float32),
         ],
-    )(region_table, block, low, high, down, below, above)
+            24,
+    )(region_table.T, block, low, high, down, below, above)
     solution, residual = call(
         solve_kernel, "solve", [(R * CELLS, LANES)] * 2, [VMEM] * 2
     )(total(moments), basis)

time: 147 us -> 127 us (0.86)
  starting transfers between devices: 40.3 us -> 30.2 us
  Pallas kernels: 31.1 us -> 22 us
  local copies, waits for them, and re-layouts: 5.69 us -> 3.02 us
  waiting for transfers between devices: 4.5 us -> 6.04 us
    ppermute x10 -> x6, starting transfers between devices: 40.3 us -> 30.2 us  [neighbour(): return lax.ppermute(value, axis, pairs)]
    pallas_call x1, Pallas kernels: 19.9 us -> 10.6 us  [body(): call(solve_kernel, 'solve', [(R * CELLS, LANES)] * 2, [VMEM] * 2)]
    unnamed x12 -> x10, local copies, waits for them, and re-layouts: 5.66 us -> 2.99 us
    ppermute x10 -> x6, waiting for transfers between devices: 4.5 us -> 6.04 us  [neighbour(): return lax.ppermute(value, axis, pairs)]
  transfers between devices with their start and end apart: 10 -> 6, of which waited for: 3 -> 4; matrix products, arithmetic and copies ran while one was open for 1% -> 0% of each run, Pallas kernels for 0% -> 0%
where the time goes in v3:
time: 127 us
  blocking collectives  64.5 us (51%)
  starting transfers between devices  30.2 us (24%)
  Pallas kernels  22 us (17%)
  waiting for transfers between devices  6.04 us (5%)
  local copies, waits for them, and re-layouts  3.02 us (2%)
    all_to_all x1, blocking collectives, total(): lax.all_to_all(jnp.broadcast_to(piece, (others,) + piece.shape), ('gx', '...  39.1 us
    ppermute x6, starting transfers between devices, neighbour(): return lax.ppermute(value, axis, pairs)  30.2 us
    all_to_all x1, blocking collectives, total(): lax.all_to_all(jnp.broadcast_to(piece, (parts,) + piece.shape), 'gz', 0, 0)  13.3 us
    all_to_all x1, blocking collectives, total(): pieces = lax.all_to_all(values.reshape(parts, -1, LANES), 'gz', 0, 0)  12.2 us
    pallas_call x1, Pallas kernels, body(): call(solve_kernel, 'solve', [(R * CELLS, LANES)] * 2, [VMEM] * 2)  10.6 us
    pallas_call x1, Pallas kernels, body(): call(power_kernel, 'powers', [(S + 1, CELLS, R, LANES), (2 * R, LANES)],...  10.2 us
    ppermute x6, waiting for transfers between devices, neighbour(): return lax.ppermute(value, axis, pairs)  6.04 us
    unnamed x10, local copies, waits for them, and re-layouts  2.99 us
  transfers between devices with their start and end apart: 6, of which 4 were waited for; matrix products, arithmetic and copies ran while one was open for 0% of the time, Pallas kernels for 0%

profile of v3, /device:TPU:1, one launch (start us, length us, event | category | flops | bytes accessed | tf_op | source)
XLA Modules:
  0.0 126.7 jit_solution(2627581352594876663)
XLA Ops:
  0.6 0.0 copy-start.3
  0.6 0.0 copy-start
  0.7 0.9 copy-done
  1.6 0.0 copy-start.1
  1.6 0.7 copy-done.1
  2.3 0.0 copy-start.2
  2.3 0.7 copy-done.2
  3.0 0.0 copy-start.4
  3.0 0.7 copy-done.4
  3.6 1.1 rhs.1
  4.7 1.3 %collective-permute-start.1 = (f32[40,128]{1,0:T(8,128)S(1)}, f32[40,128]{1,0:T(8,128)S(1)}, u32[]{:S(2)}, u32[]{:S(2)}) collective-permute-start(f32[40,128]{1,0:T(8,128)S(1)} %get-tuple-element.11), channel_id=1, source_target_pairs={{16,0},{32,16},{48,32},{17,1},{33,17},{49,33},{18,2},{34,18},{50,3... | collective-permute-start | bytes 61448 | tf_op jit(solution)/shard_map/ppermute | solution.py:357
  6.0 4.6 %collective-permute-start = (f32[40,128]{1,0:T(8,128)S(1)}, f32[40,128]{1,0:T(8,128)S(1)}, u32[]{:S(2)}, u32[]{:S(2)}) collective-permute-start(f32[40,128]{1,0:T(8,128)S(1)} %get-tuple-element.11), channel_id=1, source_target_pairs={{0,16},{16,32},{32,48},{1,17},{17,33},{33,49},{2,18},{18,34},{34,5... | collective-permute-start | bytes 61448 | tf_op jit(solution)/shard_map/ppermute | solution.py:357
  10.6 0.0 collective-permute-done.1.after_ref
  10.6 0.9 collective-permute-done.before_ref
  11.5 1.3 %collective-permute-start.3 = (f32[18,32,128]{2,1,0:T(8,128)S(1)}, f32[18,32,128]{2,1,0:T(8,128)S(1)}, u32[]{:S(2)}, u32[]{:S(2)}) collective-permute-start(f32[18,32,128]{2,1,0:T(8,128)S(1)} %join.1.own_ref), channel_id=1, source_target_pairs={{64,0},{128,64},{192,128},{256,192},{320,256},{384,320},{448,384},... | collective-permute-start | bytes 884744 | tf_op jit(solution)/shard_map/ppermute | solution.py:357
  12.8 4.9 %collective-permute-start.2 = (f32[18,32,128]{2,1,0:T(8,128)S(1)}, f32[18,32,128]{2,1,0:T(8,128)S(1)}, u32[]{:S(2)}, u32[]{:S(2)}) collective-permute-start(f32[18,32,128]{2,1,0:T(8,128)S(1)} %join.1.own_ref), channel_id=1, source_target_pairs={{0,64},{64,128},{128,192},{192,256},{256,320},{320,384},{384,448},... | collective-permute-start | bytes 884744 | tf_op jit(solution)/shard_map/ppermute | solution.py:357
  17.7 2.2 %collective-permute-done.3.high_ref = f32[18,32,128]{2,1,0:T(8,128)S(1)} collective-permute-done((f32[18,32,128]{2,1,0:T(8,128)S(1)}, f32[18,32,128]{2,1,0:T(8,128)S(1)}, u32[]{:S(2)}, u32[]{:S(2)}) %collective-permute-start.3) | collective-permute-done | bytes 294944 | tf_op jit(solution)/shard_map/ppermute | solution.py:357
  19.8 1.5 %collective-permute-done.2.low_ref = f32[18,32,128]{2,1,0:T(8,128)S(1)} collective-permute-done((f32[18,32,128]{2,1,0:T(8,128)S(1)}, f32[18,32,128]{2,1,0:T(8,128)S(1)}, u32[]{:S(2)}, u32[]{:S(2)}) %collective-permute-start.2) | collective-permute-done | bytes 294944 | tf_op jit(solution)/shard_map/ppermute | solution.py:357
  21.3 0.1 merge.1
  21.4 6.6 %collective-permute-start.4 = (f32[33,32,128]{2,1,0:T(8,128)S(1)}, f32[33,32,128]{2,1,0:T(8,128)S(1)}, u32[]{:S(2)}, u32[]{:S(2)}) collective-permute-start(f32[33,32,128]{2,1,0:T(8,128)S(1)} %get-tuple-element.13), channel_id=1, source_target_pairs={{0,1},{1,2},{2,3},{3,4},{4,5},{5,6},{6,7},{7,8},{8,9},{9,10},{10,1... | collective-permute-start | bytes 1622024 | tf_op jit(solution)/shard_map/ppermute | solution.py:357
  28.1 11.5 %collective-permute-start.5 = (f32[33,32,128]{2,1,0:T(8,128)S(1)}, f32[33,32,128]{2,1,0:T(8,128)S(1)}, u32[]{:S(2)}, u32[]{:S(2)}) collective-permute-start(f32[33,32,128]{2,1,0:T(8,128)S(1)} %get-tuple-element.12.mid_ref), channel_id=1, source_target_pairs={{1,0},{2,1},{3,2},{4,3},{5,4},{6,5},{7,6},{8,7},{9,8},{10,9},{11,1... | collective-permute-start | bytes 1622024 | tf_op jit(solution)/shard_map/ppermute | solution.py:357
  39.6 0.0 collective-permute-done.4.below_ref
  39.6 1.5 %collective-permute-done.5.above_ref = f32[33,32,128]{2,1,0:T(8,128)S(1)} collective-permute-done((f32[33,32,128]{2,1,0:T(8,128)S(1)}, f32[33,32,128]{2,1,0:T(8,128)S(1)}, u32[]{:S(2)}, u32[]{:S(2)}) %collective-permute-start.5) | collective-permute-done | bytes 540704 | tf_op jit(solution)/shard_map/ppermute | solution.py:357
  41.1 0.0 copy-done.3
  41.1 10.2 %powers.1 = (f32[5,16,32,128]{3,2,1,0:T(8,128)S(1)}, f32[64,128]{1,0:T(8,128)S(1)}) custom-call(f32[4,8]{1,0:T(4,128)S(1)} %bitcast.13, f32[18,32,128]{2,1,0:T(8,128)S(1)} %join.1.own_ref, f32[18,32,128]{2,1,0:T(8,128)S(1)} %collective-permute-done.2.low_ref, f32[18,32,128]{2,1,0:T(8,128)S(1)} %collective-permute-done.3.high_ref, ...), custom_call_target="tpu_custom_call" | custom-call | tf_op jit(solution)/shard_map/powers/pallas_call | solution.py:392
  51.4 12.2 %all_to_all.15 = f32[16,4,128]{2,1,0:T(4,128)S(1)} all-to-all(f32[16,4,128]{2,1,0:T(4,128)S(1)} %bitcast.10), channel_id=1, replica_groups=mesh['gx'=16,'gy'=4,'gz'=16] {'gz'}, dimensions={0} | all-to-all | bytes 65536 | tf_op jit(solution)/shard_map/all_to_all | solution.py:363
  63.6 39.1 %all_to_all.16 = f32[64,4,128]{2,1,0:T(4,128)S(1)} all-to-all(f32[64,4,128]{2,1,0:T(4,128)S(1)} %broadcast_in_dim.6), channel_id=1, replica_groups=mesh['gx'=16,'gy'=4,'gz'=16] {'gx','gy'}, dimensions={0} | all-to-all | bytes 262144 | tf_op jit(solution)/shard_map/all_to_all | solution.py:365
  102.7 0.1 reduce_sum.19
  102.8 13.3 %all_to_all.17 = f32[16,4,128]{2,1,0:T(4,128)S(1)} all-to-all(f32[16,4,128]{2,1,0:T(4,128)S(1)} %broadcast_in_dim.7), channel_id=1, replica_groups=mesh['gx'=16,'gy'=4,'gz'=16] {'gz'}, dimensions={0} | all-to-all | bytes 65536 | tf_op jit(solution)/shard_map/all_to_all | solution.py:369
  116.1 10.6 %solve.1 = (f32[512,128]{1,0:T(8,128)}, f32[512,128]{1,0:T(8,128)}) custom-call(f32[64,128]{1,0:T(8,128)S(1)} %bitcast.9, f32[5,16,32,128]{3,2,1,0:T(8,128)S(1)} %get-tuple-element.15.basis_ref), custom_call_target="tpu_custom_call" | custom-call | tf_op jit(solution)/shard_map/solve/pallas_call | solution.py:406
  (4 shorter events, 0.1 us)
Async XLA Ops:
  0.6 40.5 %copy-start.3 = (f32[8,4]{0,1:T(4,128)S(1)}, f32[8,4]{0,1:T(4,128)}, u32[]{:S(2)}) copy-start(f32[8,4]{0,1:T(4,128)} %param.7) | copy-start | bytes 388
  0.6 1.0 copy-start
  1.6 0.7 copy-start.1
  2.3 0.7 copy-start.2
  3.0 0.7 copy-start.4
  4.7 5.9 %collective-permute-start.1 = (f32[40,128]{1,0:T(8,128)S(1)}, f32[40,128]{1,0:T(8,128)S(1)}, u32[]{:S(2)}, u32[]{:S(2)}) collective-permute-start(f32[40,128]{1,0:T(8,128)S(1)} %get-tuple-element.11), channel_id=1, source_target_pairs={{16,0},{32,16},{48,32},{17,1},{33,17},{49,33},{18,2},{34,18},{50,3... | collective-permute-start | bytes 61448 | tf_op jit(solution)/shard_map/ppermute | solution.py:357
  6.0 5.5 %collective-permute-start = (f32[40,128]{1,0:T(8,128)S(1)}, f32[40,128]{1,0:T(8,128)S(1)}, u32[]{:S(2)}, u32[]{:S(2)}) collective-permute-start(f32[40,128]{1,0:T(8,128)S(1)} %get-tuple-element.11), channel_id=1, source_target_pairs={{0,16},{16,32},{32,48},{1,17},{17,33},{33,49},{2,18},{18,34},{34,5... | collective-permute-start | bytes 61448 | tf_op jit(solution)/shard_map/ppermute | solution.py:357
  11.5 8.3 %collective-permute-start.3 = (f32[18,32,128]{2,1,0:T(8,128)S(1)}, f32[18,32,128]{2,1,0:T(8,128)S(1)}, u32[]{:S(2)}, u32[]{:S(2)}) collective-permute-start(f32[18,32,128]{2,1,0:T(8,128)S(1)} %join.1.own_ref), channel_id=1, source_target_pairs={{64,0},{128,64},{192,128},{256,192},{320,256},{384,320},{448,384},... | collective-permute-start | bytes 884744 | tf_op jit(solution)/shard_map/ppermute | solution.py:357
  12.8 8.5 %collective-permute-start.2 = (f32[18,32,128]{2,1,0:T(8,128)S(1)}, f32[18,32,128]{2,1,0:T(8,128)S(1)}, u32[]{:S(2)}, u32[]{:S(2)}) collective-permute-start(f32[18,32,128]{2,1,0:T(8,128)S(1)} %join.1.own_ref), channel_id=1, source_target_pairs={{0,64},{64,128},{128,192},{192,256},{256,320},{320,384},{384,448},... | collective-permute-start | bytes 884744 | tf_op jit(solution)/shard_map/ppermute | solution.py:357
  21.4 18.2 %collective-permute-start.4 = (f32[33,32,128]{2,1,0:T(8,128)S(1)}, f32[33,32,128]{2,1,0:T(8,128)S(1)}, u32[]{:S(2)}, u32[]{:S(2)}) collective-permute-start(f32[33,32,128]{2,1,0:T(8,128)S(1)} %get-tuple-element.13), channel_id=1, source_target_pairs={{0,1},{1,2},{2,3},{3,4},{4,5},{5,6},{6,7},{7,8},{8,9},{9,10},{10,1... | collective-permute-start | bytes 1622024 | tf_op jit(solution)/shard_map/ppermute | solution.py:357
  28.1 13.1 %collective-permute-start.5 = (f32[33,32,128]{2,1,0:T(8,128)S(1)}, f32[33,32,128]{2,1,0:T(8,128)S(1)}, u32[]{:S(2)}, u32[]{:S(2)}) collective-permute-start(f32[33,32,128]{2,1,0:T(8,128)S(1)} %get-tuple-element.12.mid_ref), channel_id=1, source_target_pairs={{1,0},{2,1},{3,2},{4,3},{5,4},{6,5},{7,6},{8,7},{9,8},{10,9},{11,1... | collective-permute-start | bytes 1622024 | tf_op jit(solution)/shard_map/ppermute | solution.py:357

commit v4 on v3

--- a/solution.py
+++ b/solution.py
@@ -23,7 +23,6 @@
 
 VMEM = pl.BlockSpec(memory_space=pltpu.VMEM)
 SMEM = pl.BlockSpec(memory_space=pltpu.SMEM)
-HBM = pl.BlockSpec(memory_space=pltpu.HBM)
 
 
 def call(kernel, name, outs, specs, scratch=(), mebi=8):
@@ -42,29 +41,23 @@
     return lax.broadcasted_iota(jnp.int32, shape, len(shape) - 1)
 
 
-def rhs_kernel(
-    index_ref, gain_ref, source_hbm, label_hbm, block_ref, edge_ref, source_ref, label_ref, sems
-):
-    copies = [
-        pltpu.make_async_copy(source_hbm, source_ref, sems.at[0]),
-        pltpu.make_async_copy(label_hbm, label_ref, sems.at[1]),
-    ]
-    for copy in copies:
-        copy.start()
+def gain_kernel(index_ref, gain_ref, row_ref):
     sub = lax.broadcasted_iota(jnp.int32, (R, gain_ref.shape[1]), 0)
     point = jnp.zeros(sub.shape, jnp.int32)
     for j in range(R):
         point = jnp.where(sub == j, index_ref[j], point)
-    rows = lax.dot_general(
+    row_ref[...] = lax.dot_general(
         (point == lane_index(point.shape)).astype(jnp.float32),
         gain_ref[...],
         (((1,), (1,)), ((), ())),
         precision=lax.Precision.HIGHEST,
         preferred_element_type=jnp.float32,
     )
+
+
+def rhs_kernel(row_ref, source_ref, label_ref, block_ref, edge_ref):
+    rows = row_ref[...]
     columns = [jnp.broadcast_to(rows[:, k : k + 1], (R, LANES)) for k in range(NREG)]
-    for copy in copies:
-        copy.wait()
     group = lane_index((R, LANES)) // (2 * S)
     group_row = lane_index((8, LANES)) // (2 * S)
     edge = jnp.zeros((R, LANES), jnp.float32)
@@ -163,26 +156,29 @@
     lax.fori_loop(1, WIDE - 1, faces, 0)
 
 
-def power_row(source_ref, target_ref, coef_ref, z, xs):
+def outside(at):
+    return max(0, S - at, at - (S + SIDE - 1))
+
+
+def power_row(source_ref, target_ref, coef_ref, z, reach):
     lane = lane_index((R, LANES))
     first, last = lane == 0, lane == LANES - 1
-    for x in xs:
+    for x in range(S - reach, S + SIDE + reach):
         center = [source_ref[z, x, t] for t in range(2)]
-        down = [pltpu.roll(value, 1, 1) for value in center]
-        up = [pltpu.roll(value, LANES - 1, 1) for value in center]
-        for t in range(2):
+        for t in range(1 if outside(x) == reach else 2):
             row = t * HALF + x
+            here, there = center[t], center[1 - t]
+            before = pltpu.roll(jnp.where(last, there, here), 1, 1)
+            after = pltpu.roll(jnp.where(first, there, here), LANES - 1, 1)
 
             def weight(k):
                 return jnp.broadcast_to(coef_ref[k, z, row : row + 1, :], (R, LANES))
 
-            after = jnp.where(last, up[1 - t], up[t])
-            before = jnp.where(first, down[1 - t], down[t])
             beside = weight(0) * source_ref[z + 1, x, t] + weight(1) * source_ref[z - 1, x, t]
             beside = beside + weight(2) * source_ref[z, x + 1, t]
             beside = beside + weight(3) * source_ref[z, x - 1, t]
             beside = beside + weight(4) * after + weight(5) * before
-            target_ref[z, x, t] = weight(6) * center[t] - beside
+            target_ref[z, x, t] = weight(6) * here - beside
 
 
 def power_kernel(
@@ -215,6 +211,8 @@
                 label_ref[base + row, g * SIDE : (g + 1) * SIDE, :] = labels
                 edge = ref[KEPT + 4, CELLS + g : CELLS + g + 1, :]
                 for x in range(SIDE):
+                    if outside(base + row) + outside(g * SIDE + x) >= S:
+                        continue
                     turn = -((row * SIDE + x) * 2 * S + S) % LANES
                     at = HALF + g * SIDE + x
                     label_ref[base + row, at : at + 1, :] = pltpu.roll(edge, turn, 1)
@@ -232,27 +230,29 @@
             edge = ref[KEPT + g]
             for row in range(SIDE):
                 for x in range(SIDE):
+                    if outside(base + row) + outside(g * SIDE + x) >= S:
+                        continue
                     turn = -((row * SIDE + x) * 2 * S + S) % LANES
                     even_ref[base + row, g * SIDE + x, 1] = pltpu.roll(edge, turn, 1)
 
     refs = (even_ref, odd_ref)
-    flats = []
     for k in range(S + 1):
         now = refs[k % 2]
-        cells = []
         for row in range(SIDE):
             for x in range(SIDE):
-                value = now[S + row, S + x, 0]
-                basis_ref[k, row * SIDE + x] = value
-                cells.append(value)
+                basis_ref[k, row * SIDE + x] = now[S + row, S + x, 0]
         if k < S:
             later = refs[1 - k % 2]
 
-            def one(z, carry):
-                power_row(now, later, coef_ref, z, range(k + 1, WIDE - 1 - k))
-                return carry
-
-            lax.fori_loop(k + 1, WIDE - 1 - k, one, 0)
+            for far in range(S - k):
+                reach = S - 1 - k - far
+
+                def one(i, carry):
+                    z = S + i if far == 0 else S - far + i * (SIDE - 1 + 2 * far)
+                    power_row(now, later, coef_ref, z, reach)
+                    return carry
+
+                lax.fori_loop(0, SIDE if far == 0 else 2, one, 0)
     for k in range(S):
         this = jnp.concatenate([basis_ref[k, cell] for cell in range(CELLS)], 1)
         after = jnp.concatenate([basis_ref[k + 1, cell] for cell in range(CELLS)], 1)
@@ -268,15 +268,41 @@
 
 
 def eliminate(mat, right):
-    tiles = [mat[8 * i : 8 * i + 8] for i in range(16)]
-    sides = [right[8 * i : 8 * i + 8] for i in range(16)]
+    for g in range(S):
+        rows = slice(g * R, (g + 1) * R)
+        solved, sides = eliminate_rows(mat[rows], right[rows], g * R)
+        both = jnp.concatenate([solved, sides], 1)
+        taken = jnp.dot(
+            mat[:, rows],
+            both,
+            precision=lax.Precision.HIGHEST,
+            preferred_element_type=jnp.float32,
+        )
+        parts = []
+        for h in range(S):
+            at = slice(h * R, (h + 1) * R)
+            parts.append(
+                (solved, sides)
+                if h == g
+                else (mat[at] - taken[at, :LANES], right[at] - taken[at, LANES:])
+            )
+        mat = jnp.concatenate([part[0] for part in parts], 0)
+        right = jnp.concatenate([part[1] for part in parts], 0)
+    return right
+
+
+def eliminate_rows(mat, right, begin):
+    count = R // 8
+    tiles = [mat[8 * i : 8 * i + 8] for i in range(count)]
+    sides = [right[8 * i : 8 * i + 8] for i in range(count)]
     sub = lax.broadcasted_iota(jnp.int32, (8, LANES), 0)
 
     def spread(row):
         return jnp.broadcast_to(row, (8, LANES))
 
-    for k in range(0, S * R, 4):
-        p, s = divmod(k, 8)
+    for step in range(0, R, 4):
+        k = begin + step
+        p, s = divmod(step, 8)
         a = [spread(tiles[p][s + i : s + i + 1, :]) for i in range(4)]
         b = [spread(sides[p][s + i : s + i + 1, :]) for i in range(4)]
         e = {(i, j): spread(a[i][:, k + j : k + j + 1]) for i in range(4) for j in range(i, 4)}
@@ -299,7 +325,7 @@
             return [x0, x1, x2, x3]
 
         a, b = solve(a), solve(b)
-        for i in range(16):
+        for i in range(count):
             col = [spread(tiles[i][:, k + j : k + j + 1]) for j in range(4)]
             tile = tiles[i] - ((col[0] * a[0] + col[1] * a[1]) + (col[2] * a[2] + col[3] * a[3]))
             rest = sides[i] - ((col[0] * b[0] + col[1] * b[1]) + (col[2] * b[2] + col[3] * b[3]))
@@ -308,7 +334,7 @@
                     tile = jnp.where(sub == s + j, a[j], tile)
                     rest = jnp.where(sub == s + j, b[j], rest)
             tiles[i], sides[i] = tile, rest
-    return jnp.concatenate(sides, 0)
+    return jnp.concatenate(tiles, 0), jnp.concatenate(sides, 0)
 
 
 def solve_kernel(moment_ref, basis_ref, solution_ref, residual_ref):
@@ -358,30 +384,21 @@
 
 
 def total(values):
-    parts = lax.axis_size("gz")
-    others = lax.axis_size("gx") * lax.axis_size("gy")
-    pieces = lax.all_to_all(values.reshape(parts, -1, LANES), "gz", 0, 0)
+    near = ("gy", "gz")
+    parts = lax.axis_size("gy") * lax.axis_size("gz")
+    others = lax.axis_size("gx")
+    piece = lax.all_to_all(values.reshape(parts, -1, LANES), near, 0, 0).sum(0)
+    pieces = lax.all_to_all(jnp.broadcast_to(piece, (others,) + piece.shape), "gx", 0, 0)
     piece = pieces.sum(0)
-    pieces = lax.all_to_all(
-        jnp.broadcast_to(piece, (others,) + piece.shape), ("gx", "gy"), 0, 0
-    )
-    piece = pieces.sum(0)
-    pieces = lax.all_to_all(jnp.broadcast_to(piece, (parts,) + piece.shape), "gz", 0, 0)
+    pieces = lax.all_to_all(jnp.broadcast_to(piece, (parts,) + piece.shape), near, 0, 0)
     return pieces.reshape(values.shape)
 
 
 def body(sources, labels, region_table, sweep_index, sweep_gain):
+    rows = call(gain_kernel, "gains", [(R, NREG)], [SMEM, VMEM])(sweep_index, sweep_gain.T)[0]
     block, edge = call(
-        rhs_kernel,
-        "rhs",
-        [(CELLS + 1, R, LANES), (EDGE_ROWS, LANES)],
-        [SMEM, VMEM, HBM, HBM],
-        [
-            pltpu.VMEM((R * CELLS, LANES), jnp.float32),
-            pltpu.VMEM((CELLS, LANES), jnp.int32),
-            pltpu.SemaphoreType.DMA((2,)),
-        ],
-    )(sweep_index, sweep_gain.T, sources.reshape(R * CELLS, LANES), labels.reshape(CELLS, LANES))
+        rhs_kernel, "rhs", [(CELLS + 1, R, LANES), (EDGE_ROWS, LANES)], [VMEM] * 3
+    )(rows, sources.reshape(R * CELLS, LANES), labels.reshape(CELLS, LANES))
     before, after = neighbour(edge, "gy", 1), neighbour(edge, "gy", -1)
     block = call(join_kernel, "join", [(CELLS + 2, R, LANES)], [VMEM] * 3)(block, before, after)[0]
     low, high = neighbour(block, "gx", 1), neighbour(block, "gx", -1)

time: 127 us -> 123 us (0.969)
  Pallas kernels: 22 us -> 18.7 us
    pallas_call x1, Pallas kernels: 10.2 us -> 8.57 us  [body(): call(power_kernel, 'powers', [(S + 1, CELLS, R, LANES), (2 * R, LANES)],...]
    pallas_call x1, Pallas kernels: 10.6 us -> 9.07 us  [body(): call(solve_kernel, 'solve', [(R * CELLS, LANES)] * 2, [VMEM] * 2)]
where the time goes in v4:
time: 123 us; the launch traced here: 122 us
  blocking collectives  63.6 us (52%)
  starting transfers between devices  30.2 us (25%)
  Pallas kernels  18.7 us (15%)
  waiting for transfers between devices  6.04 us (5%)
  local copies, waits for them, and re-layouts  3.03 us (2%)
    all_to_all x1, blocking collectives, total(): lax.all_to_all(jnp.broadcast_to(piece, (others,) + piece.shape), 'gx', 0, 0)  31.3 us
    ppermute x6, starting transfers between devices, neighbour(): return lax.ppermute(value, axis, pairs)  30.2 us
    all_to_all x1, blocking collectives, total(): piece = lax.all_to_all(values.reshape(parts, -1, LANES), near, 0, 0).sum(0)  17.6 us
    all_to_all x1, blocking collectives, total(): lax.all_to_all(jnp.broadcast_to(piece, (parts,) + piece.shape), near, 0, 0)  14.7 us
    pallas_call x1, Pallas kernels, body(): call(solve_kernel, 'solve', [(R * CELLS, LANES)] * 2, [VMEM] * 2)  9.07 us
    pallas_call x1, Pallas kernels, body(): call(power_kernel, 'powers', [(S + 1, CELLS, R, LANES), (2 * R, LANES)],...  8.57 us
    ppermute x6, waiting for transfers between devices, neighbour(): return lax.ppermute(value, axis, pairs)  6.04 us
    unnamed x10, local copies, waits for them, and re-layouts  3 us
  transfers between devices with their start and end apart: 6, of which 4 were waited for; matrix products, arithmetic and copies ran while one was open for 0% of the time, Pallas kernels for 0%

profile of v4, /device:TPU:1, one launch (start us, length us, event | category | flops | bytes accessed | tf_op | source)
XLA Modules:
  0.0 122.5 jit_solution(4731086263485554960)
XLA Ops:
  0.6 0.0 copy-start.2
  0.6 0.7 copy-done.2
  1.3 0.0 copy-start.4
  1.3 0.7 copy-done.4
  2.0 0.0 copy-start.3
  2.0 0.7 gains.1.row_ref
  2.7 0.0 copy-start
  2.7 1.0 copy-done
  3.6 0.0 copy-start.1
  3.6 0.7 copy-done.1
  4.3 0.3 rhs.1
  4.6 1.3 %collective-permute-start.1 = (f32[40,128]{1,0:T(8,128)S(1)}, f32[40,128]{1,0:T(8,128)S(1)}, u32[]{:S(2)}, u32[]{:S(2)}) collective-permute-start(f32[40,128]{1,0:T(8,128)S(1)} %get-tuple-element.11), channel_id=1, source_target_pairs={{16,0},{32,16},{48,32},{17,1},{33,17},{49,33},{18,2},{34,18},{50,3... | collective-permute-start | bytes 61448 | tf_op jit(solution)/shard_map/ppermute | solution.py:383
  5.9 4.6 %collective-permute-start = (f32[40,128]{1,0:T(8,128)S(1)}, f32[40,128]{1,0:T(8,128)S(1)}, u32[]{:S(2)}, u32[]{:S(2)}) collective-permute-start(f32[40,128]{1,0:T(8,128)S(1)} %get-tuple-element.11), channel_id=1, source_target_pairs={{0,16},{16,32},{32,48},{1,17},{17,33},{33,49},{2,18},{18,34},{34,5... | collective-permute-start | bytes 61448 | tf_op jit(solution)/shard_map/ppermute | solution.py:383
  10.5 0.0 collective-permute-done.1.after_ref
  10.5 0.9 collective-permute-done.before_ref
  11.4 1.3 %collective-permute-start.3 = (f32[18,32,128]{2,1,0:T(8,128)S(1)}, f32[18,32,128]{2,1,0:T(8,128)S(1)}, u32[]{:S(2)}, u32[]{:S(2)}) collective-permute-start(f32[18,32,128]{2,1,0:T(8,128)S(1)} %join.1.own_ref), channel_id=1, source_target_pairs={{64,0},{128,64},{192,128},{256,192},{320,256},{384,320},{448,384},... | collective-permute-start | bytes 884744 | tf_op jit(solution)/shard_map/ppermute | solution.py:383
  12.7 4.9 %collective-permute-start.2 = (f32[18,32,128]{2,1,0:T(8,128)S(1)}, f32[18,32,128]{2,1,0:T(8,128)S(1)}, u32[]{:S(2)}, u32[]{:S(2)}) collective-permute-start(f32[18,32,128]{2,1,0:T(8,128)S(1)} %join.1.own_ref), channel_id=1, source_target_pairs={{0,64},{64,128},{128,192},{192,256},{256,320},{320,384},{384,448},... | collective-permute-start | bytes 884744 | tf_op jit(solution)/shard_map/ppermute | solution.py:383
  17.6 2.2 %collective-permute-done.3.high_ref = f32[18,32,128]{2,1,0:T(8,128)S(1)} collective-permute-done((f32[18,32,128]{2,1,0:T(8,128)S(1)}, f32[18,32,128]{2,1,0:T(8,128)S(1)}, u32[]{:S(2)}, u32[]{:S(2)}) %collective-permute-start.3) | collective-permute-done | bytes 294944 | tf_op jit(solution)/shard_map/ppermute | solution.py:383
  19.8 1.5 %collective-permute-done.2.low_ref = f32[18,32,128]{2,1,0:T(8,128)S(1)} collective-permute-done((f32[18,32,128]{2,1,0:T(8,128)S(1)}, f32[18,32,128]{2,1,0:T(8,128)S(1)}, u32[]{:S(2)}, u32[]{:S(2)}) %collective-permute-start.2) | collective-permute-done | bytes 294944 | tf_op jit(solution)/shard_map/ppermute | solution.py:383
  21.2 0.1 merge.1
  21.3 6.6 %collective-permute-start.4 = (f32[33,32,128]{2,1,0:T(8,128)S(1)}, f32[33,32,128]{2,1,0:T(8,128)S(1)}, u32[]{:S(2)}, u32[]{:S(2)}) collective-permute-start(f32[33,32,128]{2,1,0:T(8,128)S(1)} %get-tuple-element.13), channel_id=1, source_target_pairs={{0,1},{1,2},{2,3},{3,4},{4,5},{5,6},{6,7},{7,8},{8,9},{9,10},{10,1... | collective-permute-start | bytes 1622024 | tf_op jit(solution)/shard_map/ppermute | solution.py:383
  28.0 11.5 %collective-permute-start.5 = (f32[33,32,128]{2,1,0:T(8,128)S(1)}, f32[33,32,128]{2,1,0:T(8,128)S(1)}, u32[]{:S(2)}, u32[]{:S(2)}) collective-permute-start(f32[33,32,128]{2,1,0:T(8,128)S(1)} %get-tuple-element.12.mid_ref), channel_id=1, source_target_pairs={{1,0},{2,1},{3,2},{4,3},{5,4},{6,5},{7,6},{8,7},{9,8},{10,9},{11,1... | collective-permute-start | bytes 1622024 | tf_op jit(solution)/shard_map/ppermute | solution.py:383
  39.5 0.0 collective-permute-done.4.below_ref
  39.5 1.5 %collective-permute-done.5.above_ref = f32[33,32,128]{2,1,0:T(8,128)S(1)} collective-permute-done((f32[33,32,128]{2,1,0:T(8,128)S(1)}, f32[33,32,128]{2,1,0:T(8,128)S(1)}, u32[]{:S(2)}, u32[]{:S(2)}) %collective-permute-start.5) | collective-permute-done | bytes 540704 | tf_op jit(solution)/shard_map/ppermute | solution.py:383
  41.0 0.0 copy-done.3
  41.1 8.6 %powers.1 = (f32[5,16,32,128]{3,2,1,0:T(8,128)S(1)}, f32[64,128]{1,0:T(8,128)S(1)}) custom-call(f32[4,8]{1,0:T(4,128)S(1)} %bitcast.16, f32[18,32,128]{2,1,0:T(8,128)S(1)} %join.1.own_ref, f32[18,32,128]{2,1,0:T(8,128)S(1)} %collective-permute-done.2.low_ref, f32[18,32,128]{2,1,0:T(8,128)S(1)} %collective-permute-done.3.high_ref, ...), custom_call_target="tpu_custom_call" | custom-call | tf_op jit(solution)/shard_map/powers/pallas_call | solution.py:409
  49.6 17.6 %all_to_all.15 = f32[64,1,128]{2,1,0:T(1,128)S(1)} all-to-all(f32[64,1,128]{2,1,0:T(1,128)S(1)} %bitcast.13), channel_id=1, replica_groups=mesh['gx'=16,'gy'=4,'gz'=16] {'gy','gz'}, dimensions={0} | all-to-all | bytes 65536 | tf_op jit(solution)/shard_map/all_to_all | solution.py:390
  67.3 0.1 reduce_sum.18
  67.4 31.3 %all_to_all.16 = f32[16,1,128]{2,1,0:T(1,128)S(1)} all-to-all(f32[16,1,128]{2,1,0:T(1,128)S(1)} %broadcast_in_dim.6), channel_id=1, replica_groups=mesh['gx'=16,'gy'=4,'gz'=16] {'gx'}, dimensions={0} | all-to-all | bytes 16384 | tf_op jit(solution)/shard_map/all_to_all | solution.py:391
  98.7 14.7 %all_to_all.17 = f32[64,1,128]{2,1,0:T(1,128)S(1)} all-to-all(f32[64,1,128]{2,1,0:T(1,128)S(1)} %broadcast_in_dim.7), channel_id=1, replica_groups=mesh['gx'=16,'gy'=4,'gz'=16] {'gy','gz'}, dimensions={0} | all-to-all | bytes 65536 | tf_op jit(solution)/shard_map/all_to_all | solution.py:393
  113.4 9.1 %solve.1 = (f32[512,128]{1,0:T(8,128)}, f32[512,128]{1,0:T(8,128)}) custom-call(f32[64,128]{1,0:T(8,128)S(1)} %bitcast.12, f32[5,16,32,128]{3,2,1,0:T(8,128)S(1)} %get-tuple-element.15.basis_ref), custom_call_target="tpu_custom_call" | custom-call | tf_op jit(solution)/shard_map/solve/pallas_call | solution.py:423
  (4 shorter events, 0.1 us)
Async XLA Ops:
  0.6 0.7 copy-start.2
  1.3 0.7 copy-start.4
  2.0 39.1 %copy-start.3 = (f32[8,4]{0,1:T(4,128)S(1)}, f32[8,4]{0,1:T(4,128)}, u32[]{:S(2)}) copy-start(f32[8,4]{0,1:T(4,128)} %param.7) | copy-start | bytes 388
  2.7 1.0 copy-start
  3.6 0.7 copy-start.1
  4.6 5.9 %collective-permute-start.1 = (f32[40,128]{1,0:T(8,128)S(1)}, f32[40,128]{1,0:T(8,128)S(1)}, u32[]{:S(2)}, u32[]{:S(2)}) collective-permute-start(f32[40,128]{1,0:T(8,128)S(1)} %get-tuple-element.11), channel_id=1, source_target_pairs={{16,0},{32,16},{48,32},{17,1},{33,17},{49,33},{18,2},{34,18},{50,3... | collective-permute-start | bytes 61448 | tf_op jit(solution)/shard_map/ppermute | solution.py:383
  5.9 5.5 %collective-permute-start = (f32[40,128]{1,0:T(8,128)S(1)}, f32[40,128]{1,0:T(8,128)S(1)}, u32[]{:S(2)}, u32[]{:S(2)}) collective-permute-start(f32[40,128]{1,0:T(8,128)S(1)} %get-tuple-element.11), channel_id=1, source_target_pairs={{0,16},{16,32},{32,48},{1,17},{17,33},{33,49},{2,18},{18,34},{34,5... | collective-permute-start | bytes 61448 | tf_op jit(solution)/shard_map/ppermute | solution.py:383
  11.4 8.3 %collective-permute-start.3 = (f32[18,32,128]{2,1,0:T(8,128)S(1)}, f32[18,32,128]{2,1,0:T(8,128)S(1)}, u32[]{:S(2)}, u32[]{:S(2)}) collective-permute-start(f32[18,32,128]{2,1,0:T(8,128)S(1)} %join.1.own_ref), channel_id=1, source_target_pairs={{64,0},{128,64},{192,128},{256,192},{320,256},{384,320},{448,384},... | collective-permute-start | bytes 884744 | tf_op jit(solution)/shard_map/ppermute | solution.py:383
  12.7 8.5 %collective-permute-start.2 = (f32[18,32,128]{2,1,0:T(8,128)S(1)}, f32[18,32,128]{2,1,0:T(8,128)S(1)}, u32[]{:S(2)}, u32[]{:S(2)}) collective-permute-start(f32[18,32,128]{2,1,0:T(8,128)S(1)} %join.1.own_ref), channel_id=1, source_target_pairs={{0,64},{64,128},{128,192},{192,256},{256,320},{320,384},{384,448},... | collective-permute-start | bytes 884744 | tf_op jit(solution)/shard_map/ppermute | solution.py:383
  21.3 18.2 %collective-permute-start.4 = (f32[33,32,128]{2,1,0:T(8,128)S(1)}, f32[33,32,128]{2,1,0:T(8,128)S(1)}, u32[]{:S(2)}, u32[]{:S(2)}) collective-permute-start(f32[33,32,128]{2,1,0:T(8,128)S(1)} %get-tuple-element.13), channel_id=1, source_target_pairs={{0,1},{1,2},{2,3},{3,4},{4,5},{5,6},{6,7},{7,8},{8,9},{9,10},{10,1... | collective-permute-start | bytes 1622024 | tf_op jit(solution)/shard_map/ppermute | solution.py:383
  28.0 13.1 %collective-permute-start.5 = (f32[33,32,128]{2,1,0:T(8,128)S(1)}, f32[33,32,128]{2,1,0:T(8,128)S(1)}, u32[]{:S(2)}, u32[]{:S(2)}) collective-permute-start(f32[33,32,128]{2,1,0:T(8,128)S(1)} %get-tuple-element.12.mid_ref), channel_id=1, source_target_pairs={{1,0},{2,1},{3,2},{4,3},{5,4},{6,5},{7,6},{8,7},{9,8},{10,9},{11,1... | collective-permute-start | bytes 1622024 | tf_op jit(solution)/shard_map/ppermute | solution.py:383

commit v5 on v4

--- a/solution.py
+++ b/solution.py
@@ -23,6 +23,7 @@
 
 VMEM = pl.BlockSpec(memory_space=pltpu.VMEM)
 SMEM = pl.BlockSpec(memory_space=pltpu.SMEM)
+HBM = pl.BlockSpec(memory_space=pltpu.HBM)
 
 
 def call(kernel, name, outs, specs, scratch=(), mebi=8):
@@ -41,22 +42,30 @@
     return lax.broadcasted_iota(jnp.int32, shape, len(shape) - 1)
 
 
-def gain_kernel(index_ref, gain_ref, row_ref):
+def rhs_kernel(
+    index_ref, gain_hbm, source_hbm, label_hbm, block_ref, edge_ref, gain_ref, source_ref, label_ref, sems
+):
+    copies = [
+        pltpu.make_async_copy(gain_hbm, gain_ref, sems.at[0]),
+        pltpu.make_async_copy(label_hbm, label_ref, sems.at[1]),
+        pltpu.make_async_copy(source_hbm, source_ref, sems.at[2]),
+    ]
+    for copy in copies:
+        copy.start()
     sub = lax.broadcasted_iota(jnp.int32, (R, gain_ref.shape[1]), 0)
     point = jnp.zeros(sub.shape, jnp.int32)
     for j in range(R):
         point = jnp.where(sub == j, index_ref[j], point)
-    row_ref[...] = lax.dot_general(
+    copies[0].wait()
+    rows = lax.dot_general(
         (point == lane_index(point.shape)).astype(jnp.float32),
         gain_ref[...],
         (((1,), (1,)), ((), ())),
         precision=lax.Precision.HIGHEST,
         preferred_element_type=jnp.float32,
     )
-
-
-def rhs_kernel(row_ref, source_ref, label_ref, block_ref, edge_ref):
-    rows = row_ref[...]
+    copies[1].wait()
+    copies[2].wait()
     columns = [jnp.broadcast_to(rows[:, k : k + 1], (R, LANES)) for k in range(NREG)]
     group = lane_index((R, LANES)) // (2 * S)
     group_row = lane_index((8, LANES)) // (2 * S)
@@ -235,25 +244,12 @@
                     turn = -((row * SIDE + x) * 2 * S + S) % LANES
                     even_ref[base + row, g * SIDE + x, 1] = pltpu.roll(edge, turn, 1)
 
-    refs = (even_ref, odd_ref)
-    for k in range(S + 1):
-        now = refs[k % 2]
+    def keep(k):
         for row in range(SIDE):
             for x in range(SIDE):
-                basis_ref[k, row * SIDE + x] = now[S + row, S + x, 0]
-        if k < S:
-            later = refs[1 - k % 2]
-
-            for far in range(S - k):
-                reach = S - 1 - k - far
-
-                def one(i, carry):
-                    z = S + i if far == 0 else S - far + i * (SIDE - 1 + 2 * far)
-                    power_row(now, later, coef_ref, z, reach)
-                    return carry
-
-                lax.fori_loop(0, SIDE if far == 0 else 2, one, 0)
-    for k in range(S):
+                basis_ref[k, row * SIDE + x] = refs[k % 2][S + row, S + x, 0]
+
+    def moments(k):
         this = jnp.concatenate([basis_ref[k, cell] for cell in range(CELLS)], 1)
         after = jnp.concatenate([basis_ref[k + 1, cell] for cell in range(CELLS)], 1)
         pair = lax.dot_general(
@@ -265,6 +261,27 @@
         )
         half, at = divmod(2 * k * R, LANES)
         moment_ref[half * R : (half + 1) * R, at : at + 2 * R] = pair
+
+    refs = (even_ref, odd_ref)
+    keep(0)
+    for k in range(S - 1):
+        now, later = refs[k % 2], refs[1 - k % 2]
+        for far in range(S - k):
+            reach = S - 1 - k - far
+
+            def one(i, carry):
+                z = S + i if far == 0 else S - far + i * (SIDE - 1 + 2 * far)
+                power_row(now, later, coef_ref, z, reach)
+                return carry
+
+            lax.fori_loop(0, SIDE if far == 0 else 2, one, 0)
+        keep(k + 1)
+    for k in range(S - 1):
+        moments(k)
+    for row in range(SIDE):
+        power_row(refs[(S - 1) % 2], refs[S % 2], coef_ref, S + row, 0)
+    keep(S)
+    moments(S - 1)
 
 
 def eliminate(mat, right):
@@ -300,40 +317,43 @@
     def spread(row):
         return jnp.broadcast_to(row, (8, LANES))
 
-    for step in range(0, R, 4):
-        k = begin + step
-        p, s = divmod(step, 8)
-        a = [spread(tiles[p][s + i : s + i + 1, :]) for i in range(4)]
-        b = [spread(sides[p][s + i : s + i + 1, :]) for i in range(4)]
-        e = {(i, j): spread(a[i][:, k + j : k + j + 1]) for i in range(4) for j in range(i, 4)}
-        inv = 1.0 / (e[0, 0] * e[1, 1] - e[0, 1] * e[0, 1])
-        q00, q01, q11 = e[1, 1] * inv, -e[0, 1] * inv, e[0, 0] * inv
-        w = [[q00 * e[0, j] + q01 * e[1, j] for j in (2, 3)], [q01 * e[0, j] + q11 * e[1, j] for j in (2, 3)]]
-        c00 = e[2, 2] - (e[0, 2] * w[0][0] + e[1, 2] * w[1][0])
-        c01 = e[2, 3] - (e[0, 2] * w[0][1] + e[1, 2] * w[1][1])
-        c11 = e[3, 3] - (e[0, 3] * w[0][1] + e[1, 3] * w[1][1])
-        inv = 1.0 / (c00 * c11 - c01 * c01)
-        d00, d01, d11 = c11 * inv, -c01 * inv, c00 * inv
-
-        def solve(r):
-            y0 = r[2] - (w[0][0] * r[0] + w[1][0] * r[1])
-            y1 = r[3] - (w[0][1] * r[0] + w[1][1] * r[1])
-            x2 = d00 * y0 + d01 * y1
-            x3 = d01 * y0 + d11 * y1
-            x0 = (q00 * r[0] + q01 * r[1]) - (w[0][0] * x2 + w[0][1] * x3)
-            x1 = (q01 * r[0] + q11 * r[1]) - (w[1][0] * x2 + w[1][1] * x3)
-            return [x0, x1, x2, x3]
-
-        a, b = solve(a), solve(b)
+    for p in range(count):
+        k = begin + 8 * p
+        a = [spread(tiles[p][i : i + 1, :]) for i in range(8)]
+        b = [spread(sides[p][i : i + 1, :]) for i in range(8)]
+        e = {(i, j): spread(a[i][:, k + j : k + j + 1]) for i in range(8) for j in range(i, 8)}
+        upper = {}
+        for m in range(0, 8, 2):
+            n = m + 1
+            inv = 1.0 / (e[m, m] * e[n, n] - e[m, n] * e[m, n])
+            q00, q01, q11 = e[n, n] * inv, -e[m, n] * inv, e[m, m] * inv
+            for j in range(m + 2, 8):
+                upper[m, j] = q00 * e[m, j] + q01 * e[n, j]
+                upper[n, j] = q01 * e[m, j] + q11 * e[n, j]
+            for i in range(m + 2, 8):
+                for j in range(i, 8):
+                    e[i, j] = e[i, j] - (e[m, i] * upper[m, j] + e[n, i] * upper[n, j])
+            for rows in (a, b):
+                for j in range(m + 2, 8):
+                    rows[j] = rows[j] - (upper[m, j] * rows[m] + upper[n, j] * rows[n])
+                rows[m], rows[n] = q00 * rows[m] + q01 * rows[n], q01 * rows[m] + q11 * rows[n]
+        for rows in (a, b):
+            for m in range(6, 0, -2):
+                for i in range(m):
+                    rows[i] = rows[i] - (upper[i, m] * rows[m] + upper[i, m + 1] * rows[m + 1])
         for i in range(count):
-            col = [spread(tiles[i][:, k + j : k + j + 1]) for j in range(4)]
-            tile = tiles[i] - ((col[0] * a[0] + col[1] * a[1]) + (col[2] * a[2] + col[3] * a[3]))
-            rest = sides[i] - ((col[0] * b[0] + col[1] * b[1]) + (col[2] * b[2] + col[3] * b[3]))
             if i == p:
-                for j in range(4):
-                    tile = jnp.where(sub == s + j, a[j], tile)
-                    rest = jnp.where(sub == s + j, b[j], rest)
-            tiles[i], sides[i] = tile, rest
+                continue
+            col = [spread(tiles[i][:, k + j : k + j + 1]) for j in range(8)]
+            for parts, rows in ((tiles, a), (sides, b)):
+                terms = [col[j] * rows[j] for j in range(8)]
+                pairs = [terms[j] + terms[j + 1] for j in range(0, 8, 2)]
+                parts[i] = parts[i] - ((pairs[0] + pairs[1]) + (pairs[2] + pairs[3]))
+        for parts, rows in ((tiles, a), (sides, b)):
+            merged = rows[0]
+            for j in range(1, 8):
+                merged = jnp.where(sub == j, rows[j], merged)
+            parts[p] = merged
     return jnp.concatenate(tiles, 0), jnp.concatenate(sides, 0)
 
 
@@ -395,10 +415,19 @@
 
 
 def body(sources, labels, region_table, sweep_index, sweep_gain):
-    rows = call(gain_kernel, "gains", [(R, NREG)], [SMEM, VMEM])(sweep_index, sweep_gain.T)[0]
     block, edge = call(
-        rhs_kernel, "rhs", [(CELLS + 1, R, LANES), (EDGE_ROWS, LANES)], [VMEM] * 3
-    )(rows, sources.reshape(R * CELLS, LANES), labels.reshape(CELLS, LANES))
+        rhs_kernel,
+        "rhs",
+        [(CELLS + 1, R, LANES), (EDGE_ROWS, LANES)],
+        [SMEM, HBM, HBM, HBM],
+        [
+            pltpu.VMEM((NREG, sweep_gain.shape[0]), jnp.float32),
+            pltpu.VMEM((R * CELLS, LANES), jnp.float32),
+            pltpu.VMEM((CELLS, LANES), jnp.int32),
+            pltpu.SemaphoreType.DMA((3,)),
+        ],
+        60,
+    )(sweep_index, sweep_gain.T, sources.reshape(R * CELLS, LANES), labels.reshape(CELLS, LANES))
     before, after = neighbour(edge, "gy", 1), neighbour(edge, "gy", -1)
     block = call(join_kernel, "join", [(CELLS + 2, R, LANES)], [VMEM] * 3)(block, before, after)[0]
     low, high = neighbour(block, "gx", 1), neighbour(block, "gx", -1)

time: 123 us -> 121 us (0.984)
  local copies, waits for them, and re-layouts: 3.03 us -> 0.99 us
    unnamed x10 -> x4, local copies, waits for them, and re-layouts: 3 us -> 0.96 us
    pallas_call x2 -> x1, Pallas kernels: 0.96 us -> 2.7 us  [body(): call(rhs_kernel, 'rhs', [(CELLS + 1, R, LANES), (EDGE_ROWS, LANES)], [SME...]
    pallas_call x1, Pallas kernels: 9.07 us -> 7.56 us  [body(): call(solve_kernel, 'solve', [(R * CELLS, LANES)] * 2, [VMEM] * 2)]
where the time goes in v5:
time: 121 us; the launch traced here: 120 us
  blocking collectives  63.6 us (53%)
  starting transfers between devices  30.2 us (25%)
  Pallas kernels  18.5 us (15%)
  waiting for transfers between devices  6.25 us (5%)
    all_to_all x1, blocking collectives, total(): lax.all_to_all(jnp.broadcast_to(piece, (others,) + piece.shape), 'gx', 0, 0)  31.3 us
    ppermute x6, starting transfers between devices, neighbour(): return lax.ppermute(value, axis, pairs)  30.2 us
    all_to_all x1, blocking collectives, total(): piece = lax.all_to_all(values.reshape(parts, -1, LANES), near, 0, 0).sum(0)  17.6 us
    all_to_all x1, blocking collectives, total(): lax.all_to_all(jnp.broadcast_to(piece, (parts,) + piece.shape), near, 0, 0)  14.7 us
    pallas_call x1, Pallas kernels, body(): call(power_kernel, 'powers', [(S + 1, CELLS, R, LANES), (2 * R, LANES)],...  8.15 us
    pallas_call x1, Pallas kernels, body(): call(solve_kernel, 'solve', [(R * CELLS, LANES)] * 2, [VMEM] * 2)  7.56 us
    ppermute x6, waiting for transfers between devices, neighbour(): return lax.ppermute(value, axis, pairs)  6.25 us
    pallas_call x1, Pallas kernels, body(): call(rhs_kernel, 'rhs', [(CELLS + 1, R, LANES), (EDGE_ROWS, LANES)], [SME...  2.7 us
  transfers between devices with their start and end apart: 6, of which 4 were waited for; matrix products, arithmetic and copies ran while one was open for 0% of the time, Pallas kernels for 0%

profile of v5, /device:TPU:1, one launch (start us, length us, event | category | flops | bytes accessed | tf_op | source)
XLA Modules:
  0.0 120.4 jit_solution(3214667041082591810)
XLA Ops:
  0.6 0.0 copy-start.1
  0.6 2.7 %rhs.1 = (f32[17,32,128]{2,1,0:T(8,128)}, f32[40,128]{1,0:T(8,128)}) custom-call(s32[32]{0:T(128)} %index_ref.1, f32[8,32]{1,0:T(8,128)} %bitcast.17, f32[512,128]{1,0:T(8,128)} %bitcast.14, s32[16,128]{1,0:T(8,128)} %bitcast.16), custom_call_target="tpu_custom_call" | custom-call | tf_op jit(solution)/shard_map/rhs/pallas_call | solution.py:418
  3.4 1.3 %collective-permute-start.1 = (f32[40,128]{1,0:T(8,128)}, f32[40,128]{1,0:T(8,128)S(1)}, u32[]{:S(2)}, u32[]{:S(2)}) collective-permute-start(f32[40,128]{1,0:T(8,128)} %get-tuple-element.11), channel_id=1, source_target_pairs={{16,0},{32,16},{48,32},{17,1},{33,17},{49,33},{18,2},{34,18},{50,3... | collective-permute-start | bytes 61448 | tf_op jit(solution)/shard_map/ppermute | solution.py:403
  4.7 4.6 %collective-permute-start = (f32[40,128]{1,0:T(8,128)}, f32[40,128]{1,0:T(8,128)S(1)}, u32[]{:S(2)}, u32[]{:S(2)}) collective-permute-start(f32[40,128]{1,0:T(8,128)} %get-tuple-element.11), channel_id=1, source_target_pairs={{0,16},{16,32},{32,48},{1,17},{17,33},{33,49},{2,18},{18,34},{34,5... | collective-permute-start | bytes 61448 | tf_op jit(solution)/shard_map/ppermute | solution.py:403
  9.2 0.0 collective-permute-done.1.after_ref
  9.2 1.1 collective-permute-done.before_ref
  10.3 0.0 copy-start
  10.3 1.0 copy-done
  11.3 1.3 %collective-permute-start.3 = (f32[18,32,128]{2,1,0:T(8,128)S(1)}, f32[18,32,128]{2,1,0:T(8,128)S(1)}, u32[]{:S(2)}, u32[]{:S(2)}) collective-permute-start(f32[18,32,128]{2,1,0:T(8,128)S(1)} %join.1.own_ref), channel_id=1, source_target_pairs={{64,0},{128,64},{192,128},{256,192},{320,256},{384,320},{448,384},... | collective-permute-start | bytes 884744 | tf_op jit(solution)/shard_map/ppermute | solution.py:403
  12.6 4.9 %collective-permute-start.2 = (f32[18,32,128]{2,1,0:T(8,128)S(1)}, f32[18,32,128]{2,1,0:T(8,128)S(1)}, u32[]{:S(2)}, u32[]{:S(2)}) collective-permute-start(f32[18,32,128]{2,1,0:T(8,128)S(1)} %join.1.own_ref), channel_id=1, source_target_pairs={{0,64},{64,128},{128,192},{192,256},{256,320},{320,384},{384,448},... | collective-permute-start | bytes 884744 | tf_op jit(solution)/shard_map/ppermute | solution.py:403
  17.5 2.2 %collective-permute-done.3.high_ref = f32[18,32,128]{2,1,0:T(8,128)S(1)} collective-permute-done((f32[18,32,128]{2,1,0:T(8,128)S(1)}, f32[18,32,128]{2,1,0:T(8,128)S(1)}, u32[]{:S(2)}, u32[]{:S(2)}) %collective-permute-start.3) | collective-permute-done | bytes 294944 | tf_op jit(solution)/shard_map/ppermute | solution.py:403
  19.7 1.5 %collective-permute-done.2.low_ref = f32[18,32,128]{2,1,0:T(8,128)S(1)} collective-permute-done((f32[18,32,128]{2,1,0:T(8,128)S(1)}, f32[18,32,128]{2,1,0:T(8,128)S(1)}, u32[]{:S(2)}, u32[]{:S(2)}) %collective-permute-start.2) | collective-permute-done | bytes 294944 | tf_op jit(solution)/shard_map/ppermute | solution.py:403
  21.1 0.1 merge.1
  21.2 6.6 %collective-permute-start.4 = (f32[33,32,128]{2,1,0:T(8,128)S(1)}, f32[33,32,128]{2,1,0:T(8,128)S(1)}, u32[]{:S(2)}, u32[]{:S(2)}) collective-permute-start(f32[33,32,128]{2,1,0:T(8,128)S(1)} %get-tuple-element.13), channel_id=1, source_target_pairs={{0,1},{1,2},{2,3},{3,4},{4,5},{5,6},{6,7},{7,8},{8,9},{9,10},{10,1... | collective-permute-start | bytes 1622024 | tf_op jit(solution)/shard_map/ppermute | solution.py:403
  27.9 11.5 %collective-permute-start.5 = (f32[33,32,128]{2,1,0:T(8,128)S(1)}, f32[33,32,128]{2,1,0:T(8,128)S(1)}, u32[]{:S(2)}, u32[]{:S(2)}) collective-permute-start(f32[33,32,128]{2,1,0:T(8,128)S(1)} %get-tuple-element.12.mid_ref), channel_id=1, source_target_pairs={{1,0},{2,1},{3,2},{4,3},{5,4},{6,5},{7,6},{8,7},{9,8},{10,9},{11,1... | collective-permute-start | bytes 1622024 | tf_op jit(solution)/shard_map/ppermute | solution.py:403
  39.4 0.0 collective-permute-done.4.below_ref
  39.4 1.5 %collective-permute-done.5.above_ref = f32[33,32,128]{2,1,0:T(8,128)S(1)} collective-permute-done((f32[33,32,128]{2,1,0:T(8,128)S(1)}, f32[33,32,128]{2,1,0:T(8,128)S(1)}, u32[]{:S(2)}, u32[]{:S(2)}) %collective-permute-start.5) | collective-permute-done | bytes 540704 | tf_op jit(solution)/shard_map/ppermute | solution.py:403
  41.0 0.0 copy-done.1
  41.0 8.1 %powers.1 = (f32[5,16,32,128]{3,2,1,0:T(8,128)S(1)}, f32[64,128]{1,0:T(8,128)S(1)}) custom-call(f32[4,8]{1,0:T(4,128)S(1)} %bitcast.13, f32[18,32,128]{2,1,0:T(8,128)S(1)} %join.1.own_ref, f32[18,32,128]{2,1,0:T(8,128)S(1)} %collective-permute-done.2.low_ref, f32[18,32,128]{2,1,0:T(8,128)S(1)} %collective-permute-done.3.high_ref, ...), custom_call_target="tpu_custom_call" | custom-call | tf_op jit(solution)/shard_map/powers/pallas_call | solution.py:438
  49.1 17.6 %all_to_all.15 = f32[64,1,128]{2,1,0:T(1,128)S(1)} all-to-all(f32[64,1,128]{2,1,0:T(1,128)S(1)} %bitcast.12), channel_id=1, replica_groups=mesh['gx'=16,'gy'=4,'gz'=16] {'gy','gz'}, dimensions={0} | all-to-all | bytes 65536 | tf_op jit(solution)/shard_map/all_to_all | solution.py:410
  66.7 0.1 reduce_sum.18
  66.8 31.3 %all_to_all.16 = f32[16,1,128]{2,1,0:T(1,128)S(1)} all-to-all(f32[16,1,128]{2,1,0:T(1,128)S(1)} %broadcast_in_dim.6), channel_id=1, replica_groups=mesh['gx'=16,'gy'=4,'gz'=16] {'gx'}, dimensions={0} | all-to-all | bytes 16384 | tf_op jit(solution)/shard_map/all_to_all | solution.py:411
  98.2 14.7 %all_to_all.17 = f32[64,1,128]{2,1,0:T(1,128)S(1)} all-to-all(f32[64,1,128]{2,1,0:T(1,128)S(1)} %broadcast_in_dim.7), channel_id=1, replica_groups=mesh['gx'=16,'gy'=4,'gz'=16] {'gy','gz'}, dimensions={0} | all-to-all | bytes 65536 | tf_op jit(solution)/shard_map/all_to_all | solution.py:413
  112.9 7.6 %solve.1 = (f32[512,128]{1,0:T(8,128)}, f32[512,128]{1,0:T(8,128)}) custom-call(f32[64,128]{1,0:T(8,128)S(1)} %bitcast.11, f32[5,16,32,128]{3,2,1,0:T(8,128)S(1)} %get-tuple-element.15.basis_ref), custom_call_target="tpu_custom_call" | custom-call | tf_op jit(solution)/shard_map/solve/pallas_call | solution.py:452
  (4 shorter events, 0.1 us)
Async XLA Ops:
  0.6 40.3 %copy-start.1 = (f32[8,4]{0,1:T(4,128)S(1)}, f32[8,4]{0,1:T(4,128)}, u32[]{:S(2)}) copy-start(f32[8,4]{0,1:T(4,128)} %param.7) | copy-start | bytes 388
  3.4 5.9 %collective-permute-start.1 = (f32[40,128]{1,0:T(8,128)}, f32[40,128]{1,0:T(8,128)S(1)}, u32[]{:S(2)}, u32[]{:S(2)}) collective-permute-start(f32[40,128]{1,0:T(8,128)} %get-tuple-element.11), channel_id=1, source_target_pairs={{16,0},{32,16},{48,32},{17,1},{33,17},{49,33},{18,2},{34,18},{50,3... | collective-permute-start | bytes 61448 | tf_op jit(solution)/shard_map/ppermute | solution.py:403
  4.7 5.7 %collective-permute-start = (f32[40,128]{1,0:T(8,128)}, f32[40,128]{1,0:T(8,128)S(1)}, u32[]{:S(2)}, u32[]{:S(2)}) collective-permute-start(f32[40,128]{1,0:T(8,128)} %get-tuple-element.11), channel_id=1, source_target_pairs={{0,16},{16,32},{32,48},{1,17},{17,33},{33,49},{2,18},{18,34},{34,5... | collective-permute-start | bytes 61448 | tf_op jit(solution)/shard_map/ppermute | solution.py:403
  10.3 1.0 copy-start
  11.3 8.3 %collective-permute-start.3 = (f32[18,32,128]{2,1,0:T(8,128)S(1)}, f32[18,32,128]{2,1,0:T(8,128)S(1)}, u32[]{:S(2)}, u32[]{:S(2)}) collective-permute-start(f32[18,32,128]{2,1,0:T(8,128)S(1)} %join.1.own_ref), channel_id=1, source_target_pairs={{64,0},{128,64},{192,128},{256,192},{320,256},{384,320},{448,384},... | collective-permute-start | bytes 884744 | tf_op jit(solution)/shard_map/ppermute | solution.py:403
  12.6 8.5 %collective-permute-start.2 = (f32[18,32,128]{2,1,0:T(8,128)S(1)}, f32[18,32,128]{2,1,0:T(8,128)S(1)}, u32[]{:S(2)}, u32[]{:S(2)}) collective-permute-start(f32[18,32,128]{2,1,0:T(8,128)S(1)} %join.1.own_ref), channel_id=1, source_target_pairs={{0,64},{64,128},{128,192},{192,256},{256,320},{320,384},{384,448},... | collective-permute-start | bytes 884744 | tf_op jit(solution)/shard_map/ppermute | solution.py:403
  21.2 18.2 %collective-permute-start.4 = (f32[33,32,128]{2,1,0:T(8,128)S(1)}, f32[33,32,128]{2,1,0:T(8,128)S(1)}, u32[]{:S(2)}, u32[]{:S(2)}) collective-permute-start(f32[33,32,128]{2,1,0:T(8,128)S(1)} %get-tuple-element.13), channel_id=1, source_target_pairs={{0,1},{1,2},{2,3},{3,4},{4,5},{5,6},{6,7},{7,8},{8,9},{9,10},{10,1... | collective-permute-start | bytes 1622024 | tf_op jit(solution)/shard_map/ppermute | solution.py:403
  27.9 13.1 %collective-permute-start.5 = (f32[33,32,128]{2,1,0:T(8,128)S(1)}, f32[33,32,128]{2,1,0:T(8,128)S(1)}, u32[]{:S(2)}, u32[]{:S(2)}) collective-permute-start(f32[33,32,128]{2,1,0:T(8,128)S(1)} %get-tuple-element.12.mid_ref), channel_id=1, source_target_pairs={{1,0},{2,1},{3,2},{4,3},{5,4},{6,5},{7,6},{8,7},{9,8},{10,9},{11,1... | collective-permute-start | bytes 1622024 | tf_op jit(solution)/shard_map/ppermute | solution.py:403

commit v6 on v5

--- a/solution.py
+++ b/solution.py
@@ -86,13 +86,18 @@
         )
     block_ref[CELLS, 0:CELLS, :] = labels
     block_ref[CELLS, CELLS:R, :] = jnp.zeros((R - CELLS, LANES), jnp.float32)
-    edge_ref[0:R, :] = edge
-    edge_ref[R:EDGE_ROWS, :] = edge_label
-
-
-def join_kernel(block_ref, before_ref, after_ref, out_ref):
+    for slot in range(edge_ref.shape[0]):
+        edge_ref[slot, 0:R, :] = edge
+        edge_ref[slot, R:EDGE_ROWS, :] = edge_label
+
+
+def join_kernel(block_ref, edges_ref, out_ref):
+    count = edges_ref.shape[0]
+    place = lax.axis_index("gy")
     left = lane_index((EDGE_ROWS, LANES)) % (2 * S) < S
-    edge = jnp.where(left, before_ref[...], after_ref[...])
+    before = jnp.where(place > 0, edges_ref[jnp.maximum(place - 1, 0)], 0.0)
+    after = jnp.where(place < count - 1, edges_ref[jnp.minimum(place + 1, count - 1)], 0.0)
+    edge = jnp.where(left, before, after)
     out_ref[0 : CELLS + 1] = block_ref[...]
     out_ref[CELLS, CELLS : CELLS + 1, :] = edge[R : R + 1]
     out_ref[CELLS + 1] = edge[:R]
@@ -418,7 +423,7 @@
     block, edge = call(
         rhs_kernel,
         "rhs",
-        [(CELLS + 1, R, LANES), (EDGE_ROWS, LANES)],
+        [(CELLS + 1, R, LANES), (lax.axis_size("gy"), EDGE_ROWS, LANES)],
         [SMEM, HBM, HBM, HBM],
         [
             pltpu.VMEM((NREG, sweep_gain.shape[0]), jnp.float32),
@@ -428,8 +433,8 @@
         ],
         60,
     )(sweep_index, sweep_gain.T, sources.reshape(R * CELLS, LANES), labels.reshape(CELLS, LANES))
-    before, after = neighbour(edge, "gy", 1), neighbour(edge, "gy", -1)
-    block = call(join_kernel, "join", [(CELLS + 2, R, LANES)], [VMEM] * 3)(block, before, after)[0]
+    edges = lax.all_to_all(edge, "gy", 0, 0)
+    block = call(join_kernel, "join", [(CELLS + 2, R, LANES)], [VMEM] * 2)(block, edges)[0]
     low, high = neighbour(block, "gx", 1), neighbour(block, "gx", -1)
     down, up = call(merge_kernel, "merge", [(PLANES, R, LANES)] * 2, [VMEM] * 3)(
         block, low, high

time: 121 us -> 121 us (level)
  blocking collectives: 63.6 us -> 71.4 us
  starting transfers between devices: 30.2 us -> 23.4 us
    all_to_all x0 -> x1, blocking collectives: none -> 9.42 us  [body(): edges = lax.all_to_all(edge, 'gy', 0, 0)]
    ppermute x6 -> x4, starting transfers between devices: 30.2 us -> 23.4 us  [neighbour(): return lax.ppermute(value, axis, pairs)]
    all_to_all x1, blocking collectives: 17.6 us -> 16 us  [total(): piece = lax.all_to_all(values.reshape(parts, -1, LANES), near, 0, 0).sum(0)]
    ppermute x6 -> x4, waiting for transfers between devices: 6.25 us -> 5.16 us  [neighbour(): return lax.ppermute(value, axis, pairs)]
  transfers between devices with their start and end apart: 6 -> 4, of which waited for: 4 -> 3; matrix products, arithmetic and copies ran while one was open for 0% -> 0% of each run, Pallas kernels for 0% -> 0%
where the time goes in v6:
time: 121 us; the launch traced here: 120 us
  blocking collectives  71.4 us (59%)
  starting transfers between devices  23.4 us (19%)
  Pallas kernels  18.5 us (15%)
  waiting for transfers between devices  5.16 us (4%)
    all_to_all x1, blocking collectives, total(): lax.all_to_all(jnp.broadcast_to(piece, (others,) + piece.shape), 'gx', 0, 0)  31.3 us
    ppermute x4, starting transfers between devices, neighbour(): return lax.ppermute(value, axis, pairs)  23.4 us
    all_to_all x1, blocking collectives, total(): piece = lax.all_to_all(values.reshape(parts, -1, LANES), near, 0, 0).sum(0)  16 us
    all_to_all x1, blocking collectives, total(): lax.all_to_all(jnp.broadcast_to(piece, (parts,) + piece.shape), near, 0, 0)  14.7 us
    all_to_all x1, blocking collectives, body(): edges = lax.all_to_all(edge, 'gy', 0, 0)  9.42 us
    pallas_call x1, Pallas kernels, body(): call(power_kernel, 'powers', [(S + 1, CELLS, R, LANES), (2 * R, LANES)],...  8.15 us
    pallas_call x1, Pallas kernels, body(): call(solve_kernel, 'solve', [(R * CELLS, LANES)] * 2, [VMEM] * 2)  7.56 us
    ppermute x4, waiting for transfers between devices, neighbour(): return lax.ppermute(value, axis, pairs)  5.16 us
  transfers between devices with their start and end apart: 4, of which 3 were waited for; matrix products, arithmetic and copies ran while one was open for 0% of the time, Pallas kernels for 0%

profile of v6, /device:TPU:1, one launch (start us, length us, event | category | flops | bytes accessed | tf_op | source)
XLA Modules:
  0.0 120.3 jit_solution(12943194840384832916)
XLA Ops:
  0.6 0.0 copy-start.1
  0.6 2.7 %rhs.1 = (f32[17,32,128]{2,1,0:T(8,128)}, f32[4,40,128]{2,1,0:T(8,128)}) custom-call(s32[32]{0:T(128)} %index_ref.1, f32[8,32]{1,0:T(8,128)} %bitcast.17, f32[512,128]{1,0:T(8,128)} %bitcast.14, s32[16,128]{1,0:T(8,128)} %bitcast.16), custom_call_target="tpu_custom_call" | custom-call | tf_op jit(solution)/shard_map/rhs/pallas_call | solution.py:423
  3.4 9.4 %all_to_all.20.edges_ref = f32[4,40,128]{2,1,0:T(8,128)S(1)} all-to-all(f32[4,40,128]{2,1,0:T(8,128)} %get-tuple-element.11), channel_id=1, replica_groups=mesh['gx'=16,'gy'=4,'gz'=16] {'gy'}, dimensions={0} | all-to-all | bytes 163840 | tf_op jit(solution)/shard_map/all_to_all | solution.py:436
  12.8 0.0 copy-start
  12.8 1.0 copy-done
  13.8 1.3 %collective-permute-start.1 = (f32[18,32,128]{2,1,0:T(8,128)S(1)}, f32[18,32,128]{2,1,0:T(8,128)S(1)}, u32[]{:S(2)}, u32[]{:S(2)}) collective-permute-start(f32[18,32,128]{2,1,0:T(8,128)S(1)} %join.1.own_ref), channel_id=1, source_target_pairs={{64,0},{128,64},{192,128},{256,192},{320,256},{384,320},{448,384},... | collective-permute-start | bytes 884744 | tf_op jit(solution)/shard_map/ppermute | solution.py:408
  15.1 4.6 %collective-permute-start = (f32[18,32,128]{2,1,0:T(8,128)S(1)}, f32[18,32,128]{2,1,0:T(8,128)S(1)}, u32[]{:S(2)}, u32[]{:S(2)}) collective-permute-start(f32[18,32,128]{2,1,0:T(8,128)S(1)} %join.1.own_ref), channel_id=1, source_target_pairs={{0,64},{64,128},{128,192},{192,256},{256,320},{320,384},{384,448},... | collective-permute-start | bytes 884744 | tf_op jit(solution)/shard_map/ppermute | solution.py:408
  19.7 2.2 %collective-permute-done.1.high_ref = f32[18,32,128]{2,1,0:T(8,128)S(1)} collective-permute-done((f32[18,32,128]{2,1,0:T(8,128)S(1)}, f32[18,32,128]{2,1,0:T(8,128)S(1)}, u32[]{:S(2)}, u32[]{:S(2)}) %collective-permute-start.1) | collective-permute-done | bytes 294944 | tf_op jit(solution)/shard_map/ppermute | solution.py:408
  21.9 1.5 %collective-permute-done.low_ref = f32[18,32,128]{2,1,0:T(8,128)S(1)} collective-permute-done((f32[18,32,128]{2,1,0:T(8,128)S(1)}, f32[18,32,128]{2,1,0:T(8,128)S(1)}, u32[]{:S(2)}, u32[]{:S(2)}) %collective-permute-start) | collective-permute-done | bytes 294944 | tf_op jit(solution)/shard_map/ppermute | solution.py:408
  23.4 0.1 merge.1
  23.4 6.6 %collective-permute-start.2 = (f32[33,32,128]{2,1,0:T(8,128)S(1)}, f32[33,32,128]{2,1,0:T(8,128)S(1)}, u32[]{:S(2)}, u32[]{:S(2)}) collective-permute-start(f32[33,32,128]{2,1,0:T(8,128)S(1)} %get-tuple-element.13), channel_id=1, source_target_pairs={{0,1},{1,2},{2,3},{3,4},{4,5},{5,6},{6,7},{7,8},{8,9},{9,10},{10,1... | collective-permute-start | bytes 1622024 | tf_op jit(solution)/shard_map/ppermute | solution.py:408
  30.1 10.8 %collective-permute-start.3 = (f32[33,32,128]{2,1,0:T(8,128)S(1)}, f32[33,32,128]{2,1,0:T(8,128)S(1)}, u32[]{:S(2)}, u32[]{:S(2)}) collective-permute-start(f32[33,32,128]{2,1,0:T(8,128)S(1)} %get-tuple-element.12.mid_ref), channel_id=1, source_target_pairs={{1,0},{2,1},{3,2},{4,3},{5,4},{6,5},{7,6},{8,7},{9,8},{10,9},{11,1... | collective-permute-start | bytes 1622024 | tf_op jit(solution)/shard_map/ppermute | solution.py:408
  40.9 0.0 collective-permute-done.2.below_ref
  40.9 1.5 %collective-permute-done.3.above_ref = f32[33,32,128]{2,1,0:T(8,128)S(1)} collective-permute-done((f32[33,32,128]{2,1,0:T(8,128)S(1)}, f32[33,32,128]{2,1,0:T(8,128)S(1)}, u32[]{:S(2)}, u32[]{:S(2)}) %collective-permute-start.3) | collective-permute-done | bytes 540704 | tf_op jit(solution)/shard_map/ppermute | solution.py:408
  42.4 0.0 copy-done.1
  42.4 8.1 %powers.1 = (f32[5,16,32,128]{3,2,1,0:T(8,128)S(1)}, f32[64,128]{1,0:T(8,128)S(1)}) custom-call(f32[4,8]{1,0:T(4,128)S(1)} %bitcast.13, f32[18,32,128]{2,1,0:T(8,128)S(1)} %join.1.own_ref, f32[18,32,128]{2,1,0:T(8,128)S(1)} %collective-permute-done.low_ref, f32[18,32,128]{2,1,0:T(8,128)S(1)} %collective-permute-done.1.high_ref, ...), custom_call_target="tpu_custom_call" | custom-call | tf_op jit(solution)/shard_map/powers/pallas_call | solution.py:443
  50.6 16.0 %all_to_all.21 = f32[64,1,128]{2,1,0:T(1,128)S(1)} all-to-all(f32[64,1,128]{2,1,0:T(1,128)S(1)} %bitcast.12), channel_id=1, replica_groups=mesh['gx'=16,'gy'=4,'gz'=16] {'gy','gz'}, dimensions={0} | all-to-all | bytes 65536 | tf_op jit(solution)/shard_map/all_to_all | solution.py:415
  66.6 0.1 reduce_sum.18
  66.7 31.3 %all_to_all.22 = f32[16,1,128]{2,1,0:T(1,128)S(1)} all-to-all(f32[16,1,128]{2,1,0:T(1,128)S(1)} %broadcast_in_dim.6), channel_id=1, replica_groups=mesh['gx'=16,'gy'=4,'gz'=16] {'gx'}, dimensions={0} | all-to-all | bytes 16384 | tf_op jit(solution)/shard_map/all_to_all | solution.py:416
  98.0 14.7 %all_to_all.23 = f32[64,1,128]{2,1,0:T(1,128)S(1)} all-to-all(f32[64,1,128]{2,1,0:T(1,128)S(1)} %broadcast_in_dim.7), channel_id=1, replica_groups=mesh['gx'=16,'gy'=4,'gz'=16] {'gy','gz'}, dimensions={0} | all-to-all | bytes 65536 | tf_op jit(solution)/shard_map/all_to_all | solution.py:418
  112.7 7.6 %solve.1 = (f32[512,128]{1,0:T(8,128)}, f32[512,128]{1,0:T(8,128)}) custom-call(f32[64,128]{1,0:T(8,128)S(1)} %bitcast.11, f32[5,16,32,128]{3,2,1,0:T(8,128)S(1)} %get-tuple-element.15.basis_ref), custom_call_target="tpu_custom_call" | custom-call | tf_op jit(solution)/shard_map/solve/pallas_call | solution.py:457
  (4 shorter events, 0.1 us)
Async XLA Ops:
  0.6 41.8 %copy-start.1 = (f32[8,4]{0,1:T(4,128)S(1)}, f32[8,4]{0,1:T(4,128)}, u32[]{:S(2)}) copy-start(f32[8,4]{0,1:T(4,128)} %param.7) | copy-start | bytes 388
  12.8 1.0 copy-start
  13.8 8.1 %collective-permute-start.1 = (f32[18,32,128]{2,1,0:T(8,128)S(1)}, f32[18,32,128]{2,1,0:T(8,128)S(1)}, u32[]{:S(2)}, u32[]{:S(2)}) collective-permute-start(f32[18,32,128]{2,1,0:T(8,128)S(1)} %join.1.own_ref), channel_id=1, source_target_pairs={{64,0},{128,64},{192,128},{256,192},{320,256},{384,320},{448,384},... | collective-permute-start | bytes 884744 | tf_op jit(solution)/shard_map/ppermute | solution.py:408
  15.1 8.3 %collective-permute-start = (f32[18,32,128]{2,1,0:T(8,128)S(1)}, f32[18,32,128]{2,1,0:T(8,128)S(1)}, u32[]{:S(2)}, u32[]{:S(2)}) collective-permute-start(f32[18,32,128]{2,1,0:T(8,128)S(1)} %join.1.own_ref), channel_id=1, source_target_pairs={{0,64},{64,128},{128,192},{192,256},{256,320},{320,384},{384,448},... | collective-permute-start | bytes 884744 | tf_op jit(solution)/shard_map/ppermute | solution.py:408
  23.4 17.5 %collective-permute-start.2 = (f32[33,32,128]{2,1,0:T(8,128)S(1)}, f32[33,32,128]{2,1,0:T(8,128)S(1)}, u32[]{:S(2)}, u32[]{:S(2)}) collective-permute-start(f32[33,32,128]{2,1,0:T(8,128)S(1)} %get-tuple-element.13), channel_id=1, source_target_pairs={{0,1},{1,2},{2,3},{3,4},{4,5},{5,6},{6,7},{7,8},{8,9},{9,10},{10,1... | collective-permute-start | bytes 1622024 | tf_op jit(solution)/shard_map/ppermute | solution.py:408
  30.1 12.4 %collective-permute-start.3 = (f32[33,32,128]{2,1,0:T(8,128)S(1)}, f32[33,32,128]{2,1,0:T(8,128)S(1)}, u32[]{:S(2)}, u32[]{:S(2)}) collective-permute-start(f32[33,32,128]{2,1,0:T(8,128)S(1)} %get-tuple-element.12.mid_ref), channel_id=1, source_target_pairs={{1,0},{2,1},{3,2},{4,3},{5,4},{6,5},{7,6},{8,7},{9,8},{10,9},{11,1... | collective-permute-start | bytes 1622024 | tf_op jit(solution)/shard_map/ppermute | solution.py:408

commit v7 on v6

--- a/solution.py
+++ b/solution.py
@@ -141,7 +141,7 @@
             cond_ref[column, z] = fields[column]
         return carry
 
-    lax.fori_loop(0, WIDE, conduct, 0)
+    lax.fori_loop(0, WIDE, conduct, 0, unroll=3)
     lane = lane_index((2 * HALF, LANES))
 
     def faces(z, carry):
@@ -167,7 +167,7 @@
             coef_ref[k, z] = jnp.where(inside, value * (1.0 / THETA), 0.0)
         return carry
 
-    lax.fori_loop(1, WIDE - 1, faces, 0)
+    lax.fori_loop(1, WIDE - 1, faces, 0, unroll=5)
 
 
 def outside(at):
@@ -275,11 +275,15 @@
             reach = S - 1 - k - far
 
             def one(i, carry):
-                z = S + i if far == 0 else S - far + i * (SIDE - 1 + 2 * far)
-                power_row(now, later, coef_ref, z, reach)
+                for z in (S + 2 * i, S + 2 * i + 1):
+                    power_row(now, later, coef_ref, z, reach)
                 return carry
 
-            lax.fori_loop(0, SIDE if far == 0 else 2, one, 0)
+            if far == 0:
+                lax.fori_loop(0, SIDE // 2, one, 0)
+            else:
+                for z in (S - far, S + SIDE - 1 + far):
+                    power_row(now, later, coef_ref, z, reach)
         keep(k + 1)
     for k in range(S - 1):
         moments(k)

time: 121 us -> 119 us (0.983)
  Pallas kernels: 18.5 us -> 16.7 us
    pallas_call x1, Pallas kernels: 8.15 us -> 6.31 us  [body(): call(power_kernel, 'powers', [(S + 1, CELLS, R, LANES), (2 * R, LANES)],...]
where the time goes in v7:
time: 119 us; the launch traced here: 118 us
  blocking collectives  71.4 us (60%)
  starting transfers between devices  23.4 us (20%)
  Pallas kernels  16.7 us (14%)
  waiting for transfers between devices  5.16 us (4%)
    all_to_all x1, blocking collectives, total(): lax.all_to_all(jnp.broadcast_to(piece, (others,) + piece.shape), 'gx', 0, 0)  31.3 us
    ppermute x4, starting transfers between devices, neighbour(): return lax.ppermute(value, axis, pairs)  23.4 us
    all_to_all x1, blocking collectives, total(): piece = lax.all_to_all(values.reshape(parts, -1, LANES), near, 0, 0).sum(0)  16 us
    all_to_all x1, blocking collectives, total(): lax.all_to_all(jnp.broadcast_to(piece, (parts,) + piece.shape), near, 0, 0)  14.7 us
    all_to_all x1, blocking collectives, body(): edges = lax.all_to_all(edge, 'gy', 0, 0)  9.42 us
    pallas_call x1, Pallas kernels, body(): call(solve_kernel, 'solve', [(R * CELLS, LANES)] * 2, [VMEM] * 2)  7.56 us
    pallas_call x1, Pallas kernels, body(): call(power_kernel, 'powers', [(S + 1, CELLS, R, LANES), (2 * R, LANES)],...  6.31 us
    ppermute x4, waiting for transfers between devices, neighbour(): return lax.ppermute(value, axis, pairs)  5.16 us
  transfers between devices with their start and end apart: 4, of which 3 were waited for; matrix products, arithmetic and copies ran while one was open for 0% of the time, Pallas kernels for 0%

profile of v7, /device:TPU:1, one launch (start us, length us, event | category | flops | bytes accessed | tf_op | source)
XLA Modules:
  0.0 118.4 jit_solution(16807618284549824781)
XLA Ops:
  0.6 0.0 copy-start.1
  0.6 2.7 %rhs.1 = (f32[17,32,128]{2,1,0:T(8,128)}, f32[4,40,128]{2,1,0:T(8,128)}) custom-call(s32[32]{0:T(128)} %index_ref.1, f32[8,32]{1,0:T(8,128)} %bitcast.17, f32[512,128]{1,0:T(8,128)} %bitcast.14, s32[16,128]{1,0:T(8,128)} %bitcast.16), custom_call_target="tpu_custom_call" | custom-call | tf_op jit(solution)/shard_map/rhs/pallas_call | solution.py:427
  3.4 9.4 %all_to_all.20.edges_ref = f32[4,40,128]{2,1,0:T(8,128)S(1)} all-to-all(f32[4,40,128]{2,1,0:T(8,128)} %get-tuple-element.11), channel_id=1, replica_groups=mesh['gx'=16,'gy'=4,'gz'=16] {'gy'}, dimensions={0} | all-to-all | bytes 163840 | tf_op jit(solution)/shard_map/all_to_all | solution.py:440
  12.8 0.0 copy-start
  12.8 1.0 copy-done
  13.8 1.3 %collective-permute-start.1 = (f32[18,32,128]{2,1,0:T(8,128)S(1)}, f32[18,32,128]{2,1,0:T(8,128)S(1)}, u32[]{:S(2)}, u32[]{:S(2)}) collective-permute-start(f32[18,32,128]{2,1,0:T(8,128)S(1)} %join.1.own_ref), channel_id=1, source_target_pairs={{64,0},{128,64},{192,128},{256,192},{320,256},{384,320},{448,384},... | collective-permute-start | bytes 884744 | tf_op jit(solution)/shard_map/ppermute | solution.py:412
  15.1 4.6 %collective-permute-start = (f32[18,32,128]{2,1,0:T(8,128)S(1)}, f32[18,32,128]{2,1,0:T(8,128)S(1)}, u32[]{:S(2)}, u32[]{:S(2)}) collective-permute-start(f32[18,32,128]{2,1,0:T(8,128)S(1)} %join.1.own_ref), channel_id=1, source_target_pairs={{0,64},{64,128},{128,192},{192,256},{256,320},{320,384},{384,448},... | collective-permute-start | bytes 884744 | tf_op jit(solution)/shard_map/ppermute | solution.py:412
  19.7 2.2 %collective-permute-done.1.high_ref = f32[18,32,128]{2,1,0:T(8,128)S(1)} collective-permute-done((f32[18,32,128]{2,1,0:T(8,128)S(1)}, f32[18,32,128]{2,1,0:T(8,128)S(1)}, u32[]{:S(2)}, u32[]{:S(2)}) %collective-permute-start.1) | collective-permute-done | bytes 294944 | tf_op jit(solution)/shard_map/ppermute | solution.py:412
  21.9 1.5 %collective-permute-done.low_ref = f32[18,32,128]{2,1,0:T(8,128)S(1)} collective-permute-done((f32[18,32,128]{2,1,0:T(8,128)S(1)}, f32[18,32,128]{2,1,0:T(8,128)S(1)}, u32[]{:S(2)}, u32[]{:S(2)}) %collective-permute-start) | collective-permute-done | bytes 294944 | tf_op jit(solution)/shard_map/ppermute | solution.py:412
  23.4 0.1 merge.1
  23.4 6.6 %collective-permute-start.2 = (f32[33,32,128]{2,1,0:T(8,128)S(1)}, f32[33,32,128]{2,1,0:T(8,128)S(1)}, u32[]{:S(2)}, u32[]{:S(2)}) collective-permute-start(f32[33,32,128]{2,1,0:T(8,128)S(1)} %get-tuple-element.13), channel_id=1, source_target_pairs={{0,1},{1,2},{2,3},{3,4},{4,5},{5,6},{6,7},{7,8},{8,9},{9,10},{10,1... | collective-permute-start | bytes 1622024 | tf_op jit(solution)/shard_map/ppermute | solution.py:412
  30.1 10.8 %collective-permute-start.3 = (f32[33,32,128]{2,1,0:T(8,128)S(1)}, f32[33,32,128]{2,1,0:T(8,128)S(1)}, u32[]{:S(2)}, u32[]{:S(2)}) collective-permute-start(f32[33,32,128]{2,1,0:T(8,128)S(1)} %get-tuple-element.12.mid_ref), channel_id=1, source_target_pairs={{1,0},{2,1},{3,2},{4,3},{5,4},{6,5},{7,6},{8,7},{9,8},{10,9},{11,1... | collective-permute-start | bytes 1622024 | tf_op jit(solution)/shard_map/ppermute | solution.py:412
  40.9 0.0 collective-permute-done.2.below_ref
  40.9 1.5 %collective-permute-done.3.above_ref = f32[33,32,128]{2,1,0:T(8,128)S(1)} collective-permute-done((f32[33,32,128]{2,1,0:T(8,128)S(1)}, f32[33,32,128]{2,1,0:T(8,128)S(1)}, u32[]{:S(2)}, u32[]{:S(2)}) %collective-permute-start.3) | collective-permute-done | bytes 540704 | tf_op jit(solution)/shard_map/ppermute | solution.py:412
  42.4 0.0 copy-done.1
  42.4 6.3 %powers.1 = (f32[5,16,32,128]{3,2,1,0:T(8,128)S(1)}, f32[64,128]{1,0:T(8,128)S(1)}) custom-call(f32[4,8]{1,0:T(4,128)S(1)} %bitcast.13, f32[18,32,128]{2,1,0:T(8,128)S(1)} %join.1.own_ref, f32[18,32,128]{2,1,0:T(8,128)S(1)} %collective-permute-done.low_ref, f32[18,32,128]{2,1,0:T(8,128)S(1)} %collective-permute-done.1.high_ref, ...), custom_call_target="tpu_custom_call" | custom-call | tf_op jit(solution)/shard_map/powers/pallas_call | solution.py:447
  48.8 16.0 %all_to_all.21 = f32[64,1,128]{2,1,0:T(1,128)S(1)} all-to-all(f32[64,1,128]{2,1,0:T(1,128)S(1)} %bitcast.12), channel_id=1, replica_groups=mesh['gx'=16,'gy'=4,'gz'=16] {'gy','gz'}, dimensions={0} | all-to-all | bytes 65536 | tf_op jit(solution)/shard_map/all_to_all | solution.py:419
  64.7 0.1 reduce_sum.18
  64.8 31.3 %all_to_all.22 = f32[16,1,128]{2,1,0:T(1,128)S(1)} all-to-all(f32[16,1,128]{2,1,0:T(1,128)S(1)} %broadcast_in_dim.6), channel_id=1, replica_groups=mesh['gx'=16,'gy'=4,'gz'=16] {'gx'}, dimensions={0} | all-to-all | bytes 16384 | tf_op jit(solution)/shard_map/all_to_all | solution.py:420
  96.1 14.7 %all_to_all.23 = f32[64,1,128]{2,1,0:T(1,128)S(1)} all-to-all(f32[64,1,128]{2,1,0:T(1,128)S(1)} %broadcast_in_dim.7), channel_id=1, replica_groups=mesh['gx'=16,'gy'=4,'gz'=16] {'gy','gz'}, dimensions={0} | all-to-all | bytes 65536 | tf_op jit(solution)/shard_map/all_to_all | solution.py:422
  110.9 7.6 %solve.1 = (f32[512,128]{1,0:T(8,128)}, f32[512,128]{1,0:T(8,128)}) custom-call(f32[64,128]{1,0:T(8,128)S(1)} %bitcast.11, f32[5,16,32,128]{3,2,1,0:T(8,128)S(1)} %get-tuple-element.15.basis_ref), custom_call_target="tpu_custom_call" | custom-call | tf_op jit(solution)/shard_map/solve/pallas_call | solution.py:461
  (4 shorter events, 0.1 us)
Async XLA Ops:
  0.6 41.8 %copy-start.1 = (f32[8,4]{0,1:T(4,128)S(1)}, f32[8,4]{0,1:T(4,128)}, u32[]{:S(2)}) copy-start(f32[8,4]{0,1:T(4,128)} %param.7) | copy-start | bytes 388
  12.8 1.0 copy-start
  13.8 8.1 %collective-permute-start.1 = (f32[18,32,128]{2,1,0:T(8,128)S(1)}, f32[18,32,128]{2,1,0:T(8,128)S(1)}, u32[]{:S(2)}, u32[]{:S(2)}) collective-permute-start(f32[18,32,128]{2,1,0:T(8,128)S(1)} %join.1.own_ref), channel_id=1, source_target_pairs={{64,0},{128,64},{192,128},{256,192},{320,256},{384,320},{448,384},... | collective-permute-start | bytes 884744 | tf_op jit(solution)/shard_map/ppermute | solution.py:412
  15.1 8.3 %collective-permute-start = (f32[18,32,128]{2,1,0:T(8,128)S(1)}, f32[18,32,128]{2,1,0:T(8,128)S(1)}, u32[]{:S(2)}, u32[]{:S(2)}) collective-permute-start(f32[18,32,128]{2,1,0:T(8,128)S(1)} %join.1.own_ref), channel_id=1, source_target_pairs={{0,64},{64,128},{128,192},{192,256},{256,320},{320,384},{384,448},... | collective-permute-start | bytes 884744 | tf_op jit(solution)/shard_map/ppermute | solution.py:412
  23.4 17.5 %collective-permute-start.2 = (f32[33,32,128]{2,1,0:T(8,128)S(1)}, f32[33,32,128]{2,1,0:T(8,128)S(1)}, u32[]{:S(2)}, u32[]{:S(2)}) collective-permute-start(f32[33,32,128]{2,1,0:T(8,128)S(1)} %get-tuple-element.13), channel_id=1, source_target_pairs={{0,1},{1,2},{2,3},{3,4},{4,5},{5,6},{6,7},{7,8},{8,9},{9,10},{10,1... | collective-permute-start | bytes 1622024 | tf_op jit(solution)/shard_map/ppermute | solution.py:412
  30.1 12.4 %collective-permute-start.3 = (f32[33,32,128]{2,1,0:T(8,128)S(1)}, f32[33,32,128]{2,1,0:T(8,128)S(1)}, u32[]{:S(2)}, u32[]{:S(2)}) collective-permute-start(f32[33,32,128]{2,1,0:T(8,128)S(1)} %get-tuple-element.12.mid_ref), channel_id=1, source_target_pairs={{1,0},{2,1},{3,2},{4,3},{5,4},{6,5},{7,6},{8,7},{9,8},{10,9},{11,1... | collective-permute-start | bytes 1622024 | tf_op jit(solution)/shard_map/ppermute | solution.py:412

commit v8 on v7

--- a/solution.py
+++ b/solution.py
@@ -15,7 +15,7 @@
 HALF = 16
 EDGE_ROWS = R + 8
 KEPT = sum(SIDE + 2 * (S - d) for d in range(1, S + 1))
-PLANES = KEPT + 5
+PLANES = KEPT + 3
 
 
 SIGMA = 8.0
@@ -116,16 +116,15 @@
     for out_ref, order in ((down_ref, (0, 1, 2, 3)), (up_ref, (3, 2, 1, 0))):
         for slot, (row, x) in enumerate(kept_cells(order)):
             out_ref[slot] = blocks[(x + SIDE) // SIDE][row * SIDE + x % SIDE]
+            label = blocks[(x + SIDE) // SIDE][CELLS, row * SIDE + x % SIDE : row * SIDE + x % SIDE + 1, :]
+            out_ref[KEPT + 2, slot : slot + 1, :] = label
+        low_side = lane_index((R, LANES)) // (2 * S) % SIDE >= SIDE // 2
+        out_ref[KEPT] = own_ref[CELLS + 1]
+        out_ref[KEPT + 1] = jnp.where(low_side, low_ref[CELLS + 1], high_ref[CELLS + 1])
         for g in range(3):
-            out_ref[KEPT + g] = blocks[g][CELLS + 1]
-            labels = blocks[g][CELLS, 0:CELLS, :]
-            if g < 2:
-                out_ref[KEPT + 3, g * CELLS : (g + 1) * CELLS, :] = labels
-            else:
-                out_ref[KEPT + 4, 0:CELLS, :] = labels
             edge = blocks[g][CELLS, CELLS : CELLS + 1, :]
-            out_ref[KEPT + 4, CELLS + g : CELLS + g + 1, :] = edge
-        out_ref[KEPT + 4, CELLS + 3 : R, :] = jnp.zeros((R - CELLS - 3, LANES), jnp.float32)
+            out_ref[KEPT + 2, KEPT + g : KEPT + g + 1, :] = edge
+        out_ref[KEPT + 2, KEPT + 3 : R, :] = jnp.zeros((R - KEPT - 3, LANES), jnp.float32)
 
 
 def coefficients(table_ref, label_ref, cond_ref, coef_ref):
@@ -200,7 +199,6 @@
     own_ref,
     low_ref,
     high_ref,
-    mid_ref,
     below_ref,
     above_ref,
     basis_ref,
@@ -213,17 +211,20 @@
 ):
     blocks = (low_ref, own_ref, high_ref)
     label_ref[...] = jnp.zeros(label_ref.shape, jnp.float32)
-    sides = ((0, below_ref), (S, mid_ref), (S + SIDE, above_ref))
-    for base, ref in sides:
+    sides = ((0, below_ref, (3, 2, 1, 0)), (S, None, None), (S + SIDE, above_ref, (0, 1, 2, 3)))
+    for base, ref, order in sides:
+        if ref is not None:
+            for slot, (row, x) in enumerate(kept_cells(order)):
+                label_ref[base + row, S + x : S + x + 1, :] = ref[KEPT + 2, slot : slot + 1, :]
         for g in range(3):
+            if ref is None:
+                edge = blocks[g][CELLS, CELLS : CELLS + 1, :]
+            else:
+                edge = ref[KEPT + 2, KEPT + g : KEPT + g + 1, :]
             for row in range(SIDE):
-                labels = (
-                    ref[KEPT + 3, g * CELLS + row * SIDE : g * CELLS + (row + 1) * SIDE, :]
-                    if g < 2
-                    else ref[KEPT + 4, row * SIDE : (row + 1) * SIDE, :]
-                )
-                label_ref[base + row, g * SIDE : (g + 1) * SIDE, :] = labels
-                edge = ref[KEPT + 4, CELLS + g : CELLS + g + 1, :]
+                if ref is None:
+                    labels = blocks[g][CELLS, row * SIDE : (row + 1) * SIDE, :]
+                    label_ref[base + row, g * SIDE : (g + 1) * SIDE, :] = labels
                 for x in range(SIDE):
                     if outside(base + row) + outside(g * SIDE + x) >= S:
                         continue
@@ -239,9 +240,12 @@
         even_ref[row, S + x, 0] = below_ref[slot]
     for slot, (row, x) in enumerate(kept_cells((0, 1, 2, 3))):
         even_ref[S + SIDE + row, S + x, 0] = above_ref[slot]
-    for base, ref in sides:
+    for base, ref, _ in sides:
         for g in range(3):
-            edge = ref[KEPT + g]
+            if ref is None:
+                edge = blocks[g][CELLS + 1]
+            else:
+                edge = ref[KEPT + (g != 1)]
             for row in range(SIDE):
                 for x in range(SIDE):
                     if outside(base + row) + outside(g * SIDE + x) >= S:
@@ -448,7 +452,7 @@
         power_kernel,
         "powers",
         [(S + 1, CELLS, R, LANES), (2 * R, LANES)],
-        [SMEM] + [VMEM] * 6,
+        [SMEM] + [VMEM] * 5,
         [
             pltpu.VMEM((WIDE, 2 * HALF, LANES), jnp.float32),
             pltpu.VMEM((4, WIDE, 2 * HALF, LANES), jnp.float32),
@@ -457,7 +461,7 @@
             pltpu.VMEM((WIDE, WIDE, 2, R, LANES), jnp.float32),
         ],
             24,
-    )(region_table.T, block, low, high, down, below, above)
+    )(region_table.T, block, low, high, below, above)
     solution, residual = call(
         solve_kernel, "solve", [(R * CELLS, LANES)] * 2, [VMEM] * 2
     )(total(moments), basis)

time: 119 us -> 119 us (level)
  no operation moved by 1% of the time
where the time goes in v8:
time: 119 us; the launch traced here: 118 us
  blocking collectives  71.1 us (60%)
  starting transfers between devices  23.4 us (20%)
  Pallas kernels  16.7 us (14%)
  waiting for transfers between devices  5.12 us (4%)
    all_to_all x1, blocking collectives, total(): lax.all_to_all(jnp.broadcast_to(piece, (others,) + piece.shape), 'gx', 0, 0)  31.3 us
    ppermute x4, starting transfers between devices, neighbour(): return lax.ppermute(value, axis, pairs)  23.4 us
    all_to_all x1, blocking collectives, total(): piece = lax.all_to_all(values.reshape(parts, -1, LANES), near, 0, 0).sum(0)  15.7 us
    all_to_all x1, blocking collectives, total(): lax.all_to_all(jnp.broadcast_to(piece, (parts,) + piece.shape), near, 0, 0)  14.7 us
    all_to_all x1, blocking collectives, body(): edges = lax.all_to_all(edge, 'gy', 0, 0)  9.42 us
    pallas_call x1, Pallas kernels, body(): call(solve_kernel, 'solve', [(R * CELLS, LANES)] * 2, [VMEM] * 2)  7.56 us
    pallas_call x1, Pallas kernels, body(): call(power_kernel, 'powers', [(S + 1, CELLS, R, LANES), (2 * R, LANES)],...  6.31 us
    ppermute x4, waiting for transfers between devices, neighbour(): return lax.ppermute(value, axis, pairs)  5.12 us
  transfers between devices with their start and end apart: 4, of which 3 were waited for; matrix products, arithmetic and copies ran while one was open for 0% of the time, Pallas kernels for 0%

profile of v8, /device:TPU:1, one launch (start us, length us, event | category | flops | bytes accessed | tf_op | source)
XLA Modules:
  0.0 118.1 jit_solution(15750888656415197765)
XLA Ops:
  0.6 0.0 copy-start.1
  0.6 2.7 %rhs.1 = (f32[17,32,128]{2,1,0:T(8,128)}, f32[4,40,128]{2,1,0:T(8,128)}) custom-call(s32[32]{0:T(128)} %index_ref.1, f32[8,32]{1,0:T(8,128)} %bitcast.17, f32[512,128]{1,0:T(8,128)} %bitcast.14, s32[16,128]{1,0:T(8,128)} %bitcast.16), custom_call_target="tpu_custom_call" | custom-call | tf_op jit(solution)/shard_map/rhs/pallas_call | solution.py:431
  3.4 9.4 %all_to_all.20.edges_ref = f32[4,40,128]{2,1,0:T(8,128)S(1)} all-to-all(f32[4,40,128]{2,1,0:T(8,128)} %get-tuple-element.11), channel_id=1, replica_groups=mesh['gx'=16,'gy'=4,'gz'=16] {'gy'}, dimensions={0} | all-to-all | bytes 163840 | tf_op jit(solution)/shard_map/all_to_all | solution.py:444
  12.8 0.0 copy-start
  12.8 1.0 copy-done
  13.8 1.3 %collective-permute-start.1 = (f32[18,32,128]{2,1,0:T(8,128)S(1)}, f32[18,32,128]{2,1,0:T(8,128)S(1)}, u32[]{:S(2)}, u32[]{:S(2)}) collective-permute-start(f32[18,32,128]{2,1,0:T(8,128)S(1)} %join.1.own_ref), channel_id=1, source_target_pairs={{64,0},{128,64},{192,128},{256,192},{320,256},{384,320},{448,384},... | collective-permute-start | bytes 884744 | tf_op jit(solution)/shard_map/ppermute | solution.py:416
  15.1 4.6 %collective-permute-start = (f32[18,32,128]{2,1,0:T(8,128)S(1)}, f32[18,32,128]{2,1,0:T(8,128)S(1)}, u32[]{:S(2)}, u32[]{:S(2)}) collective-permute-start(f32[18,32,128]{2,1,0:T(8,128)S(1)} %join.1.own_ref), channel_id=1, source_target_pairs={{0,64},{64,128},{128,192},{192,256},{256,320},{320,384},{384,448},... | collective-permute-start | bytes 884744 | tf_op jit(solution)/shard_map/ppermute | solution.py:416
  19.7 2.2 %collective-permute-done.1.high_ref = f32[18,32,128]{2,1,0:T(8,128)S(1)} collective-permute-done((f32[18,32,128]{2,1,0:T(8,128)S(1)}, f32[18,32,128]{2,1,0:T(8,128)S(1)}, u32[]{:S(2)}, u32[]{:S(2)}) %collective-permute-start.1) | collective-permute-done | bytes 294944 | tf_op jit(solution)/shard_map/ppermute | solution.py:416
  21.9 1.5 %collective-permute-done.low_ref = f32[18,32,128]{2,1,0:T(8,128)S(1)} collective-permute-done((f32[18,32,128]{2,1,0:T(8,128)S(1)}, f32[18,32,128]{2,1,0:T(8,128)S(1)}, u32[]{:S(2)}, u32[]{:S(2)}) %collective-permute-start) | collective-permute-done | bytes 294944 | tf_op jit(solution)/shard_map/ppermute | solution.py:416
  23.4 0.1 merge.1
  23.4 6.6 %collective-permute-start.2 = (f32[31,32,128]{2,1,0:T(8,128)S(1)}, f32[31,32,128]{2,1,0:T(8,128)S(1)}, u32[]{:S(2)}, u32[]{:S(2)}) collective-permute-start(f32[31,32,128]{2,1,0:T(8,128)S(1)} %get-tuple-element.12), channel_id=1, source_target_pairs={{0,1},{1,2},{2,3},{3,4},{4,5},{5,6},{6,7},{7,8},{8,9},{9,10},{10,1... | collective-permute-start | bytes 1523720 | tf_op jit(solution)/shard_map/ppermute | solution.py:416
  30.1 10.8 %collective-permute-start.3 = (f32[31,32,128]{2,1,0:T(8,128)S(1)}, f32[31,32,128]{2,1,0:T(8,128)S(1)}, u32[]{:S(2)}, u32[]{:S(2)}) collective-permute-start(f32[31,32,128]{2,1,0:T(8,128)S(1)} %get-tuple-element.13), channel_id=1, source_target_pairs={{1,0},{2,1},{3,2},{4,3},{5,4},{6,5},{7,6},{8,7},{9,8},{10,9},{11,1... | collective-permute-start | bytes 1523720 | tf_op jit(solution)/shard_map/ppermute | solution.py:416
  40.9 0.0 collective-permute-done.2.below_ref
  40.9 1.5 %collective-permute-done.3.above_ref = f32[31,32,128]{2,1,0:T(8,128)S(1)} collective-permute-done((f32[31,32,128]{2,1,0:T(8,128)S(1)}, f32[31,32,128]{2,1,0:T(8,128)S(1)}, u32[]{:S(2)}, u32[]{:S(2)}) %collective-permute-start.3) | collective-permute-done | bytes 507936 | tf_op jit(solution)/shard_map/ppermute | solution.py:416
  42.4 0.0 copy-done.1
  42.4 6.3 %powers.1 = (f32[5,16,32,128]{3,2,1,0:T(8,128)S(1)}, f32[64,128]{1,0:T(8,128)S(1)}) custom-call(f32[4,8]{1,0:T(4,128)S(1)} %bitcast.13, f32[18,32,128]{2,1,0:T(8,128)S(1)} %join.1.own_ref, f32[18,32,128]{2,1,0:T(8,128)S(1)} %collective-permute-done.low_ref, f32[18,32,128]{2,1,0:T(8,128)S(1)} %collective-permute-done.1.high_ref, ...), custom_call_target="tpu_custom_call" | custom-call | tf_op jit(solution)/shard_map/powers/pallas_call | solution.py:451
  48.7 15.7 %all_to_all.21 = f32[64,1,128]{2,1,0:T(1,128)S(1)} all-to-all(f32[64,1,128]{2,1,0:T(1,128)S(1)} %bitcast.12), channel_id=1, replica_groups=mesh['gx'=16,'gy'=4,'gz'=16] {'gy','gz'}, dimensions={0} | all-to-all | bytes 65536 | tf_op jit(solution)/shard_map/all_to_all | solution.py:423
  64.4 0.1 reduce_sum.18
  64.5 31.3 %all_to_all.22 = f32[16,1,128]{2,1,0:T(1,128)S(1)} all-to-all(f32[16,1,128]{2,1,0:T(1,128)S(1)} %broadcast_in_dim.6), channel_id=1, replica_groups=mesh['gx'=16,'gy'=4,'gz'=16] {'gx'}, dimensions={0} | all-to-all | bytes 16384 | tf_op jit(solution)/shard_map/all_to_all | solution.py:424
  95.8 14.7 %all_to_all.23 = f32[64,1,128]{2,1,0:T(1,128)S(1)} all-to-all(f32[64,1,128]{2,1,0:T(1,128)S(1)} %broadcast_in_dim.7), channel_id=1, replica_groups=mesh['gx'=16,'gy'=4,'gz'=16] {'gy','gz'}, dimensions={0} | all-to-all | bytes 65536 | tf_op jit(solution)/shard_map/all_to_all | solution.py:426
  110.5 7.6 %solve.1 = (f32[512,128]{1,0:T(8,128)}, f32[512,128]{1,0:T(8,128)}) custom-call(f32[64,128]{1,0:T(8,128)S(1)} %bitcast.11, f32[5,16,32,128]{3,2,1,0:T(8,128)S(1)} %get-tuple-element.15.basis_ref), custom_call_target="tpu_custom_call" | custom-call | tf_op jit(solution)/shard_map/solve/pallas_call | solution.py:465
  (4 shorter events, 0.1 us)
Async XLA Ops:
  0.6 41.8 %copy-start.1 = (f32[8,4]{0,1:T(4,128)S(1)}, f32[8,4]{0,1:T(4,128)}, u32[]{:S(2)}) copy-start(f32[8,4]{0,1:T(4,128)} %param.7) | copy-start | bytes 388
  12.8 1.0 copy-start
  13.8 8.1 %collective-permute-start.1 = (f32[18,32,128]{2,1,0:T(8,128)S(1)}, f32[18,32,128]{2,1,0:T(8,128)S(1)}, u32[]{:S(2)}, u32[]{:S(2)}) collective-permute-start(f32[18,32,128]{2,1,0:T(8,128)S(1)} %join.1.own_ref), channel_id=1, source_target_pairs={{64,0},{128,64},{192,128},{256,192},{320,256},{384,320},{448,384},... | collective-permute-start | bytes 884744 | tf_op jit(solution)/shard_map/ppermute | solution.py:416
  15.1 8.3 %collective-permute-start = (f32[18,32,128]{2,1,0:T(8,128)S(1)}, f32[18,32,128]{2,1,0:T(8,128)S(1)}, u32[]{:S(2)}, u32[]{:S(2)}) collective-permute-start(f32[18,32,128]{2,1,0:T(8,128)S(1)} %join.1.own_ref), channel_id=1, source_target_pairs={{0,64},{64,128},{128,192},{192,256},{256,320},{320,384},{384,448},... | collective-permute-start | bytes 884744 | tf_op jit(solution)/shard_map/ppermute | solution.py:416
  23.4 17.5 %collective-permute-start.2 = (f32[31,32,128]{2,1,0:T(8,128)S(1)}, f32[31,32,128]{2,1,0:T(8,128)S(1)}, u32[]{:S(2)}, u32[]{:S(2)}) collective-permute-start(f32[31,32,128]{2,1,0:T(8,128)S(1)} %get-tuple-element.12), channel_id=1, source_target_pairs={{0,1},{1,2},{2,3},{3,4},{4,5},{5,6},{6,7},{7,8},{8,9},{9,10},{10,1... | collective-permute-start | bytes 1523720 | tf_op jit(solution)/shard_map/ppermute | solution.py:416
  30.1 12.3 %collective-permute-start.3 = (f32[31,32,128]{2,1,0:T(8,128)S(1)}, f32[31,32,128]{2,1,0:T(8,128)S(1)}, u32[]{:S(2)}, u32[]{:S(2)}) collective-permute-start(f32[31,32,128]{2,1,0:T(8,128)S(1)} %get-tuple-element.13), channel_id=1, source_target_pairs={{1,0},{2,1},{3,2},{4,3},{5,4},{6,5},{7,6},{8,7},{9,8},{10,9},{11,1... | collective-permute-start | bytes 1523720 | tf_op jit(solution)/shard_map/ppermute | solution.py:416
